TPU v7x, 32 devices: a whole 2x2x4 slice. The times are simulated.
32 devices in a mesh: section: 4 (over y, core), dp: 8 (over z, x).
Axes of the slice: x: 2, y: 2, z: 4, core: 2. Of those that a mesh axis runs over, the one named last changes fastest.
Arguments:
- ids: int32 [32768, 26], P(('section', 'dp')), may hold values from 0 to 8191, as said below
- dense: bfloat16 [32768, 13], P(('section', 'dp')), may hold values from -6 to 6
- labels: int32 [32768], P(('section', 'dp')), may hold values from 0 to 1
- table: bfloat16 [26, 8192, 39], P(None, 'dp'), may hold values from -6 to 6
- cross_weight: bfloat16 [3, 1027, 1027], replicated, may hold values from -0.125 to 0.125
- cross_bias: float32 [3, 1027], replicated, may hold values from -3 to 3
- tower_in: bfloat16 [1027, 1024], replicated, may hold values from -0.1875 to 0.1875
- tower_in_bias: float32 [1024], replicated, may hold values from -3 to 3
- tower_out: bfloat16 [1024, 1024], replicated, may hold values from -0.25 to 0.25
- tower_out_bias: float32 [1024], replicated, may hold values from -3 to 3
- head_weight: float32 [2051], replicated, may hold values from -0.125 to 0.125
- head_bias: float32 [1], replicated, may hold values from -3 to 3
Outputs:
- probs: float32 [32768], P(('section', 'dp'))
- loss: float32 [1], replicated
- dense_grad: float32 [32768, 13], P(('section', 'dp'))
- table_grad: float32 [26, 8192, 39], P(None, 'dp')
- cross_weight_grad: float32 [3, 1027, 1027], replicated
- cross_bias_grad: float32 [3, 1027], replicated
- tower_in_grad: float32 [1027, 1024], P(None, ('section', 'dp'))
- tower_in_bias_grad: float32 [1024], P(('section', 'dp'))
- tower_out_grad: float32 [1024, 1024], P(None, ('section', 'dp'))
- tower_out_bias_grad: float32 [1024], P(('section', 'dp'))
- head_weight_grad: float32 [2051], replicated
- head_bias_grad: float32 [1], replicated
Inputs may be any that keep to these rules, and one draw needn't show every extreme that they name: Row ids of every field are split over dp in blocks of 1024: id // 1024 is the dp index that owns the row. For each field, among the ids of the 1024 examples of one device, exactly 128 name rows of each dp index.
All inputs are finite; a program needn't handle non-finite values.
Results may differ from a plain program's by a relative error of at most 0.0059.
Values may be sent and summed in bfloat16 or wider, within the bound.
A program may use at most 384 MiB of HBM per device.

v0:
```python
import jax
import jax.numpy as jnp
from jax import lax
from jax.sharding import PartitionSpec as P


def from_behind(block, axis, distance):
    devices = range(lax.axis_size(axis))
    route = [(i - distance, i) for i in devices if i - distance in devices]
    return lax.ppermute(block, axis, route)


def contract_rows(left, right):
    return lax.dot_general(
        left, right, (((0,), (0,)), ((), ())), preferred_element_type=jnp.float32
    )


def contract_cols(left, right):
    return lax.dot_general(
        left, right, (((1,), (1,)), ((), ())), preferred_element_type=jnp.float32
    )


def send_forward(leaving):
    return from_behind(leaving, "section", 1)


def send_backward(grad_out):
    return from_behind(grad_out, "section", -1)


def take_slot(stack, slot_index):
    return lax.dynamic_index_in_dim(stack, slot_index, 0, keepdims=False)


def store_slot(stack, value, slot_index):
    return lax.dynamic_update_index_in_dim(stack, value, slot_index, 0)


def body(
    ids,
    dense,
    labels,
    table,
    cross_weight,
    cross_bias,
    tower_in,
    tower_in_bias,
    tower_out,
    tower_out_bias,
    head_weight,
    head_bias,
):
    group_count = lax.axis_size("dp")
    section_count = lax.axis_size("section")
    all_count = section_count * group_count
    section_here = lax.axis_index("section")
    row_count, field_count = ids.shape
    table_rows = table.shape[1]
    embed_width = table.shape[2]
    layer_count = cross_weight.shape[0]
    model_width = cross_weight.shape[1]
    hidden_width = tower_out.shape[0]
    sparse_width = field_count * embed_width
    capacity = row_count // group_count
    tick_count = section_count + section_count - 1
    last_section = section_count - 1
    all_rows = section_count * row_count
    owners = jnp.transpose(ids // table_rows)
    local_ids = jnp.transpose(ids % table_rows)
    owner_hot = (owners[:, :, None] == jnp.arange(group_count, dtype=jnp.int32)).astype(jnp.int32)
    slot_rank = jnp.sum((jnp.cumsum(owner_hot, axis=1) - owner_hot) * owner_hot, axis=2)
    slots = owners * capacity + slot_rank
    field_index = jnp.arange(field_count, dtype=jnp.int32)[:, None]
    requests = jnp.zeros((field_count, row_count), jnp.int32).at[field_index, slots].set(local_ids)
    arrived = lax.all_to_all(
        requests.reshape(field_count, group_count, capacity),
        "dp",
        split_axis=1,
        concat_axis=1,
        tiled=True,
    ).reshape(field_count, row_count)
    looked_up = table[field_index, arrived]
    replies = lax.all_to_all(
        looked_up.reshape(field_count, group_count, capacity, embed_width),
        "dp",
        split_axis=1,
        concat_axis=1,
        tiled=True,
    ).reshape(field_count, row_count, embed_width)
    embedded = jnp.transpose(replies[field_index, slots], (1, 0, 2)).reshape(
        row_count, sparse_width
    )
    first_rows = jnp.concatenate([embedded, dense], axis=1)
    shared_rows, shared_labels = (
        lax.all_gather(first_rows, "section", axis=0, tiled=True),
        lax.all_gather(labels.astype(jnp.bfloat16), "section", axis=0, tiled=True),
    )
    base_stack = shared_rows.reshape(section_count, row_count, model_width)
    layer_here = jnp.minimum(section_here, layer_count - 1)
    is_cross = section_here < layer_count
    weight_here = lax.dynamic_index_in_dim(cross_weight, layer_here, 0, keepdims=False)
    bias_here = lax.dynamic_index_in_dim(cross_bias, layer_here, 0, keepdims=False)
    entries = jnp.zeros((section_count, row_count, model_width), jnp.bfloat16)
    mixed_store = jnp.zeros((section_count, row_count, model_width), jnp.float32)
    incoming = jnp.zeros((row_count, model_width), jnp.bfloat16)
    for tick in range(tick_count):
        micro_index = tick - section_here
        active = (micro_index >= 0) & (micro_index < section_count)
        slot_index = jnp.clip(micro_index, 0, section_count - 1)
        base_rows = take_slot(base_stack, slot_index)
        entering = jnp.where(section_here == 0, base_rows, incoming)

        def cross_step():
            mixed = jnp.dot(entering, weight_here, preferred_element_type=jnp.float32) + bias_here
            leaving = (base_rows.astype(jnp.float32) * mixed + entering.astype(jnp.float32)).astype(
                jnp.bfloat16
            )
            return (leaving, mixed)

        def pass_step():
            return (entering, jnp.zeros((row_count, model_width), jnp.float32))

        leaving, mixed = lax.cond(is_cross & active, cross_step, pass_step)
        entries = store_slot(
            entries, jnp.where(active, entering, take_slot(entries, slot_index)), slot_index
        )
        mixed_store = store_slot(
            mixed_store, jnp.where(active, mixed, take_slot(mixed_store, slot_index)), slot_index
        )
        if tick + 1 < tick_count:
            incoming = send_forward(leaving)
    head_cross = head_weight[:model_width]
    head_tower = head_weight[model_width:]
    targets = shared_labels.astype(jnp.float32)

    def tower_head():
        cross_rows = entries.reshape(all_rows, model_width).astype(jnp.float32)
        inner_pre = (
            jnp.dot(shared_rows, tower_in, preferred_element_type=jnp.float32) + tower_in_bias
        )
        inner_act, inner_back = jax.vjp(jax.nn.gelu, inner_pre)
        inner_low = inner_act.astype(jnp.bfloat16)
        outer_pre = (
            jnp.dot(inner_low, tower_out, preferred_element_type=jnp.float32) + tower_out_bias
        )
        outer_act, outer_back = jax.vjp(jax.nn.gelu, outer_pre)
        logits = (
            jnp.sum(cross_rows * head_cross, axis=1)
            + jnp.sum(outer_act * head_tower, axis=1)
            + head_bias[0]
        )
        chance = jax.nn.sigmoid(logits)
        loss_sum = jnp.sum(jnp.logaddexp(0.0, logits) - targets * logits)
        slope = chance - targets
        head_grad = jnp.concatenate(
            [
                jnp.sum(slope[:, None] * cross_rows, axis=0),
                jnp.sum(slope[:, None] * outer_act, axis=0),
            ]
        )
        head_b_grad = jnp.sum(slope).reshape(1)
        outer_grad = outer_back(slope[:, None] * head_tower)[0].astype(jnp.bfloat16)
        inner_grad = inner_back(contract_cols(outer_grad, tower_out))[0].astype(jnp.bfloat16)
        outer_w = contract_rows(inner_low, outer_grad)
        outer_b = jnp.sum(outer_grad.astype(jnp.float32), axis=0)
        inner_w = contract_rows(shared_rows, inner_grad)
        inner_b = jnp.sum(inner_grad.astype(jnp.float32), axis=0)
        tower_entry = contract_cols(inner_grad, tower_in)
        last_grad = (slope[:, None] * head_cross).astype(jnp.bfloat16)
        return (
            chance,
            loss_sum.reshape(1),
            head_grad,
            head_b_grad,
            inner_w,
            inner_b,
            outer_w,
            outer_b,
            tower_entry,
            last_grad,
        )

    def tower_spare():
        return (
            jnp.zeros((all_rows,), jnp.float32),
            jnp.zeros((1,), jnp.float32),
            jnp.zeros((model_width + hidden_width,), jnp.float32),
            jnp.zeros((1,), jnp.float32),
            jnp.zeros((model_width, hidden_width), jnp.float32),
            jnp.zeros((hidden_width,), jnp.float32),
            jnp.zeros((hidden_width, hidden_width), jnp.float32),
            jnp.zeros((hidden_width,), jnp.float32),
            jnp.zeros((all_rows, model_width), jnp.float32),
            jnp.zeros((all_rows, model_width), jnp.bfloat16),
        )

    (
        chance,
        loss_sum,
        head_grad,
        head_b_grad,
        inner_w_g,
        inner_b_g,
        outer_w_g,
        outer_b_g,
        tower_entry,
        last_grad,
    ) = lax.cond(section_here == last_section, tower_head, tower_spare)
    entry_stack = tower_entry.reshape(section_count, row_count, model_width)
    last_stack = last_grad.reshape(section_count, row_count, model_width)
    weight_grad = jnp.zeros((model_width, model_width), jnp.float32)
    bias_grad = jnp.zeros((model_width,), jnp.float32)
    returning = jnp.zeros((row_count, model_width), jnp.bfloat16)
    for tick in range(tick_count):
        micro_index = tick - (last_section - section_here)
        active = (micro_index >= 0) & (micro_index < section_count)
        slot_index = jnp.clip(micro_index, 0, section_count - 1)
        grad_next = jnp.where(
            section_here == last_section, take_slot(last_stack, slot_index), returning
        )

        def cross_back():
            base_rows = take_slot(base_stack, slot_index)
            layer_rows = take_slot(entries, slot_index)
            mixed = take_slot(mixed_store, slot_index)
            grad_wide = grad_next.astype(jnp.float32)
            mix_grad = (grad_wide * base_rows.astype(jnp.float32)).astype(jnp.bfloat16)
            weight_part = contract_rows(layer_rows, mix_grad)
            bias_part = jnp.sum(mix_grad.astype(jnp.float32), axis=0)
            back_rows = grad_wide + contract_cols(mix_grad, weight_here)
            entry_part = grad_wide * mixed + jnp.where(section_here == 0, back_rows, 0.0)
            return (back_rows.astype(jnp.bfloat16), weight_part, bias_part, entry_part)

        def pass_back():
            return (
                grad_next,
                jnp.zeros((model_width, model_width), jnp.float32),
                jnp.zeros((model_width,), jnp.float32),
                jnp.zeros((row_count, model_width), jnp.float32),
            )

        grad_out, weight_part, bias_part, entry_part = lax.cond(
            is_cross & active, cross_back, pass_back
        )
        weight_grad = weight_grad + weight_part
        bias_grad = bias_grad + bias_part
        entry_stack = store_slot(
            entry_stack, take_slot(entry_stack, slot_index) + entry_part, slot_index
        )
        if tick + 1 < tick_count:
            returning = send_backward(grad_out)
    input_mine, prob_mine = (
        lax.psum_scatter(
            entry_stack.reshape(all_rows, model_width), "section", scatter_dimension=0, tiled=True
        ),
        lax.psum_scatter(chance, "section", scatter_dimension=0, tiled=True),
    )
    dense_grad = input_mine[:, sparse_width:]
    field_grads = jnp.transpose(
        input_mine[:, :sparse_width].reshape(row_count, field_count, embed_width), (1, 0, 2)
    )
    packed = (
        jnp.zeros((field_count, row_count, embed_width), jnp.float32)
        .at[field_index, slots]
        .set(field_grads)
    )
    delivered = lax.all_to_all(
        packed.reshape(field_count, group_count, capacity, embed_width),
        "dp",
        split_axis=1,
        concat_axis=1,
        tiled=True,
    ).reshape(field_count, row_count, embed_width)
    local_grad = (
        jnp.zeros((field_count, table_rows, embed_width), jnp.float32)
        .at[field_index, arrived]
        .add(delivered)
    )
    table_grad = lax.psum(local_grad, "section")
    summed_w, summed_b, summed_head, summed_hb, summed_loss = lax.psum(
        (weight_grad[None], bias_grad[None], head_grad[None], head_b_grad[None], loss_sum[None]),
        "dp",
    )
    every_w, every_b, every_head, every_hb, every_loss = (
        lax.all_gather(summed_w, "section", axis=0, tiled=True),
        lax.all_gather(summed_b, "section", axis=0, tiled=True),
        lax.all_gather(summed_head, "section", axis=0, tiled=True),
        lax.all_gather(summed_hb, "section", axis=0, tiled=True),
        lax.all_gather(summed_loss, "section", axis=0, tiled=True),
    )
    cross_w_out = every_w[:layer_count]
    cross_b_out = every_b[:layer_count]
    head_w_out = every_head[last_section]
    head_b_out = every_hb[last_section]
    loss_out = every_loss[last_section]
    inner_w_out, inner_b_out, outer_w_out, outer_b_out = (
        lax.psum_scatter(inner_w_g, ("section", "dp"), scatter_dimension=1, tiled=True),
        lax.psum_scatter(inner_b_g[None], ("section", "dp"), scatter_dimension=1, tiled=True),
        lax.psum_scatter(outer_w_g, ("section", "dp"), scatter_dimension=1, tiled=True),
        lax.psum_scatter(outer_b_g[None], ("section", "dp"), scatter_dimension=1, tiled=True),
    )
    loss_mean = loss_out / (row_count * all_count)
    return (
        prob_mine,
        loss_mean,
        dense_grad,
        table_grad,
        cross_w_out,
        cross_b_out,
        inner_w_out,
        inner_b_out[0],
        outer_w_out,
        outer_b_out[0],
        head_w_out,
        head_b_out,
    )


def solution(mesh):
    return jax.shard_map(
        body,
        mesh=mesh,
        in_specs=(
            P(("section", "dp"), None),
            P(("section", "dp"), None),
            P(("section", "dp")),
            P(None, "dp", None),
            P(),
            P(),
            P(),
            P(),
            P(),
            P(),
            P(),
            P(),
        ),
        out_specs=(
            P(("section", "dp")),
            P(),
            P(("section", "dp"), None),
            P(None, "dp", None),
            P(),
            P(),
            P(None, ("section", "dp")),
            P(("section", "dp")),
            P(None, ("section", "dp")),
            P(("section", "dp")),
            P(),
            P(),
        ),
        check_vma=False,
    )
```

profile of v0, /device:TPU:1, one launch (start us, length us, event | category | flops | bytes accessed | tf_op | source)
XLA Modules:
  0.0 3739.0 jit_solution(7717334056589662185)
XLA Ops:
  8.4 58.5 %reduce-window.6 = s32[26,8,8,128]{3,2,1,0:T(8,128)S(1)} reduce-window(s32[26,8,8,128]{3,2,1,0:T(8,128)S(1)} %fusion.100, s32[]{:T(128)} %constant.351.clone.1), window={size=1x1x1x128 pad=0_0x0_0x0_0x127_0}, to_apply=%region_0.1 | reduce-window | flops 27049984 | bytes 1703940 | tf_op jit(solution)/shard_map/reduce-window
  69.8 97.7 %scatter_custom_fusion = s32[26624]{0:T(1024)S(1)} fusion(s32[26624]{0:T(1024)S(1)} %reshape.208, s32[26624]{0:T(1024)S(1)} %reshape.210, s32[]{:T(128)} %constant.351.clone.1), kind=kCustom, calls=%fused_computation.234 | custom fusion | bytes 106500
  181.6 450.0 %gather_fusion = bf16[26624,39]{1,0:T(8,128)(2,1)} fusion(bf16[26,1024,39]{2,1,0:T(8,128)(2,1)} %copy.207, s32[26624]{0:T(1024)S(1)} %reshape.196), kind=kCustom, calls=%fused_computation | custom fusion | bytes 4366336 | tf_op jit(solution)/shard_map/gather | solution.py:84
  642.9 47.4 %all-to-all-done.1 = bf16[26,8,128,39]{2,3,0,1:T(8,128)(2,1)S(1)} async-done(((bf16[26,8,128,39]{2,3,0,1:T(8,128)(2,1)}), bf16[26,8,128,39]{2,3,0,1:T(8,128)(2,1)S(1)}, u32[]{:S(2)}, u32[]{:S(2)}) %all-to-all-start.1) | async-done | bytes 2076704 | tf_op jit(solution)/shard_map/all_to_all | solution.py:85
  695.7 450.0 %gather_fusion.1 = bf16[26624,39]{1,0:T(8,128)(2,1)} fusion(bf16[26,1024,39]{2,1,0:T(8,128)(2,1)} %bitcast.375, s32[26624]{0:T(1024)S(1)} %reshape.202), kind=kCustom, calls=%fused_computation.1 | custom fusion | bytes 4366336 | tf_op jit(solution)/shard_map/gather | solution.py:92
  1160.5 56.5 %all-gather.5.cloned.1.call-done = bf16[4096,1027]{0,1:T(8,128)(2,1)} async-done(((bf16[1024,1027]{0,1:T(8,128)(2,1)}), bf16[4096,1027]{0,1:T(8,128)(2,1)}) %all-gather.5.cloned.1.call-update) | async-done | bytes 8413200 | tf_op jit(solution)/shard_map/all_gather | solution.py:97
  1217.0 18.1 reshape.170
  1235.1 40.4 %constant_dynamic-slice_fusion.19 = (bf16[1,1024,1027]{1,0,2:T(2,128)(2,1)}, bf16[1,1024,1027]{1,0,2:T(2,128)(2,1)}, bf16[1,1024,1027]{1,0,2:T(2,128)(2,1)}, bf1...) fusion(bf16[4,1024,1027]{1,0,2:T(4,128)(2,1)} %reshape.170, ...), kind=kLoop, calls=%fused_computation.257 | loop fusion | flops 2103296 | bytes 31549470 | tf_op jit(solution)/shard_map/jit(dynamic_index_in_dim)/dynamic_slice | solution.py:34
  1285.9 23.4 all_gather.22
  1578.9 27.7 conditional.21
  1643.9 14.1 collective-permute-done.6
  1676.1 153.1 %collective-permute-done.7 = bf16[1024,1027]{0,1:T(8,128)(2,1)} collective-permute-done((bf16[1024,1027]{0,1:T(8,128)(2,1)}, bf16[1024,1027]{0,1:T(8,128)(2,1)}, u32[]{:S(2)}, u32[]{:S(2)}) %collective-permute-start.7) | collective-permute-done | bytes 2103328 | tf_op jit(solution)/shard_map/ppermute | solution.py:10
  1833.0 29.7 conditional.25
  1843.0 11.3 fusion.39
  1868.9 21.7 collective-permute-done.8
  1894.3 29.7 conditional.26
  1904.5 11.2 fusion.48
  1939.4 12.5 collective-permute-done.9
  1955.1 29.3 conditional.27
  1964.8 11.1 fusion.57
  1991.5 16.9 copy.228
  2008.4 76.9 %dynamic_update_slice.79 = f32[4,1024,1027]{1,0,2:T(4,128)} dynamic-update-slice(f32[4,1024,1027]{1,0,2:T(4,128)} %get-tuple-element.395, f32[1,1024,1027]{1,0,2:T(1,128)} %copy.228, s32[]{:T(128)} %min.54, s32[]{:T(128)} %constant.351.clone.1, s32[]{:T(128)} %constant.351.clone.1) | dynamic-update-slice | bytes 8413188 | tf_op jit(solution)/shard_map/jit(dynamic_update_index_in_dim)/dynamic_update_slice | solution.py:38
  2098.6 16.9 copy.231
  2115.5 76.9 %dynamic_update_slice.80 = f32[4,1024,1027]{1,0,2:T(4,128)} dynamic-update-slice(f32[4,1024,1027]{1,0,2:T(4,128)} %dynamic_update_slice.79, f32[1,1024,1027]{1,0,2:T(1,128)} %copy.231, s32[]{:T(128)} %min.55, s32[]{:T(128)} %constant.351.clone.1, s32[]{:T(128)} %constant.351.clone.1) | dynamic-update-slice | bytes 8413188 | tf_op jit(solution)/shard_map/jit(dynamic_update_index_in_dim)/dynamic_update_slice | solution.py:38
  2203.3 28.1 conditional.28
  2238.5 17.0 copy.234
  2255.5 76.9 %dynamic_update_slice.81 = f32[4,1024,1027]{1,0,2:T(4,128)} dynamic-update-slice(f32[4,1024,1027]{1,0,2:T(4,128)} %dynamic_update_slice.80, f32[1,1024,1027]{1,0,2:T(1,128)} %copy.234, s32[]{:T(128)} %min.56, s32[]{:T(128)} %constant.351.clone.1, s32[]{:T(128)} %constant.351.clone.1) | dynamic-update-slice | bytes 8413188 | tf_op jit(solution)/shard_map/jit(dynamic_update_index_in_dim)/dynamic_update_slice | solution.py:38
  2343.3 17.0 copy.237
  2360.2 77.0 %dynamic_update_slice.82 = f32[4,1024,1027]{1,0,2:T(4,128)} dynamic-update-slice(f32[4,1024,1027]{1,0,2:T(4,128)} %dynamic_update_slice.81, f32[1,1024,1027]{1,0,2:T(1,128)} %copy.237, s32[]{:T(128)} %min.57, s32[]{:T(128)} %constant.351.clone.1, s32[]{:T(128)} %constant.351.clone.1) | dynamic-update-slice | bytes 8413188 | tf_op jit(solution)/shard_map/jit(dynamic_update_index_in_dim)/dynamic_update_slice | solution.py:38
  2442.6 13.6 add_bitcast_fusion
  2467.6 17.0 copy.240
  2484.6 77.2 %dynamic_update_slice.83 = f32[4,1024,1027]{1,0,2:T(4,128)} dynamic-update-slice(f32[4,1024,1027]{1,0,2:T(4,128)} %dynamic_update_slice.82, f32[1,1024,1027]{1,0,2:T(1,128)} %copy.240, s32[]{:T(128)} %min.58, s32[]{:T(128)} %constant.351.clone.1, s32[]{:T(128)} %constant.351.clone.1) | dynamic-update-slice | bytes 8413188 | tf_op jit(solution)/shard_map/jit(dynamic_update_index_in_dim)/dynamic_update_slice | solution.py:38
  2572.7 16.9 copy.243
  2589.6 76.9 %dynamic_update_slice.84 = f32[4,1024,1027]{1,0,2:T(4,128)} dynamic-update-slice(f32[4,1024,1027]{1,0,2:T(4,128)} %dynamic_update_slice.83, f32[1,1024,1027]{1,0,2:T(1,128)} %copy.243, s32[]{:T(128)} %min.59, s32[]{:T(128)} %constant.351.clone.1, s32[]{:T(128)} %constant.351.clone.1) | dynamic-update-slice | bytes 8413188 | tf_op jit(solution)/shard_map/jit(dynamic_update_index_in_dim)/dynamic_update_slice | solution.py:38
  2677.5 17.1 copy.246
  2694.5 76.9 %dynamic_update_slice.85 = f32[4,1024,1027]{1,0,2:T(4,128)} dynamic-update-slice(f32[4,1024,1027]{1,0,2:T(4,128)} %dynamic_update_slice.84, f32[1,1024,1027]{1,0,2:T(1,128)} %copy.246, s32[]{:T(128)} %min.60, s32[]{:T(128)} %constant.351.clone.1, s32[]{:T(128)} %constant.351.clone.1) | dynamic-update-slice | bytes 8413188 | tf_op jit(solution)/shard_map/jit(dynamic_update_index_in_dim)/dynamic_update_slice | solution.py:38
  2781.0 19.5 copy.287
  2804.0 136.5 %reduce-scatter.10.cloned.1.call-done = f32[1024,1027]{0,1:T(8,128)} async-done(((f32[4096,1027]{0,1:T(8,128)}), f32[1024,1027]{0,1:T(8,128)}) %reduce-scatter.10.cloned.1.call-update) | async-done | bytes 4206608 | tf_op jit(solution)/shard_map/reduce_scatter | solution.py:255
  2959.6 71.3 %scatter_custom_fusion.1 = f32[26624,39]{1,0:T(8,128)} fusion(s32[26624]{0:T(1024)} %copy-done.24, f32[26624,39]{1,0:T(8,128)} %bitcast.397, f32[]{:T(128)} %constant.363.clone.1), kind=kCustom, calls=%fused_computation.139 | custom fusion | bytes 4153856
  3046.3 95.2 %all-to-all-done.2 = f32[26,8,128,39]{2,3,0,1:T(8,128)} async-done(((f32[26,8,128,39]{2,3,0,1:T(8,128)}), f32[26,8,128,39]{2,3,0,1:T(8,128)}, u32[]{:S(2)}, u32[]{:S(2)}) %all-to-all-start.2) | async-done | bytes 4153376 | tf_op jit(solution)/shard_map/all_to_all | solution.py:269
  3150.8 147.4 %scatter_custom_fusion.2 = f32[26624,39]{1,0:T(8,128)} fusion(s32[26624]{0:T(1024)S(1)} %reshape.220, f32[26624,39]{1,0:T(8,128)} %bitcast.398, f32[]{:T(128)} %constant.363.clone.1), kind=kCustom, calls=%fused_computation.141 | custom fusion | flops 1038336 | bytes 4153856
  3298.2 11.4 copy.260
  3325.5 31.0 all-reduce.3
  3359.1 17.4 all-reduce.4
  3391.7 11.4 slice.56
  3404.7 72.9 %all-reduce.8.cloned.1.call-done = f32[26,1024,39]{1,0,2:T(8,128)} async-done(((f32[26,1024,39]{1,0,2:T(8,128)}), f32[26,1024,39]{1,0,2:T(8,128)}) %all-reduce.8.cloned.1.call-update) | async-done | bytes 4153360 | tf_op jit(solution)/shard_map/psum | solution.py:281
  3484.6 105.8 %reduce-scatter.12.cloned.1.call-done = f32[1027,32]{0,1:T(8,128)} async-done(((f32[1027,1024]{0,1:T(8,128)}), f32[1027,32]{0,1:T(8,128)}) %reduce-scatter.12.cloned.1.call-update) | async-done | bytes 131472 | tf_op jit(solution)/shard_map/reduce_scatter | solution.py:299
  3590.4 140.8 %reduce-scatter.14.cloned.1.call-done = f32[1024,32]{0,1:T(8,128)} async-done(((f32[1024,1024]{0,1:T(8,128)}), f32[1024,32]{0,1:T(8,128)}) %reduce-scatter.14.cloned.1.call-update) | async-done | bytes 131088 | tf_op jit(solution)/shard_map/reduce_scatter | solution.py:301
  (375 shorter events, 776.2 us)
Async XLA Ops:
  7.2 1150.1 %copy-start = (f32[3,1027]{1,0:T(4,128)S(1)}, f32[3,1027]{1,0:T(4,128)}, u32[]{:S(2)}) copy-start(f32[3,1027]{1,0:T(4,128)} %param.47) | copy-start | bytes 36976
  68.5 106.0 %copy-start.22 = (bf16[26,1024,39]{1,2,0:T(8,128)(2,1)S(1)}, bf16[26,1024,39]{1,2,0:T(8,128)(2,1)}, u32[]{:S(2)}) copy-start(bf16[26,1024,39]{1,2,0:T(8,128)(2,1)} %param.45) | copy-start | bytes 6230020
  69.8 109.9 %copy-start.24 = (s32[26624]{0:T(1024)}, s32[26624]{0:T(1024)S(1)}, u32[]{:S(2)}) copy-start(s32[26624]{0:T(1024)S(1)} %reshape.208) | copy-start | bytes 319492
  168.2 12.6 all-to-all-start
  638.4 51.9 %all-to-all-start.1 = ((bf16[26,8,128,39]{2,3,0,1:T(8,128)(2,1)}), bf16[26,8,128,39]{2,3,0,1:T(8,128)(2,1)S(1)}, u32[]{:S(2)}, u32[]{:S(2)}) async-start(bf16[26,8,128,39]{2,3,0,1:T(8,128)(2,1)} %copy.208), calls=%async_computation.1 | async-start | bytes 4259840 | tf_op jit(solution)/shard_map/all_to_all | solution.py:85
  642.8 574.2 %all-gather.5.cloned.1.call-start = ((), (), s32[]{:S(2)}) async-start(), calls=%async_computation.8 | async-start | bytes 10567680 | tf_op jit(solution)/shard_map/all_gather | solution.py:97
  1157.0 1646.4 %all-reduce.10.cloned.1.call-start = ((), (), s32[]{:S(2)}) async-start(), calls=%async_computation.11 | async-start | bytes 9510912 | tf_op jit(solution)/shard_map/psum | solution.py:282
  1157.3 373.9 %copy-start.45 = (f32[1027]{0:T(1024)}, f32[1027]{0:T(1024)S(1)}, u32[]{:S(2)}) copy-start(f32[1027]{0:T(1024)S(1)} %fusion.107) | copy-start | bytes 12328
  1283.7 57.0 %collective-permute-start = (bf16[1024,1027]{0,1:T(8,128)(2,1)}, bf16[1024,1027]{0,1:T(8,128)(2,1)}, u32[]{:S(2)}, u32[]{:S(2)}) collective-permute-start(bf16[1024,1027]{0,1:T(8,128)(2,1)} %get-tuple-element.387), channel_id=1, source_target_pairs={{0,8},{8,16},{16,24},{1,9},{9,17},{17,25},{2,10},{10,18},{18,26},{... | collective-permute-start | bytes 6309896 | tf_op jit(solution)/shard_map/ppermute | solution.py:10
  1360.4 25.4 collective-permute-start.1
  1366.2 19.6 slice-start.8
  1368.7 17.1 slice-start.9
  1403.6 27.8 collective-permute-start.2
  1411.4 20.0 slice-start.6
  1413.9 17.6 slice-start.7
  1420.9 10.5 copy-start.5
  1449.4 27.8 collective-permute-start.3
  1457.3 20.0 slice-start.4
  1459.7 17.6 slice-start.5
  1466.8 10.5 copy-start.6
  1495.1 27.8 collective-permute-start.4
  1501.3 21.6 slice-start.2
  1505.6 17.4 slice-start.3
  1537.0 31.8 collective-permute-start.5
  1546.9 21.9 slice-start.12
  1551.2 17.5 slice-start.13
  1556.9 11.8 copy-start.11
  1629.4 28.6 collective-permute-start.6
  1670.0 163.0 %copy-start.31 = (f32[1027]{0:T(1024)}, f32[1027]{0:T(1024)S(1)}, u32[]{:S(2)}) copy-start(f32[1027]{0:T(1024)S(1)} %get-tuple-element.424) | copy-start | bytes 12328
  1670.0 159.2 %collective-permute-start.7 = (bf16[1024,1027]{0,1:T(8,128)(2,1)}, bf16[1024,1027]{0,1:T(8,128)(2,1)}, u32[]{:S(2)}, u32[]{:S(2)}) collective-permute-start(bf16[1024,1027]{0,1:T(8,128)(2,1)} %get-tuple-element.406), channel_id=1, source_target_pairs={{8,0},{16,8},{24,16},{9,1},{17,9},{25,17},{10,2},{18,10},{26,18},{... | collective-permute-start | bytes 6309896 | tf_op jit(solution)/shard_map/ppermute | solution.py:10
  1862.7 31.6 copy-start.33
  1862.7 27.8 collective-permute-start.8
  1924.1 15.4 copy-start.35
  1924.1 27.8 collective-permute-start.9
  1930.4 21.5 copy-start.10
  1984.3 217.1 %collective-permute-start.10 = (bf16[1024,1027]{0,1:T(8,128)(2,1)}, bf16[1024,1027]{0,1:T(8,128)(2,1)}, u32[]{:S(2)}, u32[]{:S(2)}) collective-permute-start(bf16[1024,1027]{0,1:T(8,128)(2,1)} %get-tuple-element.412), channel_id=1, source_target_pairs={{8,0},{16,8},{24,16},{9,1},{17,9},{25,17},{10,2},{18,10},{26,18},{... | collective-permute-start | bytes 6309896 | tf_op jit(solution)/shard_map/ppermute | solution.py:10
  2231.4 205.9 %collective-permute-start.11 = (bf16[1024,1027]{0,1:T(8,128)(2,1)}, bf16[1024,1027]{0,1:T(8,128)(2,1)}, u32[]{:S(2)}, u32[]{:S(2)}) collective-permute-start(bf16[1024,1027]{0,1:T(8,128)(2,1)} %get-tuple-element.414), channel_id=1, source_target_pairs={{8,0},{16,8},{24,16},{9,1},{17,9},{25,17},{10,2},{18,10},{26,18},{... | collective-permute-start | bytes 6309896 | tf_op jit(solution)/shard_map/ppermute | solution.py:10
  2360.2 77.0 %copy-start.15 = (bf16[1027,1027]{1,0:T(8,128)(2,1)S(1)}, bf16[1027,1027]{1,0:T(8,128)(2,1)}, u32[]{:S(2)}) copy-start(bf16[1027,1027]{1,0:T(8,128)(2,1)} %dynamic-slice_bitcast_fusion) | copy-start | bytes 6328378
  2456.2 484.2 %reduce-scatter.10.cloned.1.call-start = ((), (), s32[]{:S(2)}) async-start(), calls=%async_computation.9 | async-start | bytes 21135360 | tf_op jit(solution)/shard_map/reduce_scatter | solution.py:255
  2800.5 522.3 %reduce-scatter.16.cloned.1.call-start = ((), (), s32[]{:S(2)}) async-start(), calls=%async_computation.15 | async-start | bytes 540672
  2802.3 521.9 %reduce-scatter.18.cloned.1.call-start = ((), (), s32[]{:S(2)}) async-start(), calls=%async_computation.16 | async-start | bytes 540672
  2803.4 588.4 %all-gather.7.cloned.1.call-start = ((), (), s32[]{:S(2)}) async-start(), calls=%async_computation.12 | async-start | bytes 23777280 | tf_op jit(solution)/shard_map/all_gather | solution.py:287
  3040.6 100.9 %all-to-all-start.2 = ((f32[26,8,128,39]{2,3,0,1:T(8,128)}), f32[26,8,128,39]{2,3,0,1:T(8,128)}, u32[]{:S(2)}, u32[]{:S(2)}) async-start(f32[26,8,128,39]{2,3,0,1:T(8,128)} %copy.249), calls=%async_computation.3 | async-start | bytes 8519680 | tf_op jit(solution)/shard_map/all_to_all | solution.py:269
  3045.9 431.7 %all-reduce.8.cloned.1.call-start = ((), (), s32[]{:S(2)}) async-start(), calls=%async_computation.10 | async-start | bytes 10223616 | tf_op jit(solution)/shard_map/psum | solution.py:281
  3309.7 280.7 %reduce-scatter.12.cloned.1.call-start = ((), (), s32[]{:S(2)}) async-start(), calls=%async_computation.13 | async-start | bytes 4866048 | tf_op jit(solution)/shard_map/reduce_scatter | solution.py:299
  3315.3 415.8 %reduce-scatter.14.cloned.1.call-start = ((), (), s32[]{:S(2)}) async-start(), calls=%async_computation.14 | async-start | bytes 4325376 | tf_op jit(solution)/shard_map/reduce_scatter | solution.py:301
  3320.8 38.3 %copy-start.27 = (f32[4096]{0:T(1024)S(1)}, f32[4096]{0:T(1024)}, u32[]{:S(2)}) copy-start(f32[4096]{0:T(1024)} %copy-done.26) | copy-start | bytes 49156
  3403.2 327.9 %copy-start.1 = (f32[3,1027]{1,0:T(4,128)S(1)}, f32[3,1027]{1,0:T(4,128)}, u32[]{:S(2)}) copy-start(f32[3,1027]{1,0:T(4,128)} %param.47) | copy-start | bytes 36976
  (41 other events, 234.0 us)
Sparse Core Ops, SparseCore 0:
  1157.1 59.8 all-gather.4
  2456.3 182.7 all-reduce.9
  2800.6 139.7 reduce-scatter.9
  2942.6 157.3 reduce-scatter.15
  3102.1 144.2 reduce-scatter.17
  3247.9 126.9 all-gather.6
  3377.4 100.2 all-reduce.7
  3484.6 105.6 reduce-scatter.11
  3593.2 137.8 reduce-scatter.13
where the time goes:
time: 3780 us; the launch traced here: 3740 us
  local copies, waits for them, and re-layouts  2180 us (58%)
  waiting for transfers between devices  886 us (23%)
  other arithmetic  394 us (10%)
  matrix products  115 us (3%)
  blocking collectives  83.3 us (2%)
  starting transfers between devices  55.2 us (1%)
    dynamic_update_slice x14, local copies, waits for them, and re-layouts, store_slot(): return lax.dynamic_update_index_in_dim(stack, value, slot_index, 0)  549 us
    gather x2, local copies, waits for them, and re-layouts, body(): replies[field_index, slots]  456 us
    gather x1, local copies, waits for them, and re-layouts, body(): looked_up = table[field_index, arrived]  450 us
    unnamed x143, local copies, waits for them, and re-layouts  233 us
    ppermute x12, waiting for transfers between devices, from_behind(): return lax.ppermute(block, axis, route)  230 us
    unnamed x14, other arithmetic  148 us
    reduce_scatter x1, waiting for transfers between devices, body(): lax.psum_scatter(outer_w_g, ('section', 'dp'), scatter_dimension=1, tiled...  141 us
    reduce_scatter x1, waiting for transfers between devices, body(): lax.psum_scatter(entry_stack.reshape(all_rows, model_width), 'section', s...  136 us
  transfers between devices with their start and end apart: 24, of which 17 were waited for; matrix products, arithmetic and copies ran while one was open for 33% of the time, Pallas kernels for 0%

commit v1 on v0

v1 whole, which is shorter than its diff:
```python
import jax
import jax.numpy as jnp
from jax import lax
from jax.sharding import PartitionSpec as P

BF = jnp.bfloat16
F32 = jnp.float32


def mm(left, right, contract):
    return lax.dot_general(
        left, right, ((contract[:1], contract[1:]), ((), ())), preferred_element_type=F32
    )


def gelu_parts(pre):
    act, back = jax.vjp(jax.nn.gelu, pre)
    return act, back(jnp.ones_like(pre))[0]


def body(
    ids,
    dense,
    labels,
    table,
    cross_weight,
    cross_bias,
    tower_in,
    tower_in_bias,
    tower_out,
    tower_out_bias,
    head_weight,
    head_bias,
):
    groups = lax.axis_size("dp")
    sections = lax.axis_size("section")
    device_count = groups * sections
    examples, fields = ids.shape
    table_rows, edim = table.shape[1:]
    layers, width = cross_weight.shape[:2]
    hidden = tower_out.shape[0]
    capacity = examples // groups
    sparse = fields * edim
    me = lax.axis_index("section") * groups + lax.axis_index("dp")

    idt = ids.T
    owner = idt // table_rows
    local = idt % table_rows
    owner_hot = owner[:, None, :] == jnp.arange(groups, dtype=jnp.int32)[None, :, None]
    lane = jnp.arange(examples, dtype=jnp.int32)
    before = (lane[:, None] < lane[None, :]).astype(BF)
    counts = mm(owner_hot.reshape(fields * groups, examples).astype(BF), before, (1, 0))
    rank = jnp.sum(jnp.where(owner_hot, counts.reshape(fields, groups, examples), 0.0), axis=1)
    slot = owner * capacity + rank.astype(jnp.int32)
    slot_hot = (slot[:, None, :] == lane[None, :, None]).astype(BF)
    halves = jnp.stack([local // 32, local % 32], axis=1).astype(BF)
    sent = lax.dot_general(
        halves, slot_hot, (((2,), (2,)), ((0,), (0,))), preferred_element_type=F32
    )
    requests = (sent[:, 0] * 32 + sent[:, 1]).astype(jnp.int32)
    requests = requests.reshape(fields, groups, capacity).transpose(1, 0, 2)
    arrived = lax.all_to_all(requests, "dp", 0, 0, tiled=True)
    arrived = arrived.transpose(1, 0, 2).reshape(fields, examples)
    row_hot = (
        arrived[:, None, :] == jnp.arange(table_rows, dtype=jnp.int32)[None, :, None]
    ).astype(BF)
    table_t = table.transpose(0, 2, 1)
    found = lax.dot_general(
        table_t, row_hot, (((2,), (1,)), ((0,), (0,))), preferred_element_type=F32
    ).astype(BF)
    found = found.reshape(sparse, groups, capacity).transpose(1, 0, 2)
    replies = lax.all_to_all(found, "dp", 0, 0, tiled=True)
    replies = replies.transpose(1, 0, 2).reshape(fields, edim, examples)
    embedded = lax.dot_general(
        replies, slot_hot, (((2,), (1,)), ((0,), (0,))), preferred_element_type=F32
    ).astype(BF)
    x0 = jnp.concatenate([embedded.reshape(sparse, examples), dense.T], axis=0)

    x0w = x0.astype(F32)
    xs, us = [x0], []
    for layer in range(layers):
        u = mm(cross_weight[layer], xs[-1], (0, 0)) + cross_bias[layer][:, None]
        us.append(u)
        xs.append((x0w * u + xs[-1].astype(F32)).astype(BF))
    p1 = mm(tower_in, x0, (0, 0)) + tower_in_bias[:, None]
    a1, d1 = gelu_parts(p1)
    h1 = a1.astype(BF)
    p2 = mm(tower_out, h1, (0, 0)) + tower_out_bias[:, None]
    h2, d2 = gelu_parts(p2)
    head_cross, head_tower = head_weight[:width], head_weight[width:]
    last = xs[-1].astype(F32)
    z = (
        jnp.sum(last * head_cross[:, None], axis=0)
        + jnp.sum(h2 * head_tower[:, None], axis=0)
        + head_bias[0]
    )
    probs = jax.nn.sigmoid(z)
    target = labels.astype(F32)
    loss = jnp.sum(jnp.logaddexp(0.0, z) - target * z)
    s = probs - target
    head_grad = jnp.concatenate([jnp.sum(s * last, axis=1), jnp.sum(s * h2, axis=1)])

    q2 = (s[None, :] * head_tower[:, None] * d2).astype(BF)
    tower_out_g = mm(q2, h1, (1, 1))
    q1 = (mm(tower_out, q2, (1, 0)) * d1).astype(BF)
    tower_in_g = mm(q1, x0, (1, 1))
    tower_biases = [jnp.sum(q1.astype(F32), axis=1), jnp.sum(q2.astype(F32), axis=1)]
    dx0 = mm(tower_in, q1, (1, 0))
    g = (s[None, :] * head_cross[:, None]).astype(BF)
    cross_g, cross_b = [None] * layers, [None] * layers
    for layer in reversed(range(layers)):
        gw = g.astype(F32)
        v = (gw * x0w).astype(BF)
        cross_g[layer] = mm(xs[layer], v, (1, 1))
        cross_b[layer] = jnp.sum(v.astype(F32), axis=1)
        dx0 = dx0 + gw * us[layer]
        g = gw + mm(cross_weight[layer], v, (1, 0))
        if layer:
            g = g.astype(BF)
    dx0 = dx0 + g

    packed = lax.dot_general(
        dx0[:sparse].astype(BF).reshape(fields, edim, examples),
        slot_hot,
        (((2,), (2,)), ((0,), (0,))),
        preferred_element_type=F32,
    ).astype(BF)
    packed = packed.reshape(sparse, groups, capacity).transpose(1, 0, 2)
    delivered = lax.all_to_all(packed, "dp", 0, 0, tiled=True)
    delivered = delivered.transpose(1, 0, 2).reshape(fields, edim, examples)
    table_g = lax.dot_general(
        delivered, row_hot, (((2,), (2,)), ((0,), (0,))), preferred_element_type=F32
    )
    table_g = lax.psum(table_g.astype(BF), "section").astype(F32).transpose(0, 2, 1)

    small = jnp.concatenate(
        cross_b + [head_grad, jnp.sum(s).reshape(1), loss.reshape(1)] + tower_biases
    )
    small = lax.psum(small, ("section", "dp"))
    sizes = [layers * width, width + hidden, 1, 1, hidden, hidden]
    ends = [sum(sizes[: i + 1]) for i in range(len(sizes))]
    pieces = [small[e - n : e] for e, n in zip(ends, sizes)]
    cross_b_out = pieces[0].reshape(layers, width)
    share = hidden // device_count
    bias_in, bias_out = (lax.dynamic_slice(p, (me * share,), (share,)) for p in pieces[4:])
    cross_out = lax.psum(jnp.stack(cross_g).astype(BF), ("section", "dp")).astype(F32)
    tower_in_out = lax.psum_scatter(
        tower_in_g, ("section", "dp"), scatter_dimension=0, tiled=True
    )
    tower_out_out = lax.psum_scatter(
        tower_out_g, ("section", "dp"), scatter_dimension=0, tiled=True
    )
    return (
        probs,
        pieces[3] / (examples * device_count),
        dx0[sparse:].T,
        table_g,
        cross_out,
        cross_b_out,
        tower_in_out.astype(F32).T,
        bias_in,
        tower_out_out.astype(F32).T,
        bias_out,
        pieces[1],
        pieces[2],
    )


def solution(mesh):
    both = ("section", "dp")
    return jax.shard_map(
        body,
        mesh=mesh,
        in_specs=(P(both, None), P(both, None), P(both), P(None, "dp", None)) + (P(),) * 8,
        out_specs=(
            P(both),
            P(),
            P(both, None),
            P(None, "dp", None),
            P(),
            P(),
            P(None, both),
            P(both),
            P(None, both),
            P(both),
            P(),
            P(),
        ),
        check_vma=False,
    )
```

time: 3780 us -> 792 us (0.21)
  local copies, waits for them, and re-layouts: 2180 us -> 37.5 us
  waiting for transfers between devices: 886 us -> 434 us
  other arithmetic: 394 us -> 25.8 us
  matrix products: 115 us -> 193 us
  starting transfers between devices: 55.2 us -> 9.98 us
    gather x3 -> x0, local copies, waits for them, and re-layouts: 906 us -> none  [the longest x2 456 us: body(): replies[field_index, slots]]
    dynamic_update_slice x14 -> x0, local copies, waits for them, and re-layouts: 549 us -> none  [store_slot(): return lax.dynamic_update_index_in_dim(stack, value, slot_index, 0)]
    ppermute x12 -> x0, waiting for transfers between devices: 230 us -> none  [from_behind(): return lax.ppermute(block, axis, route)]
    unnamed x143 -> x48, local copies, waits for them, and re-layouts: 233 us -> 4.33 us
    unnamed x14 -> x0, other arithmetic: 148 us -> none
    broadcast_in_dim x18 -> x0, local copies, waits for them, and re-layouts: 140 us -> none  [the longest x13 136 us: store_slot(): return lax.dynamic_update_index_in_dim(stack, value, slot_index, 0)]
    dynamic_slice x32 -> x2, local copies, waits for them, and re-layouts: 136 us -> 1.17 us  [body(): lax.dynamic_slice(p, (me * share,), (share,))]
    reduce_scatter x3 -> x2, waiting for transfers between devices: 383 us -> 248 us  [the longest x1 140 us: body(): lax.psum_scatter(tower_out_g, ('section', 'dp'), scatter_dimension=0, til...]
  transfers between devices with their start and end apart: 24 -> 6, of which waited for: 17 -> 6; matrix products, arithmetic and copies ran while one was open for 33% -> 9% of each run, Pallas kernels for 0% -> 0%
where the time goes in v1:
time: 792 us; the launch traced here: 776 us
  waiting for transfers between devices  434 us (55%)
  matrix products  193 us (24%)
  blocking collectives  59.1 us (7%)
  local copies, waits for them, and re-layouts  37.5 us (5%)
  other arithmetic  25.8 us (3%)
  between operations  17.1 us (2%)
  starting transfers between devices  9.98 us (1%)
    reduce_scatter x1, waiting for transfers between devices, body(): lax.psum_scatter(tower_out_g, ('section', 'dp'), scatter_dimension=0, til...  140 us
    reduce_scatter x1, waiting for transfers between devices, body(): lax.psum_scatter(tower_in_g, ('section', 'dp'), scatter_dimension=0, tile...  108 us
    dot_general x16, matrix products, mm(): lax.dot_general(left, right, ((contract[:1], contract[1:]), ((), ())), pr...  80.5 us
    psum x1, waiting for transfers between devices, body(): lax.psum(jnp.stack(cross_g).astype(BF), ('section', 'dp')).astype(F32)  48.6 us
    all_to_all x1, waiting for transfers between devices, body(): delivered = lax.all_to_all(packed, 'dp', 0, 0, tiled=True)  47.5 us
    psum x1, blocking collectives, body(): small = lax.psum(small, ('section', 'dp'))  46.5 us
    all_to_all x1, waiting for transfers between devices, body(): replies = lax.all_to_all(found, 'dp', 0, 0, tiled=True)  45 us
    psum x1, waiting for transfers between devices, body(): lax.psum(table_g.astype(BF), 'section').astype(F32).transpose(0, 2, 1)  44.7 us
  transfers between devices with their start and end apart: 6, of which 6 were waited for; matrix products, arithmetic and copies ran while one was open for 9% of the time, Pallas kernels for 0%

profile of v1, /device:TPU:1, one launch (start us, length us, event | category | flops | bytes accessed | tf_op | source)
XLA Modules:
  0.0 776.4 jit_solution(17162273400837830205)
XLA Ops:
  10.5 19.9 %fusion.4 = f32[26,2,1024]{2,1,0:T(2,128)S(1)} fusion(s32[26,1024]{1,0:T(8,128)S(1)} %get-tuple-element.28, bf16[26,1,1024]{2,1,0:T(2,128)(2,1)S(1)} %copy.36, bf16[26,1,1024]{2,1,0:T(2,128)(2,1)S(1)} %copy.35), kind=kOutput, calls=%fused_computation.6 | convolution fusion | flops 136527872 | bytes 425984 | tf_op jit(solution)/shard_map/dot_general | solution.py:57
  30.6 12.6 %all_to_all.15 = s32[8,26,128]{2,1,0:T(8,128)S(1)} all-to-all(s32[8,26,128]{2,1,0:T(8,128)S(1)} %bitcast.188), channel_id=1, replica_groups=mesh['section'=4,'dp'=8] {'dp'}, dimensions={0} | all-to-all | bytes 212992 | tf_op jit(solution)/shard_map/all_to_all | solution.py:62
  44.0 21.6 %convert_bitcast_fusion.1 = bf16[26,39,1024]{2,1,0:T(8,128)(2,1)} fusion(bf16[26,1024,39]{1,2,0:T(8,128)(2,1)S(1)} %copy-done, s32[26,1024]{1,0:T(8,128)S(1)} %bitcast.192), kind=kOutput, calls=%fused_computation.106 | convolution fusion | flops 2154813440 | bytes 4259840 | tf_op jit(solution)/shard_map/dot_general | solution.py:68
  65.6 3.1 reshape.79
  68.7 1.6 copy.48
  70.3 4.0 all-to-all-start.1
  75.1 45.0 %all-to-all-done.1 = bf16[8,1014,128]{2,1,0:T(8,128)(2,1)S(1)} async-done(((bf16[8,1014,128]{2,1,0:T(8,128)(2,1)}), bf16[8,1014,128]{2,1,0:T(8,128)(2,1)S(1)}, u32[]{:S(2)}, u32[]{:S(2)}) %all-to-all-start.1) | async-done | bytes 2076704 | tf_op jit(solution)/shard_map/all_to_all | solution.py:72
  120.1 1.6 copy.40
  121.7 3.1 reshape.80
  124.8 22.5 %fusion.66 = bf16[26,39,1024]{2,1,0:T(8,128)(2,1)} fusion(bf16[26,39,1024]{2,1,0:T(8,128)(2,1)S(1)} %reshape.80, s32[26,1024]{1,0:T(8,128)S(1)} %get-tuple-element.28), kind=kOutput, calls=%fused_computation.116 | convolution fusion | flops 2154813440 | bytes 4259840 | tf_op jit(solution)/shard_map/dot_general | solution.py:74
  147.3 4.1 reshape.81
  151.4 6.4 fusion.100
  157.8 4.7 fusion.13
  162.6 5.4 fusion.24
  168.1 6.3 fusion.20
  174.4 4.0 multiply_reduce_fusion.1
  179.6 4.9 fusion.52
  184.5 4.3 convert_reduce_fusion.3
  188.8 5.4 convert_reduce_fusion.4
  194.2 4.5 fusion.11
  198.7 6.4 convert_reduce_fusion
  205.2 4.5 fusion.10
  209.7 3.5 fusion.19
  213.2 4.9 fusion.16
  218.2 2.0 copy-done.11
  220.5 2.2 reshape.84
  222.7 24.0 %fusion.67 = bf16[26,39,1024]{2,1,0:T(8,128)(2,1)} fusion(bf16[26,39,1024]{2,1,0:T(8,128)(2,1)} %reshape.84, s32[26,1024]{1,0:T(8,128)S(1)} %get-tuple-element.28), kind=kOutput, calls=%fused_computation.117 | convolution fusion | flops 2154813440 | bytes 4259840 | tf_op jit(solution)/shard_map/dot_general | solution.py:122
  246.6 3.3 reshape.85
  250.0 1.6 copy.47
  251.5 5.8 all-to-all-start.2
  257.4 5.4 fusion.12
  262.9 4.3 pad_maximum_fusion
  267.2 47.5 %all-to-all-done.2 = bf16[8,1014,128]{2,1,0:T(8,128)(2,1)S(1)} async-done(((bf16[8,1014,128]{2,1,0:T(8,128)(2,1)}), bf16[8,1014,128]{2,1,0:T(8,128)(2,1)S(1)}, u32[]{:S(2)}, u32[]{:S(2)}) %all-to-all-start.2) | async-done | bytes 2076704 | tf_op jit(solution)/shard_map/all_to_all | solution.py:129
  314.7 1.6 copy.42
  316.3 4.3 reshape.86
  320.6 24.1 %convert_bitcast_fusion = bf16[26,1024,39]{1,2,0:T(8,128)(2,1)} fusion(bf16[26,39,1024]{2,1,0:T(8,128)(2,1)} %reshape.86, s32[26,1024]{1,0:T(8,128)S(1)} %bitcast.193), kind=kOutput, calls=%fused_computation.105 | convolution fusion | flops 2154813440 | bytes 4259840 | tf_op jit(solution)/shard_map/dot_general | solution.py:131
  344.8 6.5 fusion.99
  351.4 1.5 copy-done.9
  353.0 6.8 fusion.95
  359.8 1.4 concatenate.7
  361.2 46.5 %psum.21 = f32[7182]{0:T(1024)S(1)} all-reduce(f32[7182]{0:T(1024)S(1)} %concatenate.7), channel_id=1, replica_groups=mesh['section'=4,'dp'=8] {'section','dp'}, use_global_device_ids=true, to_apply=%region_12.13 | all-reduce | flops 7182 | bytes 57456 | tf_op jit(solution)/shard_map/psum | solution.py:139
  411.5 1.5 slice_bitcast_fusion
  413.1 48.6 %all-reduce.5.cloned.1.call-done = bf16[3,1027,1027]{2,1,0:T(8,128)(2,1)} async-done(((bf16[3,1027,1027]{2,1,0:T(8,128)(2,1)}), bf16[3,1027,1027]{2,1,0:T(8,128)(2,1)}) %all-reduce.5.cloned.1.call-update) | async-done | bytes 6328390 | tf_op jit(solution)/shard_map/psum | solution.py:146
  461.7 9.4 %convert_element_type.145 = f32[3,1027,1027]{2,1,0:T(8,128)} convert(bf16[3,1027,1027]{2,1,0:T(8,128)(2,1)} %all-reduce.5.cloned.1.call-done) | non-fusion elementwise | flops 3164187 | bytes 18985122 | tf_op jit(solution)/shard_map/convert_element_type | solution.py:146
  471.1 44.7 %all-reduce.3.cloned.1.call-done = bf16[26,1024,39]{1,2,0:T(8,128)(2,1)} async-done(((bf16[26,1024,39]{1,2,0:T(8,128)(2,1)}), bf16[26,1024,39]{1,2,0:T(8,128)(2,1)}) %all-reduce.3.cloned.1.call-update) | async-done | bytes 2076688 | tf_op jit(solution)/shard_map/psum | solution.py:134
  515.8 4.1 transpose.99
  519.9 108.4 %reduce-scatter.3.cloned.1.call-done = f32[32,1027]{1,0:T(8,128)} async-done(((f32[1024,1027]{1,0:T(8,128)}), f32[32,1027]{1,0:T(8,128)}) %reduce-scatter.3.cloned.1.call-update) | async-done | bytes 131472 | tf_op jit(solution)/shard_map/reduce_scatter | solution.py:147
  628.3 140.0 %reduce-scatter.5.cloned.1.call-done = f32[32,1024]{1,0:T(8,128)} async-done(((f32[1024,1024]{1,0:T(8,128)}), f32[32,1024]{1,0:T(8,128)}) %reduce-scatter.5.cloned.1.call-update) | async-done | bytes 131088 | tf_op jit(solution)/shard_map/reduce_scatter | solution.py:150
  (74 shorter events, 9.4 us)
Async XLA Ops:
  7.2 36.8 %copy-start = (bf16[26,1024,39]{1,2,0:T(8,128)(2,1)S(1)}, bf16[26,1024,39]{1,2,0:T(8,128)(2,1)}, u32[]{:S(2)}) copy-start(bf16[26,1024,39]{1,2,0:T(8,128)(2,1)} %param.15) | copy-start | bytes 6230020
  43.3 0.7 copy-start.12
  68.7 5.6 copy-start.14
  68.7 6.3 copy-start.15
  70.3 49.8 %all-to-all-start.1 = ((bf16[8,1014,128]{2,1,0:T(8,128)(2,1)}), bf16[8,1014,128]{2,1,0:T(8,128)(2,1)S(1)}, u32[]{:S(2)}, u32[]{:S(2)}) async-start(bf16[8,1014,128]{2,1,0:T(8,128)(2,1)} %bitcast.187), calls=%async_computation.1 | async-start | bytes 4161536 | tf_op jit(solution)/shard_map/all_to_all | solution.py:72
  147.3 4.1 copy-start.6
  147.3 4.1 copy-start.19
  151.4 6.4 copy-start.10
  168.0 6.4 copy-start.22
  168.0 6.4 copy-start.17
  168.0 6.4 copy-start.18
  168.0 6.4 copy-start.20
  168.1 6.4 copy-start.21
  174.4 4.0 copy-start.16
  188.8 5.4 copy-start.8
  194.2 15.4 %copy-start.2 = (bf16[1024,1024]{0,1:T(8,128)(2,1)}, bf16[1024,1024]{0,1:T(8,128)(2,1)S(1)}, u32[]{:S(2)}) copy-start(bf16[1024,1024]{0,1:T(8,128)(2,1)S(1)} %get-tuple-element.42) | copy-start | bytes 6291460
  205.2 4.5 copy-start.7
  218.2 2.0 copy-start.11
  251.5 63.2 %all-to-all-start.2 = ((bf16[8,1014,128]{2,1,0:T(8,128)(2,1)}), bf16[8,1014,128]{2,1,0:T(8,128)(2,1)S(1)}, u32[]{:S(2)}, u32[]{:S(2)}) async-start(bf16[8,1014,128]{2,1,0:T(8,128)(2,1)} %bitcast.185), calls=%async_computation.2 | async-start | bytes 4161536 | tf_op jit(solution)/shard_map/all_to_all | solution.py:129
  257.4 204.3 %all-reduce.5.cloned.1.call-start = ((), (), s32[]{:S(2)}) async-start(), calls=%async_computation.6 | async-start | bytes 14266368 | tf_op jit(solution)/shard_map/psum | solution.py:146
  257.4 5.5 copy-start.4
  257.4 5.4 copy-start.5
  267.2 53.4 %copy-start.13 = (s32[4,8,8,128]{3,1,2,0:T(8,128)S(1)}, s32[4,8,8,128]{3,1,2,0:T(8,128)}, u32[]{:S(2)}) copy-start(s32[4,8,8,128]{3,1,2,0:T(8,128)} %copy-done.12) | copy-start | bytes 393220
  267.2 248.6 %all-reduce.3.cloned.1.call-start = ((), (), s32[]{:S(2)}) async-start(), calls=%async_computation.5 | async-start | bytes 4259840 | tf_op jit(solution)/shard_map/psum | solution.py:134
  320.6 24.2 %copy-start.3 = (bf16[1024,1024]{0,1:T(8,128)(2,1)S(1)}, bf16[1024,1024]{0,1:T(8,128)(2,1)}, u32[]{:S(2)}) copy-start(bf16[1024,1024]{0,1:T(8,128)(2,1)} %copy-done.2) | copy-start | bytes 6291460
  344.8 283.6 %reduce-scatter.3.cloned.1.call-start = ((), (), s32[]{:S(2)}) async-start(), calls=%async_computation.7 | async-start | bytes 4866048 | tf_op jit(solution)/shard_map/reduce_scatter | solution.py:147
  351.4 1.6 copy-start.9
  351.4 416.9 %reduce-scatter.5.cloned.1.call-start = ((), (), s32[]{:S(2)}) async-start(), calls=%async_computation.8 | async-start | bytes 4325376 | tf_op jit(solution)/shard_map/reduce_scatter | solution.py:150
  461.7 306.6 %copy-start.1 = (bf16[26,1024,39]{1,2,0:T(8,128)(2,1)S(1)}, bf16[26,1024,39]{1,2,0:T(8,128)(2,1)}, u32[]{:S(2)}) copy-start(bf16[26,1024,39]{1,2,0:T(8,128)(2,1)} %param.15) | copy-start | bytes 6230020
Sparse Core Ops, SparseCore 0:
  267.3 194.3 all-reduce.4
  464.2 51.5 all-reduce.2
  522.8 105.5 reduce-scatter.2
  631.0 137.2 reduce-scatter.4

commit v2 on v1

--- a/solution.py
+++ b/solution.py
@@ -1,6 +1,8 @@
 import jax
 import jax.numpy as jnp
 from jax import lax
+from jax.experimental import pallas as pl
+from jax.experimental.pallas import tpu as pltpu
 from jax.sharding import PartitionSpec as P
 
 BF = jnp.bfloat16
@@ -16,6 +18,286 @@
 def gelu_parts(pre):
     act, back = jax.vjp(jax.nn.gelu, pre)
     return act, back(jnp.ones_like(pre))[0]
+
+
+VIEW = (2, 2, 4, 2)
+
+
+def reduce_kernel(
+    units, gathered, *refs
+):
+    grads = refs[:units]
+    table_ref, small_ref = refs[units : units + 2]
+    whole, pieces, table_out, small_out = refs[units + 2 : units + 6]
+    (rc, sa1, ra1, sb1, rb1, sa2, ra2, sb2, rb2, sz, rz, rtc, st, rt, sm, rm, rmz, send, recv) = refs[units + 6 :]
+    section, dp = lax.axis_index("section"), lax.axis_index("dp")
+    y, c = section // 2, section % 2
+    z, x = dp // 2, dp % 2
+    core_peer = (y * 2 + 1 - c, dp)
+    y_peer = ((1 - y) * 2 + c, dp)
+    x_peer = (section, z * 2 + 1 - x)
+    half = 512
+    lo, hi = pl.ds(0, half), pl.ds(half, half)
+
+    def z_peer(j):
+        return (section, lax.rem(z + j, 4) * 2 + x)
+
+    peers = [core_peer, y_peer, x_peer] + [z_peer(j) for j in (1, 2, 3)]
+    barrier = pltpu.get_barrier_semaphore()
+    for peer in peers:
+        pl.semaphore_signal(barrier, inc=1, device_id=peer, device_id_type=pl.DeviceIdType.MESH)
+    pl.semaphore_wait(barrier, len(peers))
+
+    flying = []
+
+    def start(src, dst, m, k, peer):
+        copy = pltpu.make_async_remote_copy(
+            src_ref=src,
+            dst_ref=dst,
+            send_sem=send.at[m, k],
+            recv_sem=recv.at[m, k],
+            device_id=peer,
+            device_id_type=pl.DeviceIdType.MESH,
+        )
+        copy.start()
+        flying.append(copy)
+        return copy
+
+    def wide(value):
+        return value.astype(F32)
+
+    copies = {}
+
+    def acc(m, stage, cols, yy, zz, xx):
+        g = grads[m]
+        total = wide(g[yy, c, zz, xx, :, cols]) + wide(rc[m, yy, zz, xx, :, cols])
+        if cols is lo:
+            if stage >= 2:
+                total += wide(ra1[m, yy, zz])
+            if stage >= 3:
+                total += wide(ra2[m, zz])
+        else:
+            if stage >= 2:
+                total += wide(rb1[m, zz, xx])
+            if stage >= 3:
+                total += wide(rb2[m, zz])
+        return total
+
+    def step0(m):
+        copies[m, 0] = start(grads[m].at[:, 1 - c], rc.at[m], m, 0, core_peer)
+
+    def step1(m):
+        copies[m, 0].wait_recv()
+
+        @pl.loop(0, 4)
+        def _(zz):
+            for i in range(2):
+                sa1[m, i, zz] = acc(m, 1, lo, i, zz, 1 - x).astype(BF)
+                sb1[m, zz, i] = acc(m, 1, hi, 1 - y, zz, i).astype(BF)
+
+        copies[m, 1] = start(sa1.at[m], ra1.at[m], m, 1, x_peer)
+        copies[m, 2] = start(sb1.at[m], rb1.at[m], m, 2, y_peer)
+
+    def step2(m):
+        copies[m, 1].wait_recv()
+        copies[m, 2].wait_recv()
+
+        @pl.loop(0, 4)
+        def _(zz):
+            sa2[m, zz] = acc(m, 2, lo, 1 - y, zz, x).astype(BF)
+            sb2[m, zz] = acc(m, 2, hi, y, zz, 1 - x).astype(BF)
+
+        copies[m, 3] = start(sa2.at[m], ra2.at[m], m, 3, y_peer)
+        copies[m, 4] = start(sb2.at[m], rb2.at[m], m, 4, x_peer)
+
+    def step3(m):
+        copies[m, 3].wait_recv()
+        copies[m, 4].wait_recv()
+        for j in (1, 2, 3):
+            zz = lax.rem(z + j, 4)
+            sz[m, j - 1, :, lo] = acc(m, 3, lo, y, zz, x).astype(BF)
+            sz[m, j - 1, :, hi] = acc(m, 3, hi, y, zz, x).astype(BF)
+            copies[m, 4 + j] = start(sz.at[m, j - 1], rz.at[m, j - 1], m, 4 + j, z_peer(j))
+
+    def step4(m):
+        for j in (1, 2, 3):
+            copies[m, 4 + j].wait_recv()
+        for cols in (lo, hi):
+            total = acc(m, 3, cols, y, z, x)
+            for j in range(3):
+                total += wide(rz[m, j, :, cols])
+            if m < gathered:
+                whole[m, y, c, z, x, :, cols] = total.astype(BF)
+            else:
+                pieces[m - gathered, :, cols] = total
+        if m < gathered:
+            for j in (1, 2, 3):
+                mine = whole.at[m, y, c, z, x]
+                copies[m, 7 + j] = start(mine, mine, m, 7 + j, z_peer(j))
+
+    def step5(m):
+        for j in (1, 2, 3):
+            copies[m, 7 + j].wait_recv()
+        ours = whole.at[m, y, c, :, x, :, lo]
+        copies[m, 11] = start(ours, ours, m, 11, y_peer)
+        ours = whole.at[m, y, c, :, x, :, hi]
+        copies[m, 12] = start(ours, ours, m, 12, x_peer)
+
+    def step6(m):
+        copies[m, 11].wait_recv()
+        copies[m, 12].wait_recv()
+        ours = whole.at[m, :, c, :, x, :, lo]
+        copies[m, 13] = start(ours, ours, m, 13, x_peer)
+        ours = whole.at[m, y, c, :, :, :, hi]
+        copies[m, 14] = start(ours, ours, m, 14, y_peer)
+
+    def step7(m):
+        copies[m, 13].wait_recv()
+        copies[m, 14].wait_recv()
+        ours = whole.at[m, :, c]
+        copies[m, 15] = start(ours, ours, m, 15, core_peer)
+
+    def step8(m):
+        copies[m, 15].wait_recv()
+
+    t = units
+
+    def table0():
+        copies[t, 0] = start(table_ref.at[:, 1 - c], rtc, t, 0, core_peer)
+
+    def table1():
+        copies[t, 0].wait_recv()
+
+        @pl.loop(0, 8)
+        def _(i):
+            rows = pl.ds(pl.multiple_of(i * 32, 32), 32)
+            st[rows] = (wide(table_ref[1 - y, c, rows]) + wide(rtc[1 - y, rows])).astype(BF)
+
+        copies[t, 1] = start(st, rt, t, 1, y_peer)
+
+    def table2():
+        copies[t, 1].wait_recv()
+
+        @pl.loop(0, 8)
+        def _(i):
+            rows = pl.ds(pl.multiple_of(i * 32, 32), 32)
+            total = wide(table_ref[y, c, rows]) + wide(rtc[y, rows]) + wide(rt[rows])
+            table_out[y, c, rows] = total.astype(BF)
+
+        ours = table_out.at[y, c]
+        copies[t, 2] = start(ours, ours, t, 2, y_peer)
+
+    def table3():
+        copies[t, 2].wait_recv()
+        ours = table_out.at[:, c]
+        copies[t, 3] = start(ours, ours, t, 3, core_peer)
+
+    def table4():
+        copies[t, 3].wait_recv()
+
+    s = units + 1
+
+    def small0():
+        copies[s, 0] = start(small_ref.at[1 - c], rm.at[0], s, 0, core_peer)
+
+    def small1():
+        copies[s, 0].wait_recv()
+        sm[0] = small_ref[c] + rm[0]
+        copies[s, 1] = start(sm.at[0], rm.at[1], s, 1, x_peer)
+
+    def small2():
+        copies[s, 1].wait_recv()
+        sm[1] = sm[0] + rm[1]
+        copies[s, 2] = start(sm.at[1], rm.at[2], s, 2, y_peer)
+
+    def small3():
+        copies[s, 2].wait_recv()
+        sm[2] = sm[1] + rm[2]
+        for j in (1, 2, 3):
+            copies[s, 2 + j] = start(sm.at[2], rmz.at[j - 1], s, 2 + j, z_peer(j))
+
+    def small4():
+        for j in (1, 2, 3):
+            copies[s, 2 + j].wait_recv()
+        even = lax.rem(z, 2)
+        near = [sm[2], rmz[0], rmz[1], rmz[2]]
+        first = near[0] + near[2]
+        second = near[1] + near[3]
+        small_out[c] = jnp.where(even == 0, first, second) + jnp.where(even == 0, second, first)
+        ours = small_out.at[c]
+        copies[s, 6] = start(ours, ours, s, 6, core_peer)
+
+    def small5():
+        copies[s, 6].wait_recv()
+
+    small0()
+    for m in range(units):
+        step0(m)
+    table0()
+    steps = [step1, step2, step3, step4, step5, step6, step7, step8]
+    extras = [small1, small2, table1, small3, table2, small4, table3, small5, table4]
+    for now in range(units + len(steps)):
+        for k, step in enumerate(steps):
+            m = now - k
+            if 0 <= m < units and (k < 4 or m < gathered):
+                step(m)
+        if now < len(extras):
+            extras[now]()
+    for copy in flying:
+        copy.wait_send()
+
+
+def reduce_all(grads, gathered, table_g, small):
+    units = len(grads)
+    piece = (32, 1024)
+    vmem = pl.BlockSpec(memory_space=pltpu.VMEM)
+    outs = pl.pallas_call(
+        lambda *refs: reduce_kernel(units, gathered, *refs),
+        out_shape=[
+            jax.ShapeDtypeStruct((gathered,) + VIEW + piece, BF),
+            jax.ShapeDtypeStruct((units - gathered,) + piece, F32),
+            jax.ShapeDtypeStruct((2, 2, 256, 1024), BF),
+            jax.ShapeDtypeStruct((2, 16, 1024), F32),
+        ],
+        in_specs=[vmem] * (units + 2),
+        out_specs=[vmem] * 4,
+        scratch_shapes=[
+            pltpu.VMEM((units, 2, 4, 2) + piece, BF),
+            pltpu.VMEM((units, 2, 4, 32, 512), BF),
+            pltpu.VMEM((units, 2, 4, 32, 512), BF),
+            pltpu.VMEM((units, 4, 2, 32, 512), BF),
+            pltpu.VMEM((units, 4, 2, 32, 512), BF),
+            pltpu.VMEM((units, 4, 32, 512), BF),
+            pltpu.VMEM((units, 4, 32, 512), BF),
+            pltpu.VMEM((units, 4, 32, 512), BF),
+            pltpu.VMEM((units, 4, 32, 512), BF),
+            pltpu.VMEM((units, 3) + piece, BF),
+            pltpu.VMEM((units, 3) + piece, BF),
+            pltpu.VMEM((2, 256, 1024), BF),
+            pltpu.VMEM((256, 1024), BF),
+            pltpu.VMEM((256, 1024), BF),
+            pltpu.VMEM((3, 16, 1024), F32),
+            pltpu.VMEM((3, 16, 1024), F32),
+            pltpu.VMEM((3, 16, 1024), F32),
+            pltpu.SemaphoreType.DMA((units + 2, 16)),
+            pltpu.SemaphoreType.DMA((units + 2, 16)),
+        ],
+        compiler_params=pltpu.CompilerParams(
+            collective_id=0, has_side_effects=True, vmem_limit_bytes=56 * 2**20
+        ),
+        name="reduce_all",
+    )(
+        *[g.reshape(VIEW + piece) for g in grads],
+        table_g.reshape(2, 2, 256, 1024),
+        small.reshape(2, 16, 1024),
+    )
+    whole, pieces, table_sum, small_sum = outs
+    return (
+        whole.reshape(gathered, 1024, 1024),
+        pieces,
+        table_sum.reshape(1024, 1024),
+        small_sum.reshape(-1),
+    )
 
 
 def body(
@@ -131,25 +413,57 @@
     table_g = lax.dot_general(
         delivered, row_hot, (((2,), (2,)), ((0,), (0,))), preferred_element_type=F32
     )
-    table_g = lax.psum(table_g.astype(BF), "section").astype(F32).transpose(0, 2, 1)
-
     small = jnp.concatenate(
         cross_b + [head_grad, jnp.sum(s).reshape(1), loss.reshape(1)] + tower_biases
     )
-    small = lax.psum(small, ("section", "dp"))
+    both = ("section", "dp")
+    share = hidden // device_count
+    main = hidden
+    if (sections, groups) == (4, 8):
+        edges = [jnp.concatenate([g[main:].reshape(-1), g[:main, main:].reshape(-1)]) for g in cross_g]
+        edges.append(tower_in_g[:, main:].reshape(-1))
+        flat = jnp.concatenate([small] + edges)
+        filled = jnp.zeros((32 * 1024,), F32).at[: flat.shape[0]].set(flat)
+        table_flat = jnp.pad(
+            table_g.astype(BF).reshape(sparse, table_rows), ((0, 1024 - sparse), (0, 0))
+        )
+        whole, pieces32, table_sum, flat = reduce_all(
+            [g[:main, :main].astype(BF) for g in cross_g]
+            + [tower_in_g[:, :main].astype(BF), tower_out_g.astype(BF)],
+            layers,
+            table_flat,
+            filled.reshape(32, 1024),
+        )
+        table_g = table_sum[:sparse].reshape(fields, edim, table_rows)
+        at = small.shape[0]
+        small = flat[:at]
+        rest = width - main
+        crosses = []
+        for layer in range(layers):
+            bottom = flat[at : at + rest * width].reshape(rest, width)
+            at += rest * width
+            side = flat[at : at + main * rest].reshape(main, rest)
+            at += main * rest
+            top = jnp.concatenate([whole[layer].astype(F32), side], axis=1)
+            crosses.append(jnp.concatenate([top, bottom], axis=0))
+        cross_out = jnp.stack(crosses)
+        side = lax.dynamic_slice(
+            flat[at : at + hidden * rest].reshape(hidden, rest), (me * share, 0), (share, rest)
+        )
+        tower_in_out = jnp.concatenate([pieces32[0], side], axis=1)
+        tower_out_out = pieces32[1]
+    else:
+        table_g = lax.psum(table_g, "section")
+        small = lax.psum(small, both)
+        cross_out = lax.psum(jnp.stack(cross_g), both)
+        tower_in_out = lax.psum_scatter(tower_in_g, both, scatter_dimension=0, tiled=True)
+        tower_out_out = lax.psum_scatter(tower_out_g, both, scatter_dimension=0, tiled=True)
+    table_g = table_g.astype(F32).transpose(0, 2, 1)
     sizes = [layers * width, width + hidden, 1, 1, hidden, hidden]
     ends = [sum(sizes[: i + 1]) for i in range(len(sizes))]
     pieces = [small[e - n : e] for e, n in zip(ends, sizes)]
     cross_b_out = pieces[0].reshape(layers, width)
-    share = hidden // device_count
     bias_in, bias_out = (lax.dynamic_slice(p, (me * share,), (share,)) for p in pieces[4:])
-    cross_out = lax.psum(jnp.stack(cross_g).astype(BF), ("section", "dp")).astype(F32)
-    tower_in_out = lax.psum_scatter(
-        tower_in_g, ("section", "dp"), scatter_dimension=0, tiled=True
-    )
-    tower_out_out = lax.psum_scatter(
-        tower_out_g, ("section", "dp"), scatter_dimension=0, tiled=True
-    )
     return (
         probs,
         pieces[3] / (examples * device_count),
@@ -157,9 +471,9 @@
         table_g,
         cross_out,
         cross_b_out,
-        tower_in_out.astype(F32).T,
+        tower_in_out.T,
         bias_in,
-        tower_out_out.astype(F32).T,
+        tower_out_out.T,
         bias_out,
         pieces[1],
         pieces[2],

time: 792 us -> 490 us (0.62)
  waiting for transfers between devices: 434 us -> 50.2 us
  Pallas kernels: 0 us -> 113 us
  blocking collectives: 59.1 us -> 12.6 us
  local copies, waits for them, and re-layouts: 37.5 us -> 68.5 us
  between operations: 17.1 us -> 4.01 us
    reduce_scatter x2 -> x0, waiting for transfers between devices: 248 us -> none  [the longest x1 140 us: body(): lax.psum_scatter(tower_out_g, ('section', 'dp'), scatter_dimension=0, til...]
    pallas_call x0 -> x1, Pallas kernels: none -> 113 us  [reduce_all(): pl.pallas_call(lambda *refs: reduce_kernel(units, gathered, *refs), out_s...]
    psum x2 -> x0, waiting for transfers between devices: 93.3 us -> none  [the longest x1 48.6 us: body(): lax.psum(jnp.stack(cross_g).astype(BF), ('section', 'dp')).astype(F32)]
    psum x1 -> x0, blocking collectives: 46.5 us -> none  [body(): small = lax.psum(small, ('section', 'dp'))]
    all_to_all x1, waiting for transfers between devices: 47.5 us -> 5.2 us  [body(): delivered = lax.all_to_all(packed, 'dp', 0, 0, tiled=True)]
    another operation x1 -> x4, other arithmetic: 4.27 us -> 19.4 us  [body(): cross_out = jnp.stack(crosses)]
    slice x0 -> x16, local copies, waits for them, and re-layouts: none -> 13.3 us  [the longest x3 5.05 us: body(): g[:main, :main].astype(BF)]
  transfers between devices with their start and end apart: 6 -> 2, of which waited for: 6 -> 2; matrix products, arithmetic and copies ran while one was open for 9% -> 8% of each run, Pallas kernels for 0% -> 0%
where the time goes in v2:
time: 490 us; the launch traced here: 482 us
  matrix products  191 us (39%)
  Pallas kernels  113 us (23%)
  local copies, waits for them, and re-layouts  68.5 us (14%)
  waiting for transfers between devices  50.2 us (10%)
  other arithmetic  32.4 us (7%)
  blocking collectives  12.6 us (3%)
  starting transfers between devices  10.2 us (2%)
    pallas_call x1, Pallas kernels, reduce_all(): pl.pallas_call(lambda *refs: reduce_kernel(units, gathered, *refs), out_s...  113 us
    dot_general x16, matrix products, mm(): lax.dot_general(left, right, ((contract[:1], contract[1:]), ((), ())), pr...  79 us
    all_to_all x1, waiting for transfers between devices, body(): replies = lax.all_to_all(found, 'dp', 0, 0, tiled=True)  45 us
    dot_general x1, matrix products, body(): lax.dot_general(dx0[:sparse].astype(BF).reshape(fields, edim, examples),...  24.1 us
    dot_general x1, matrix products, body(): lax.dot_general(delivered, row_hot, (((2,), (2,)), ((0,), (0,))), preferr...  24 us
    dot_general x1, matrix products, body(): lax.dot_general(replies, slot_hot, (((2,), (1,)), ((0,), (0,))), preferre...  22.5 us
    dot_general x1, matrix products, body(): lax.dot_general(table_t, row_hot, (((2,), (1,)), ((0,), (0,))), preferred...  21.6 us
    dot_general x1, matrix products, body(): lax.dot_general(halves, slot_hot, (((2,), (2,)), ((0,), (0,))), preferred...  19.9 us
  transfers between devices with their start and end apart: 2, of which 2 were waited for; matrix products, arithmetic and copies ran while one was open for 8% of the time, Pallas kernels for 0%

profile of v2, /device:TPU:1, one launch (start us, length us, event | category | flops | bytes accessed | tf_op | source)
XLA Modules:
  0.0 482.3 jit_solution(13757892028679338072)
XLA Ops:
  3.9 19.9 %fusion.4 = f32[26,2,1024]{2,1,0:T(2,128)S(1)} fusion(s32[26,1024]{1,0:T(8,128)S(1)} %get-tuple-element.65, bf16[26,1,1024]{2,1,0:T(2,128)(2,1)S(1)} %copy.43, bf16[26,1,1024]{2,1,0:T(2,128)(2,1)S(1)} %copy.42), kind=kOutput, calls=%fused_computation.6 | convolution fusion | flops 136527872 | bytes 425984 | tf_op jit(solution)/shard_map/dot_general | solution.py:339
  24.1 12.6 %all_to_all.15 = s32[8,26,128]{2,1,0:T(8,128)S(1)} all-to-all(s32[8,26,128]{2,1,0:T(8,128)S(1)} %bitcast.222), channel_id=1, replica_groups=mesh['section'=4,'dp'=8] {'dp'}, dimensions={0} | all-to-all | bytes 212992 | tf_op jit(solution)/shard_map/all_to_all | solution.py:344
  37.5 21.6 %convert_bitcast_fusion = bf16[26,39,1024]{2,1,0:T(8,128)(2,1)} fusion(bf16[26,1024,39]{1,2,0:T(8,128)(2,1)S(1)} %copy-done, s32[26,1024]{1,0:T(8,128)S(1)} %bitcast.226), kind=kOutput, calls=%fused_computation.106 | convolution fusion | flops 2154813440 | bytes 4259840 | tf_op jit(solution)/shard_map/dot_general | solution.py:350
  59.1 3.1 reshape.186
  63.8 4.1 all-to-all-start.1
  68.8 45.0 %all-to-all-done.1 = bf16[8,1014,128]{2,1,0:T(8,128)(2,1)S(1)} async-done(((bf16[8,1014,128]{2,1,0:T(8,128)(2,1)}), bf16[8,1014,128]{2,1,0:T(8,128)(2,1)S(1)}, u32[]{:S(2)}, u32[]{:S(2)}) %all-to-all-start.1) | async-done | bytes 2076704 | tf_op jit(solution)/shard_map/all_to_all | solution.py:354
  115.3 3.1 reshape.187
  118.4 22.5 %fusion.63 = bf16[26,39,1024]{2,1,0:T(8,128)(2,1)} fusion(bf16[26,39,1024]{2,1,0:T(8,128)(2,1)S(1)} %reshape.187, s32[26,1024]{1,0:T(8,128)S(1)} %get-tuple-element.65), kind=kOutput, calls=%fused_computation.120 | convolution fusion | flops 2154813440 | bytes 4259840 | tf_op jit(solution)/shard_map/dot_general | solution.py:356
  140.9 4.2 reshape.188
  145.2 4.7 fusion.100
  150.0 6.2 %fusion.10 = f32[1027,1024]{1,0:T(8,128)S(1)} fusion(f32[1027]{0:T(1024)S(1)} %get-tuple-element.36, bf16[3,1027,1027]{2,1,0:T(8,128)(2,1)} %param.18, bf16[13,1024]{1,0:T(8,128)(2,1)S(1)} %bitcast.230, bf16[1014,1024]{1,0:T(8,128)(2,1)S(1)} %copy-done.13), kind=kOutput, calls=%fused_computation.38 | convolution fusion | flops 2165343232 | bytes 8691724 | tf_op jit(solution)/shard_map/dot_general | solution.py:13
  156.2 8.2 %fusion.21 = (bf16[1027,1024]{1,0:T(8,128)(2,1)}, f32[1027,1024]{1,0:T(8,128)S(1)}) fusion(bf16[13,1024]{1,0:T(8,128)(2,1)S(1)} %bitcast.231, bf16[1014,1024]{1,0:T(8,128)(2,1)S(1)} %copy-done.13, f32[1027,1024]{1,0:T(8,128)S(1)} %fusion.10, f32[1027]{0:T(1024)S(1)} %get-tuple-element.37, bf16[3,1027,1027]{2,1,0:T(8,128)(2,1)} %param.18), kind=kOutput, calls=%fused_computation.53 | convolution fusion | flops 2180066304 | bytes 21377024 | tf_op jit(solution)/shard_map/dot_general | solution.py:13
  164.5 7.1 %fusion.17 = (f32[1024]{0:T(1024)S(1)}, bf16[1027,1024]{1,0:T(8,128)(2,1)S(1)}, f32[1027,1024]{1,0:T(8,128)S(1)}) fusion(f32[1027]{0:T(1024)S(1)} %slice.163, bf16[1027,1024]{1,0:T(8,128)(2,1)} %get-tuple-element.68, bf16[13,1024]{1,0:T(8,128)(2,1)S(1)} %bitcast.232, bf16[1014,1024]{1,0:T(8,128)(2,1)S(1)} %copy-done.13, f32[1027]{0:T(1024)S(1)} %get-tuple-element.35, ...), kind=kOutput, calls=%fused_computation.49 | convolution fusion | flops 2172703744 | bytes 15030296 | tf_op jit(solution)/shard_map/dot_general | solution.py:13
  171.7 3.7 multiply_reduce_fusion.1
  176.6 4.9 %fusion.49 = bf16[1027,1024]{1,0:T(8,128)(2,1)S(1)} fusion(f32[1024]{0:T(1024)S(1)} %get-tuple-element.42, f32[1027]{0:T(1024)S(1)} %slice.163, bf16[3,1027,1027]{2,1,0:T(8,128)(2,1)} %param.18, bf16[13,1024]{1,0:T(8,128)(2,1)S(1)} %bitcast.233, bf16[1014,1024]{1,0:T(8,128)(2,1)S(1)} %copy-done.13), kind=kOutput, calls=%fused_computation.98 | convolution fusion | flops 2174808064 | bytes 6619136 | tf_op jit(solution)/shard_map/dot_general | solution.py:13
  181.5 4.3 convert_reduce_fusion.3
  185.8 5.4 %convert_reduce_fusion.4 = (f32[1024]{0:T(1024)S(1)}, bf16[1024,1024]{0,1:T(8,128)(2,1)S(1)}) fusion(f32[1024,1024]{1,0:T(8,128)S(1)} %copy-done.28, f32[1024]{0:T(1024)S(1)} %copy-done.26, bf16[1024,1024]{0,1:T(8,128)(2,1)S(1)} %get-tuple-element.40, bf16[1024,1024]{1,0:T(8,128)(2,1)S(1)} %copy-done.24), kind=kOutput, calls=%fused_computation.91 | convolution fusion | flops 2170551296 | bytes 10493952 | tf_op jit(solution)/shard_map/dot_general | solution.py:13
  191.3 7.3 %convert_reduce_fusion = (f32[1027]{0:T(1024)S(1)}, f32[1027]{0:T(1024)S(1)}, f32[1027]{0:T(1024)S(1)}, f32[1027]{0:T(1024)S(1)}, bf16[1027,1024]{1,0:T(8,128)(2,1)S(1)}) fusion(f32[1027]{0:T(1024)S(1)} %slice.163, f32[1024]{0:T(1024)S(1)} %get-tuple-element.42, bf16[13,1024]{1,0:T(8,128)(2,1)S(1)} %bitcast.234, bf16[1014,1024]{1,0:T(8,128)(2,1)S(1)} %copy-done.13, ...), kind=kOutput, calls=%fused_computation.59 | convolution fusion | flops 2194785280 | bytes 15077424 | tf_op jit(solution)/shard_map/dot_general | solution.py:13
  198.7 3.4 fusion.16
  202.1 4.9 %fusion.13 = f32[1027,1024]{1,0:T(8,128)S(1)} fusion(f32[1027,1024]{1,0:T(8,128)S(1)} %fusion.16, bf16[1027,1024]{1,0:T(8,128)(2,1)S(1)} %get-tuple-element.73, bf16[3,1027,1027]{2,1,0:T(8,128)(2,1)} %param.18, bf16[13,1024]{1,0:T(8,128)(2,1)S(1)} %bitcast.235, bf16[1014,1024]{1,0:T(8,128)(2,1)S(1)} %copy-done.13), kind=kOutput, calls=%fused_computation.42 | convolution fusion | flops 2170601472 | bytes 17152000 | tf_op jit(solution)/shard_map/dot_general | solution.py:13
  207.0 2.0 copy-done.17
  209.3 2.1 reshape.194
  211.4 24.1 %fusion.64 = bf16[26,39,1024]{2,1,0:T(8,128)(2,1)} fusion(bf16[26,39,1024]{2,1,0:T(8,128)(2,1)} %reshape.194, s32[26,1024]{1,0:T(8,128)S(1)} %get-tuple-element.65), kind=kOutput, calls=%fused_computation.121 | convolution fusion | flops 2154813440 | bytes 4259840 | tf_op jit(solution)/shard_map/dot_general | solution.py:404
  235.6 3.1 reshape.195
  240.3 6.1 %all-to-all-start.2 = ((bf16[8,1014,128]{2,1,0:T(8,128)(2,1)}), bf16[8,1014,128]{2,1,0:T(8,128)(2,1)}, u32[]{:S(2)}, u32[]{:S(2)}) async-start(bf16[8,1014,128]{2,1,0:T(8,128)(2,1)} %bitcast.203), calls=%async_computation.2 | async-start | bytes 4161536 | tf_op jit(solution)/shard_map/all_to_all | solution.py:411
  246.4 7.1 %fusion.75 = f32[1027,1027]{1,0:T(8,128)S(1)} fusion(bf16[1027,1024]{1,0:T(8,128)(2,1)} %copy-done.5, bf16[13,1024]{1,0:T(8,128)(2,1)S(1)} %bitcast.236, bf16[1014,1024]{1,0:T(8,128)(2,1)} %reshape.188, f32[1027,1024]{1,0:T(8,128)} %copy-done.2), kind=kOutput, calls=%fused_computation.128 | convolution fusion | flops 2174808064 | bytes 12632100 | tf_op jit(solution)/shard_map/dot_general | solution.py:13
  253.5 1.7 slice.270
  258.1 2.4 fusion.99
  262.1 3.1 fusion.93
  265.3 1.7 slice.269
  267.3 3.0 fusion.67
  271.2 1.6 slice.271
  273.2 2.9 copy.48
  281.0 6.7 %convolution_convert_fusion = bf16[1024,1024]{1,0:T(8,128)(2,1)} fusion(bf16[1024,1024]{0,1:T(8,128)(2,1)} %copy-done.12, f32[1024,1024]{1,0:T(8,128)} %copy-done.27, f32[1024]{0:T(1024)S(1)} %copy-done.26), kind=kOutput, calls=%fused_computation.123 | convolution fusion | flops 2159017984 | bytes 8392704 | tf_op jit(solution)/shard_map/dot_general | solution.py:13
  287.8 5.2 %all-to-all-done.2 = bf16[8,1014,128]{2,1,0:T(8,128)(2,1)} async-done(((bf16[8,1014,128]{2,1,0:T(8,128)(2,1)}), bf16[8,1014,128]{2,1,0:T(8,128)(2,1)}, u32[]{:S(2)}, u32[]{:S(2)}) %all-to-all-start.2) | async-done | bytes 2076704 | tf_op jit(solution)/shard_map/all_to_all | solution.py:411
  293.0 1.9 copy.50
  294.8 2.2 reshape.196
  297.0 24.0 %fusion.65 = bf16[26,39,1024]{2,1,0:T(8,128)(2,1)} fusion(bf16[26,39,1024]{2,1,0:T(8,128)(2,1)} %reshape.196, s32[26,1024]{1,0:T(8,128)S(1)} %bitcast.227), kind=kOutput, calls=%fused_computation.122 | convolution fusion | flops 2154813440 | bytes 4259840 | tf_op jit(solution)/shard_map/dot_general | solution.py:413
  321.0 2.8 reshape.197
  325.3 113.1 %reduce_all.1 = (bf16[3,2,2,4,2,32,1024]{6,5,4,3,2,1,0:T(8,128)(2,1)}, f32[2,32,1024]{2,1,0:T(8,128)}, bf16[2,2,256,1024]{3,2,1,0:T(8,128)(2,1)}, f32[2,16,1024]{2,1,0:T(8,128)}) custom-call(bf16[2,2,4,2,32,1024]{5,4,3,2,1,0:T(8,128)(2,1)} %bitcast.209, bf16[2,2,4,2,32,1024]{5,4,3,2,1,0:T(8,128)(2,1)} %bitcast.207, ...), custom_call_target="tpu_custom_call" | custom-call | tf_op jit(solution)/shard_map/reduce_all/pallas_call | solution.py:254
  443.1 1.7 slice_bitcast_fusion
  447.0 2.5 slice_convert_fusion.5
  449.5 5.1 %reshape.221 = f32[26,39,1024]{2,1,0:T(8,128)} reshape(f32[1014,1024]{1,0:T(8,128)} %slice_convert_fusion.5) | data formatting | bytes 8306688 | tf_op jit(solution)/shard_map/transpose | solution.py:461
  454.6 3.7 fusion.106
  461.6 2.7 maximum_bitcast_fusion
  464.3 2.6 maximum_bitcast_fusion.2
  466.8 2.6 maximum_bitcast_fusion.1
  469.5 11.5 %pad_maximum_fusion = f32[3,1027,1027]{2,1,0:T(8,128)} fusion(f32[1,1027,1027]{2,1,0:T(8,128)} %maximum_bitcast_fusion.2, f32[1,1027,1027]{2,1,0:T(8,128)} %maximum_bitcast_fusion.1, f32[1,1027,1027]{2,1,0:T(8,128)} %maximum_bitcast_fusion), kind=kLoop, calls=%fused_computation.12 | loop fusion | flops 6328374 | bytes 25313496 | tf_op jit(solution)/shard_map/stack | solution.py:449
  (119 shorter events, 32.6 us)
Async XLA Ops:
  0.6 36.9 %copy-start = (bf16[26,1024,39]{1,2,0:T(8,128)(2,1)S(1)}, bf16[26,1024,39]{1,2,0:T(8,128)(2,1)}, u32[]{:S(2)}) copy-start(bf16[26,1024,39]{1,2,0:T(8,128)(2,1)} %param.17) | copy-start | bytes 6230020
  36.8 0.7 copy-start.18
  62.2 5.7 %copy-start.20 = (f32[2051]{0:T(1024)S(1)}, f32[2051]{0:T(1024)}, u32[]{:S(2)}) copy-start(f32[2051]{0:T(1024)} %param.24) | copy-start | bytes 24616
  62.3 6.5 %copy-start.21 = (f32[3,1027]{1,0:T(4,128)S(1)}, f32[3,1027]{1,0:T(4,128)}, u32[]{:S(2)}) copy-start(f32[3,1027]{1,0:T(4,128)} %param.19) | copy-start | bytes 36976
  63.8 49.9 %all-to-all-start.1 = ((bf16[8,1014,128]{2,1,0:T(8,128)(2,1)}), bf16[8,1014,128]{2,1,0:T(8,128)(2,1)S(1)}, u32[]{:S(2)}, u32[]{:S(2)}) async-start(bf16[8,1014,128]{2,1,0:T(8,128)(2,1)} %bitcast.213), calls=%async_computation.1 | async-start | bytes 4161536 | tf_op jit(solution)/shard_map/all_to_all | solution.py:354
  140.9 4.3 copy-start.8
  140.9 4.3 copy-start.25
  145.2 4.7 copy-start.13
  149.9 21.7 %copy-start.27 = (f32[1024,1024]{1,0:T(8,128)}, f32[1024,1024]{1,0:T(8,128)S(1)}, u32[]{:S(2)}) copy-start(f32[1024,1024]{1,0:T(8,128)S(1)} %fusion.100) | copy-start | bytes 12582916
  156.2 42.4 %copy-start.2 = (f32[1027,1024]{1,0:T(8,128)}, f32[1027,1024]{1,0:T(8,128)S(1)}, u32[]{:S(2)}) copy-start(f32[1027,1024]{1,0:T(8,128)S(1)} %fusion.10) | copy-start | bytes 12619780
  164.5 7.2 %copy-start.23 = (f32[1024]{0:T(1024)S(1)}, f32[1024]{0:T(1024)}, u32[]{:S(2)}) copy-start(f32[1024]{0:T(1024)} %param.23) | copy-start | bytes 12292
  164.5 7.2 %copy-start.24 = (bf16[1024,1024]{1,0:T(8,128)(2,1)S(1)}, bf16[1024,1024]{1,0:T(8,128)(2,1)}, u32[]{:S(2)}) copy-start(bf16[1024,1024]{1,0:T(8,128)(2,1)} %param.22) | copy-start | bytes 6291460
  164.5 7.2 %copy-start.26 = (f32[1024]{0:T(1024)S(1)}, f32[1024]{0:T(1024)}, u32[]{:S(2)}) copy-start(f32[1024]{0:T(1024)} %param.21) | copy-start | bytes 12292
  171.7 3.7 copy-start.22
  181.5 17.2 %copy-start.5 = (bf16[1027,1024]{1,0:T(8,128)(2,1)}, bf16[1027,1024]{1,0:T(8,128)(2,1)S(1)}, u32[]{:S(2)}) copy-start(bf16[1027,1024]{1,0:T(8,128)(2,1)S(1)} %fusion.49) | copy-start | bytes 6309892
  181.5 4.4 copy-start.28
  185.8 5.4 %copy-start.12 = (bf16[1024,1024]{0,1:T(8,128)(2,1)}, bf16[1024,1024]{0,1:T(8,128)(2,1)S(1)}, u32[]{:S(2)}) copy-start(bf16[1024,1024]{0,1:T(8,128)(2,1)S(1)} %get-tuple-element.40) | copy-start | bytes 6291460
  191.3 7.4 %copy-start.6 = (bf16[1024,1024]{0,1:T(8,128)(2,1)}, bf16[1024,1024]{0,1:T(8,128)(2,1)S(1)}, u32[]{:S(2)}) copy-start(bf16[1024,1024]{0,1:T(8,128)(2,1)S(1)} %get-tuple-element.75) | copy-start | bytes 6291460
  191.3 7.4 %copy-start.9 = (bf16[1027,1024]{1,0:T(8,128)(2,1)S(1)}, bf16[1027,1024]{1,0:T(8,128)(2,1)}, u32[]{:S(2)}) copy-start(bf16[1027,1024]{1,0:T(8,128)(2,1)} %param.20) | copy-start | bytes 6309892
  198.6 3.4 copy-start.3
  207.0 2.0 copy-start.17
  240.3 52.7 %all-to-all-start.2 = ((bf16[8,1014,128]{2,1,0:T(8,128)(2,1)}), bf16[8,1014,128]{2,1,0:T(8,128)(2,1)}, u32[]{:S(2)}, u32[]{:S(2)}) async-start(bf16[8,1014,128]{2,1,0:T(8,128)(2,1)} %bitcast.203), calls=%async_computation.2 | async-start | bytes 4161536 | tf_op jit(solution)/shard_map/all_to_all | solution.py:411
  253.5 7.0 %copy-start.16 = (f32[1027,1027]{1,0:T(8,128)}, f32[1027,1027]{1,0:T(8,128)S(1)}, u32[]{:S(2)}) copy-start(f32[1027,1027]{1,0:T(8,128)S(1)} %fusion.75) | copy-start | bytes 12656752
  253.5 3.1 copy-start.7
  253.5 4.6 copy-start.14
  260.5 1.6 copy-start.29
  265.2 2.1 copy-start.4
  270.3 2.5 slice-start
  273.2 3.9 copy-start.11
  287.8 9.2 %copy-start.19 = (s32[4,8,8,128]{3,1,2,0:T(8,128)S(1)}, s32[4,8,8,128]{3,1,2,0:T(8,128)}, u32[]{:S(2)}) copy-start(s32[4,8,8,128]{3,1,2,0:T(8,128)} %copy-done.18) | copy-start | bytes 393220
  438.5 8.6 %copy-start.15 = (bf16[2,2,256,1024]{3,2,1,0:T(8,128)(2,1)S(1)}, bf16[2,2,256,1024]{3,2,1,0:T(8,128)(2,1)}, u32[]{:S(2)}) copy-start(bf16[2,2,256,1024]{3,2,1,0:T(8,128)(2,1)} %get-tuple-element.29) | copy-start | bytes 6291460
  460.3 1.3 copy-start.10
  469.5 11.5 %copy-start.1 = (bf16[26,1024,39]{1,2,0:T(8,128)(2,1)S(1)}, bf16[26,1024,39]{1,2,0:T(8,128)(2,1)}, u32[]{:S(2)}) copy-start(bf16[26,1024,39]{1,2,0:T(8,128)(2,1)} %param.17) | copy-start | bytes 6230020

commit v3 on v2

--- a/solution.py
+++ b/solution.py
@@ -1,3 +1,5 @@
+import functools
+
 import jax
 import jax.numpy as jnp
 from jax import lax
@@ -300,6 +302,169 @@
     )
 
 
+def one_hot(places, count):
+    rows = lax.broadcasted_iota(jnp.int32, (count, places.shape[1]), 0)
+    return (rows == places).astype(F32).astype(BF)
+
+
+def lookup_kernel(
+    fields, edim, ids_ref, table_ref, dense_ref, x0_ref, arr_ref, inv_ref,
+    ids, slots, req, found, rep, pair, wide_rows, x0f, id_send, id_recv, send, recv,
+):
+    section, me = lax.axis_index("section"), lax.axis_index("dp")
+    dot = functools.partial(jnp.dot, preferred_element_type=F32)
+    count = ids.shape[1]
+
+    def peer(j):
+        return lax.rem(me + j, 8)
+
+    def lanes(place):
+        return pl.ds(pl.multiple_of(place * 128, 128), 128)
+
+    barrier = pltpu.get_barrier_semaphore()
+    for j in range(1, 8):
+        pl.semaphore_signal(
+            barrier, inc=1, device_id=(section, peer(j)), device_id_type=pl.DeviceIdType.MESH
+        )
+
+    ids[...] = jnp.zeros_like(ids)
+    ids[:fields] = ids_ref[...]
+    every = ids[...]
+    owner = lax.shift_right_logical(every, 10)
+    hot = jnp.concatenate([(owner == o).astype(F32) for o in range(8)], axis=0).astype(BF)
+    before = (
+        lax.broadcasted_iota(jnp.int32, (count, count), 0)
+        < lax.broadcasted_iota(jnp.int32, (count, count), 1)
+    )
+    ranks = dot(hot, before.astype(F32).astype(BF))
+    rank = jnp.zeros((32, count), F32)
+    for o in range(8):
+        rank = jnp.where(owner == o, ranks[32 * o : 32 * o + 32], rank)
+    slots[...] = owner * 128 + rank.astype(jnp.int32)
+    ids[...] = every & 1023
+    @pl.loop(0, 4)
+    def _(group):
+        eight = pl.ds(pl.multiple_of(8 * group, 8), 8)
+        slot8, local8 = slots[eight], ids[eight]
+        place = lax.broadcasted_iota(jnp.int32, (1, count), 1)
+        column = lax.broadcasted_iota(jnp.int32, (8, count), 0)
+        wanted, source = [], []
+        for k in range(8):
+            slot, local = slot8[k : k + 1], local8[k : k + 1]
+            owners = column == lax.shift_right_logical(slot, 7)
+            parts = [local >> 5, local & 31, place >> 5, place & 31]
+            left = jnp.concatenate(
+                [jnp.where(owners, p.astype(F32), 0.0) for p in parts], axis=0
+            ).astype(BF)
+            right = one_hot(slot & 127, 128)
+            sent = lax.dot_general(
+                left, right, (((1,), (1,)), ((), ())), preferred_element_type=F32
+            )
+            rows = [
+                (sent[n : n + 8] * 32 + sent[n + 8 : n + 16]).astype(jnp.int32) for n in (0, 16)
+            ]
+            for taken, r in zip((wanted, source), rows):
+                taken.append(jnp.concatenate([r[o : o + 1] for o in range(8)], axis=1))
+        req[eight] = jnp.concatenate(wanted, axis=0)
+        inv_ref[eight] = jnp.concatenate(source, axis=0)
+
+    def id_copy(j):
+        return pltpu.make_async_remote_copy(
+            src_ref=req.at[:, lanes(peer(j))],
+            dst_ref=arr_ref.at[:, lanes(me)],
+            send_sem=id_send.at[j],
+            recv_sem=id_recv.at[j],
+            device_id=(section, peer(j)),
+            device_id_type=pl.DeviceIdType.MESH,
+        )
+
+    pl.semaphore_wait(barrier, 7)
+    for j in range(1, 8):
+        id_copy(j).start()
+    arr_ref[:, lanes(me)] = req[:, lanes(me)]
+    for j in range(1, 8):
+        id_copy(j).wait_recv()
+
+    def row_copy(i, j):
+        return pltpu.make_async_remote_copy(
+            src_ref=found.at[i, :, lanes(peer(j))],
+            dst_ref=rep.at[i, :, lanes(me)],
+            send_sem=send.at[i, j],
+            recv_sem=recv.at[i, j],
+            device_id=(section, peer(j)),
+            device_id_type=pl.DeviceIdType.MESH,
+        )
+
+    pair[...] = jnp.zeros_like(pair)
+
+    @pl.loop(0, fields // 2)
+    def _(i):
+        for h in range(2):
+            hot = one_hot(arr_ref[pl.ds(2 * i + h, 1)], count)
+            pair[40 * h : 40 * h + edim] = dot(table_ref[2 * i + h], hot)
+        found[i] = pair[...].astype(BF)
+        for j in range(1, 8):
+            row_copy(i, j).start()
+        rep[i, :, lanes(me)] = found[i, :, lanes(me)]
+
+    @pl.loop(0, fields // 2)
+    def _(i):
+        for j in range(1, 8):
+            row_copy(i, j).wait_recv()
+        wide_rows[2 * i] = dot(rep[i, 0:48], one_hot(slots[pl.ds(2 * i, 1)], count))[0:40]
+        wide_rows[2 * i + 1] = dot(rep[i, 32:80], one_hot(slots[pl.ds(2 * i + 1, 1)], count))[8:48]
+
+    sparse, extra = fields * edim, dense_ref.shape[0]
+    x0f[sparse // 8 * 8 :] = jnp.zeros_like(x0f[sparse // 8 * 8 :])
+    for f in range(fields):
+        x0f[f * edim : f * edim + edim] = wide_rows[f, :edim]
+    x0f[sparse : sparse + extra] = dense_ref[...].astype(F32)
+    x0_ref[...] = x0f[...].astype(BF)
+
+    @pl.loop(0, fields // 2)
+    def _(i):
+        for j in range(1, 8):
+            row_copy(i, j).wait_send()
+
+    for j in range(1, 8):
+        id_copy(j).wait_send()
+
+
+def look_up(ids_t, table_t, dense_t):
+    fields, count = ids_t.shape
+    edim = table_t.shape[1]
+    tall = -(-(fields * edim + dense_t.shape[0]) // 16) * 16
+    vmem = pl.BlockSpec(memory_space=pltpu.VMEM)
+    return pl.pallas_call(
+        functools.partial(lookup_kernel, fields, edim),
+        out_shape=[
+            jax.ShapeDtypeStruct((tall, count), BF),
+            jax.ShapeDtypeStruct((32, count), jnp.int32),
+            jax.ShapeDtypeStruct((32, count), jnp.int32),
+        ],
+        in_specs=[vmem] * 3,
+        out_specs=[vmem] * 3,
+        scratch_shapes=[
+            pltpu.VMEM((32, count), jnp.int32),
+            pltpu.VMEM((32, count), jnp.int32),
+            pltpu.VMEM((32, count), jnp.int32),
+            pltpu.VMEM((fields // 2, 80, count), BF),
+            pltpu.VMEM((fields // 2, 80, count), BF),
+            pltpu.VMEM((80, count), F32),
+            pltpu.VMEM((fields, 40, count), F32),
+            pltpu.VMEM((tall, count), F32),
+            pltpu.SemaphoreType.DMA((8,)),
+            pltpu.SemaphoreType.DMA((8,)),
+            pltpu.SemaphoreType.DMA((fields // 2, 8)),
+            pltpu.SemaphoreType.DMA((fields // 2, 8)),
+        ],
+        compiler_params=pltpu.CompilerParams(
+            collective_id=1, has_side_effects=True, vmem_limit_bytes=48 * 2**20
+        ),
+        name="look_up",
+    )(ids_t, table_t, dense_t)
+
+
 def body(
     ids,
     dense,
@@ -326,37 +491,49 @@
     me = lax.axis_index("section") * groups + lax.axis_index("dp")
 
     idt = ids.T
-    owner = idt // table_rows
-    local = idt % table_rows
-    owner_hot = owner[:, None, :] == jnp.arange(groups, dtype=jnp.int32)[None, :, None]
+    table_t = table.transpose(0, 2, 1)
     lane = jnp.arange(examples, dtype=jnp.int32)
-    before = (lane[:, None] < lane[None, :]).astype(BF)
-    counts = mm(owner_hot.reshape(fields * groups, examples).astype(BF), before, (1, 0))
-    rank = jnp.sum(jnp.where(owner_hot, counts.reshape(fields, groups, examples), 0.0), axis=1)
-    slot = owner * capacity + rank.astype(jnp.int32)
-    slot_hot = (slot[:, None, :] == lane[None, :, None]).astype(BF)
-    halves = jnp.stack([local // 32, local % 32], axis=1).astype(BF)
-    sent = lax.dot_general(
-        halves, slot_hot, (((2,), (2,)), ((0,), (0,))), preferred_element_type=F32
-    )
-    requests = (sent[:, 0] * 32 + sent[:, 1]).astype(jnp.int32)
-    requests = requests.reshape(fields, groups, capacity).transpose(1, 0, 2)
-    arrived = lax.all_to_all(requests, "dp", 0, 0, tiled=True)
-    arrived = arrived.transpose(1, 0, 2).reshape(fields, examples)
-    row_hot = (
-        arrived[:, None, :] == jnp.arange(table_rows, dtype=jnp.int32)[None, :, None]
-    ).astype(BF)
-    table_t = table.transpose(0, 2, 1)
-    found = lax.dot_general(
-        table_t, row_hot, (((2,), (1,)), ((0,), (0,))), preferred_element_type=F32
-    ).astype(BF)
-    found = found.reshape(sparse, groups, capacity).transpose(1, 0, 2)
-    replies = lax.all_to_all(found, "dp", 0, 0, tiled=True)
-    replies = replies.transpose(1, 0, 2).reshape(fields, edim, examples)
-    embedded = lax.dot_general(
-        replies, slot_hot, (((2,), (1,)), ((0,), (0,))), preferred_element_type=F32
-    ).astype(BF)
-    x0 = jnp.concatenate([embedded.reshape(sparse, examples), dense.T], axis=0)
+    here = (sections, groups, capacity, table_rows) == (4, 8, 128, 1024)
+    if here:
+        x0, arrived, source = look_up(idt, table_t, dense.T)
+        x0 = x0[:width]
+        arrived, source = arrived[:fields], source[:fields]
+    else:
+        owner = idt // table_rows
+        local = idt % table_rows
+        owner_hot = owner[:, None, :] == jnp.arange(groups, dtype=jnp.int32)[None, :, None]
+        before = (lane[:, None] < lane[None, :]).astype(BF)
+        counts = mm(owner_hot.reshape(fields * groups, examples).astype(BF), before, (1, 0))
+        rank = jnp.sum(jnp.where(owner_hot, counts.reshape(fields, groups, examples), 0.0), axis=1)
+        slot = owner * capacity + rank.astype(jnp.int32)
+        slot_hot = (slot[:, None, :] == lane[None, :, None]).astype(BF)
+        values = [local // 32, local % 32] + [
+            jnp.broadcast_to(part, idt.shape) for part in (lane // 32, lane % 32)
+        ]
+        sent = lax.dot_general(
+            jnp.stack(values, axis=1).astype(BF),
+            slot_hot,
+            (((2,), (2,)), ((0,), (0,))),
+            preferred_element_type=F32,
+        )
+        requests = (sent[:, 0] * 32 + sent[:, 1]).astype(jnp.int32)
+        source = (sent[:, 2] * 32 + sent[:, 3]).astype(jnp.int32)
+        requests = requests.reshape(fields, groups, capacity).transpose(1, 0, 2)
+        arrived = lax.all_to_all(requests, "dp", 0, 0, tiled=True)
+        arrived = arrived.transpose(1, 0, 2).reshape(fields, examples)
+        row_hot = (
+            arrived[:, None, :] == jnp.arange(table_rows, dtype=jnp.int32)[None, :, None]
+        ).astype(BF)
+        found = lax.dot_general(
+            table_t, row_hot, (((2,), (1,)), ((0,), (0,))), preferred_element_type=F32
+        ).astype(BF)
+        found = found.reshape(sparse, groups, capacity).transpose(1, 0, 2)
+        replies = lax.all_to_all(found, "dp", 0, 0, tiled=True)
+        replies = replies.transpose(1, 0, 2).reshape(fields, edim, examples)
+        embedded = lax.dot_general(
+            replies, slot_hot, (((2,), (1,)), ((0,), (0,))), preferred_element_type=F32
+        ).astype(BF)
+        x0 = jnp.concatenate([embedded.reshape(sparse, examples), dense.T], axis=0)
 
     x0w = x0.astype(F32)
     xs, us = [x0], []
@@ -403,15 +580,18 @@
 
     packed = lax.dot_general(
         dx0[:sparse].astype(BF).reshape(fields, edim, examples),
-        slot_hot,
-        (((2,), (2,)), ((0,), (0,))),
+        (source[:, None, :] == lane[None, :, None]).astype(BF),
+        (((2,), (1,)), ((0,), (0,))),
         preferred_element_type=F32,
     ).astype(BF)
     packed = packed.reshape(sparse, groups, capacity).transpose(1, 0, 2)
     delivered = lax.all_to_all(packed, "dp", 0, 0, tiled=True)
     delivered = delivered.transpose(1, 0, 2).reshape(fields, edim, examples)
+    row_hot = (
+        arrived[:, :, None] == jnp.arange(table_rows, dtype=jnp.int32)[None, None, :]
+    ).astype(BF)
     table_g = lax.dot_general(
-        delivered, row_hot, (((2,), (2,)), ((0,), (0,))), preferred_element_type=F32
+        delivered, row_hot, (((2,), (1,)), ((0,), (0,))), preferred_element_type=F32
     )
     small = jnp.concatenate(
         cross_b + [head_grad, jnp.sum(s).reshape(1), loss.reshape(1)] + tower_biases
@@ -419,7 +599,7 @@
     both = ("section", "dp")
     share = hidden // device_count
     main = hidden
-    if (sections, groups) == (4, 8):
+    if here:
         edges = [jnp.concatenate([g[main:].reshape(-1), g[:main, main:].reshape(-1)]) for g in cross_g]
         edges.append(tower_in_g[:, main:].reshape(-1))
         flat = jnp.concatenate([small] + edges)

time: 490 us -> 402 us (0.82)
  matrix products: 191 us -> 116 us
  Pallas kernels: 113 us -> 174 us
  waiting for transfers between devices: 50.2 us -> 7.24 us
  blocking collectives: 12.6 us -> 0 us
  local copies, waits for them, and re-layouts: 68.5 us -> 59.5 us
  starting transfers between devices: 10.2 us -> 4.56 us
    dot_general x4 -> x1, matrix products: 88.1 us -> 23.5 us  [body(): lax.dot_general(delivered, row_hot, (((2,), (1,)), ((0,), (0,))), preferr...]
    pallas_call x0 -> x1, Pallas kernels: none -> 61.1 us  [look_up(): pl.pallas_call(functools.partial(lookup_kernel, fields, edim), out_shape=...]
    all_to_all x1 -> x0, waiting for transfers between devices: 45 us -> none  [body(): replies = lax.all_to_all(found, 'dp', 0, 0, tiled=True)]
    all_to_all x1 -> x0, blocking collectives: 12.6 us -> none  [body(): arrived = lax.all_to_all(requests, 'dp', 0, 0, tiled=True)]
    reshape x4 -> x0, local copies, waits for them, and re-layouts: 12 us -> none  [the longest x2 4.66 us: body(): found = found.reshape(sparse, groups, capacity).transpose(1, 0, 2)]
    dot_general x16 -> x15, matrix products: 79 us -> 69.1 us  [mm(): lax.dot_general(left, right, ((contract[:1], contract[1:]), ((), ())), pr...]
  transfers between devices with their start and end apart: 2 -> 1, of which waited for: 2 -> 1; matrix products, arithmetic and copies ran while one was open for 8% -> 9% of each run, Pallas kernels for 0% -> 0%
where the time goes in v3:
time: 402 us; the launch traced here: 396 us
  Pallas kernels  174 us (43%)
  matrix products  116 us (29%)
  local copies, waits for them, and re-layouts  59.5 us (15%)
  other arithmetic  31.5 us (8%)
  waiting for transfers between devices  7.24 us (2%)
  starting transfers between devices  4.56 us (1%)
  between operations  4.2 us (1%)
    pallas_call x1, Pallas kernels, reduce_all(): pl.pallas_call(lambda *refs: reduce_kernel(units, gathered, *refs), out_s...  113 us
    dot_general x15, matrix products, mm(): lax.dot_general(left, right, ((contract[:1], contract[1:]), ((), ())), pr...  69.1 us
    pallas_call x1, Pallas kernels, look_up(): pl.pallas_call(functools.partial(lookup_kernel, fields, edim), out_shape=...  61.1 us
    dot_general x1, matrix products, body(): lax.dot_general(delivered, row_hot, (((2,), (1,)), ((0,), (0,))), preferr...  23.5 us
    dot_general x1, matrix products, body(): lax.dot_general(dx0[:sparse].astype(BF).reshape(fields, edim, examples),...  22.9 us
    another operation x4, other arithmetic, body(): cross_out = jnp.stack(crosses)  19.4 us
    unnamed x55, local copies, waits for them, and re-layouts  9.24 us
  transfers between devices with their start and end apart: 1, of which 1 were waited for; matrix products, arithmetic and copies ran while one was open for 9% of the time, Pallas kernels for 0%

profile of v3, /device:TPU:1, one launch (start us, length us, event | category | flops | bytes accessed | tf_op | source)
XLA Modules:
  0.0 396.4 jit_solution(1012371795928106126)
XLA Ops:
  3.8 1.6 copy-done.2
  7.1 61.1 %look_up.1 = (bf16[1040,1024]{1,0:T(8,128)(2,1)S(1)}, s32[32,1024]{1,0:T(8,128)S(1)}, s32[32,1024]{1,0:T(8,128)S(1)}) custom-call(s32[26,1024]{1,0:T(8,128)S(1)} %bitcast.157, bf16[26,39,1024]{2,1,0:T(8,128)(2,1)S(1)} %bitcast.156, bf16[13,1024]{1,0:T(8,128)(2,1)S(1)} %bitcast.158), custom_call_target="tpu_custom_call" | custom-call | tf_op jit(solution)/shard_map/look_up/pallas_call | solution.py:438
  68.2 4.7 %fusion.68 = f32[1024,1024]{1,0:T(8,128)} fusion(bf16[1027,1024]{1,0:T(8,128)(2,1)S(1)} %copy-done, bf16[1040,1024]{1,0:T(8,128)(2,1)S(1)} %get-tuple-element.31), kind=kOutput, calls=%fused_computation.131 | convolution fusion | flops 2153775104 | bytes 8421376 | tf_op jit(solution)/shard_map/dot_general | solution.py:15
  73.5 3.3 fusion.13
  76.8 3.5 fusion.15
  80.4 5.1 %fusion.11 = (f32[1024]{0:T(1024)S(1)}, bf16[1027,1024]{1,0:T(8,128)(2,1)}, f32[1027,1024]{1,0:T(8,128)S(1)}) fusion(f32[1027]{0:T(1024)S(1)} %slice.165, bf16[1027,1024]{1,0:T(8,128)(2,1)S(1)} %get-tuple-element.73, bf16[1040,1024]{1,0:T(8,128)(2,1)S(1)} %get-tuple-element.31, f32[1027]{0:T(1024)S(1)} %get-tuple-element.41, ...), kind=kOutput, calls=%fused_computation.43 | convolution fusion | flops 2169548800 | bytes 15048704 | tf_op jit(solution)/shard_map/dot_general | solution.py:15
  85.5 6.2 %multiply_reduce_fusion.1 = (f32[1024]{0:T(1024)S(1)}, f32[1024,1024]{1,0:T(8,128)S(1)}) fusion(f32[1024]{0:T(1024)S(1)} %slice.166, f32[1024]{0:T(1024)S(1)} %copy-done.17, bf16[1024,1024]{1,0:T(8,128)(2,1)S(1)} %copy-done.19, f32[1024,1024]{1,0:T(8,128)} %fusion.68, f32[1024]{0:T(1024)S(1)} %copy-done.21), kind=kOutput, calls=%fused_computation.87 | convolution fusion | flops 2169502720 | bytes 10502144 | tf_op jit(solution)/shard_map/dot_general | solution.py:15
  91.7 1.2 fusion.78
  92.9 3.2 fusion.40
  96.1 4.3 %convert_reduce_fusion.3 = (f32[1024]{0:T(1024)S(1)}, bf16[1024,1024]{0,1:T(8,128)(2,1)S(1)}, f32[1024]{0:T(1024)S(1)}) fusion(f32[1024,1024]{1,0:T(8,128)S(1)} %get-tuple-element.77, f32[1024]{0:T(1024)S(1)} %copy-done.17, f32[1024]{0:T(1024)S(1)} %slice.166, f32[1024]{0:T(1024)S(1)} %get-tuple-element.48), kind=kLoop, calls=%fused_computation.84 | loop fusion | flops 27260928 | bytes 6311936 | tf_op jit(solution)/shard_map/reduce_sum | solution.py:566
  100.5 6.5 %convert_reduce_fusion.4 = (f32[1024]{0:T(1024)S(1)}, bf16[1024,1024]{0,1:T(8,128)(2,1)}) fusion(f32[1024,1024]{1,0:T(8,128)S(1)} %copy-done.23, f32[1024]{0:T(1024)S(1)} %copy-done.21, bf16[1024,1024]{0,1:T(8,128)(2,1)S(1)} %get-tuple-element.46, bf16[1024,1024]{1,0:T(8,128)(2,1)S(1)} %copy-done.20), kind=kOutput, calls=%fused_computation.85 | convolution fusion | flops 2170551296 | bytes 10493952 | tf_op jit(solution)/shard_map/dot_general | solution.py:15
  107.0 6.3 %convert_reduce_fusion = (f32[1027]{0:T(1024)S(1)}, f32[1027]{0:T(1024)S(1)}, f32[1027]{0:T(1024)S(1)}, f32[1027]{0:T(1024)S(1)}, bf16[1027,1024]{1,0:T(8,128)(2,1)S(1)}) fusion(bf16[1040,1024]{1,0:T(8,128)(2,1)S(1)} %get-tuple-element.31, f32[1027]{0:T(1024)S(1)} %slice.165, f32[1024]{0:T(1024)S(1)} %get-tuple-element.48, ...), kind=kOutput, calls=%fused_computation.53 | convolution fusion | flops 2188475392 | bytes 15077424 | tf_op jit(solution)/shard_map/dot_general | solution.py:15
  113.3 5.4 %fusion.10 = f32[1027,1024]{1,0:T(8,128)S(1)} fusion(bf16[1024,1024]{0,1:T(8,128)(2,1)} %get-tuple-element.80, bf16[1027,1024]{1,0:T(8,128)(2,1)S(1)} %copy-done, f32[1027,1024]{1,0:T(8,128)S(1)} %get-tuple-element.75, f32[1027,1024]{1,0:T(8,128)S(1)} %get-tuple-element.74, bf16[1027,1024]{1,0:T(8,128)(2,1)S(1)} %fusion.40, ...), kind=kOutput, calls=%fused_computation.40 | convolution fusion | flops 2165343232 | bytes 25241612 | tf_op jit(solution)/shard_map/dot_general | solution.py:15
  118.7 4.7 %fusion.7 = f32[1027,1024]{1,0:T(8,128)S(1)} fusion(f32[1027,1024]{1,0:T(8,128)S(1)} %fusion.10, bf16[1027,1024]{1,0:T(8,128)(2,1)S(1)} %get-tuple-element.78, bf16[3,1027,1027]{2,1,0:T(8,128)(2,1)} %param.18, bf16[1040,1024]{1,0:T(8,128)(2,1)S(1)} %get-tuple-element.31), kind=kOutput, calls=%fused_computation.36 | convolution fusion | flops 2167446528 | bytes 17152000 | tf_op jit(solution)/shard_map/dot_general | solution.py:15
  123.4 2.0 copy-done.15
  125.7 2.2 reshape.164
  127.9 22.9 %fusion.55 = bf16[26,39,1024]{2,1,0:T(8,128)(2,1)S(1)} fusion(bf16[26,39,1024]{2,1,0:T(8,128)(2,1)} %reshape.164, s32[26,1024]{1,0:T(8,128)S(1)} %bitcast.160), kind=kOutput, calls=%fused_computation.109 | convolution fusion | flops 2154813440 | bytes 4259840 | tf_op jit(solution)/shard_map/dot_general | solution.py:581
  150.9 2.2 reshape.165
  153.1 3.4 copy.33
  156.4 4.6 %all-to-all-start = ((bf16[8,1014,128]{2,1,0:T(8,128)(2,1)}), bf16[8,1014,128]{2,1,0:T(8,128)(2,1)}, u32[]{:S(2)}, u32[]{:S(2)}) async-start(bf16[8,1014,128]{2,1,0:T(8,128)(2,1)} %bitcast.166), calls=%async_computation | async-start | bytes 4161536 | tf_op jit(solution)/shard_map/all_to_all | solution.py:588
  161.0 5.2 %fusion.59 = f32[1027,1027]{1,0:T(8,128)S(1)} fusion(bf16[1027,1024]{1,0:T(8,128)(2,1)} %copy-done.22, bf16[1027,1024]{1,0:T(8,128)(2,1)} %copy-done.8, bf16[1040,1024]{1,0:T(8,128)(2,1)S(1)} %copy-done.6), kind=kOutput, calls=%fused_computation.112 | convolution fusion | flops 2164291584 | bytes 10539044 | tf_op jit(solution)/shard_map/dot_general | solution.py:15
  166.3 1.7 slice.298
  169.3 2.5 fusion.65
  171.8 1.7 slice.296
  174.1 3.0 fusion.57
  177.1 1.7 slice.299
  179.2 3.1 fusion.71
  183.1 1.7 slice.297
  185.2 2.8 copy.27
  189.3 1.4 concatenate.26
  191.4 1.5 slice_bitcast_fusion.2
  192.9 6.7 %convolution_convert_fusion = bf16[1024,1024]{1,0:T(8,128)(2,1)} fusion(bf16[1024,1024]{0,1:T(8,128)(2,1)} %copy-done.13, f32[1024,1024]{1,0:T(8,128)} %fusion.68, f32[1024]{0:T(1024)S(1)} %copy-done.21), kind=kOutput, calls=%fused_computation.110 | convolution fusion | flops 2159017984 | bytes 8392704 | tf_op jit(solution)/shard_map/dot_general | solution.py:15
  199.6 7.2 %all-to-all-done = bf16[8,1014,128]{2,1,0:T(8,128)(2,1)} async-done(((bf16[8,1014,128]{2,1,0:T(8,128)(2,1)}), bf16[8,1014,128]{2,1,0:T(8,128)(2,1)}, u32[]{:S(2)}, u32[]{:S(2)}) %all-to-all-start) | async-done | bytes 2076704 | tf_op jit(solution)/shard_map/all_to_all | solution.py:588
  206.9 1.9 copy.29
  208.7 2.2 reshape.166
  210.9 23.5 %fusion.54 = bf16[26,39,1024]{2,1,0:T(8,128)(2,1)} fusion(bf16[26,39,1024]{2,1,0:T(8,128)(2,1)} %reshape.166, s32[26,1024]{1,0:T(8,128)S(1)} %bitcast.159), kind=kOutput, calls=%fused_computation.108 | convolution fusion | flops 2154813440 | bytes 4259840 | tf_op jit(solution)/shard_map/dot_general | solution.py:593
  234.4 2.7 reshape.167
  237.1 1.5 pad.7
  238.6 112.8 %reduce_all.1 = (bf16[3,2,2,4,2,32,1024]{6,5,4,3,2,1,0:T(8,128)(2,1)}, f32[2,32,1024]{2,1,0:T(8,128)}, bf16[2,2,256,1024]{3,2,1,0:T(8,128)(2,1)}, f32[2,16,1024]{2,1,0:T(8,128)}) custom-call(bf16[2,2,4,2,32,1024]{5,4,3,2,1,0:T(8,128)(2,1)} %bitcast.162, bf16[2,2,4,2,32,1024]{5,4,3,2,1,0:T(8,128)(2,1)} %bitcast.161, ...), custom_call_target="tpu_custom_call" | custom-call | tf_op jit(solution)/shard_map/reduce_all/pallas_call | solution.py:256
  355.9 1.7 slice_bitcast_fusion
  359.0 4.0 %slice_convert_fusion.5 = f32[1014,1024]{1,0:T(8,128)} fusion(bf16[1024,1024]{1,0:T(8,128)(2,1)} %bitcast.169), kind=kLoop, calls=%fused_computation.106 | loop fusion | flops 1038336 | bytes 6230016 | tf_op jit(solution)/shard_map/transpose | solution.py:641
  363.1 5.4 %reshape.191 = f32[26,39,1024]{2,1,0:T(8,128)} reshape(f32[1014,1024]{1,0:T(8,128)} %slice_convert_fusion.5) | data formatting | bytes 8306688 | tf_op jit(solution)/shard_map/transpose | solution.py:641
  368.4 3.7 fusion.80
  374.1 1.3 bitcast_convert_fusion
  375.4 2.7 maximum_bitcast_fusion
  378.1 2.6 maximum_bitcast_fusion.2
  380.6 2.6 maximum_bitcast_fusion.1
  383.2 11.5 %pad_maximum_fusion = f32[3,1027,1027]{2,1,0:T(8,128)} fusion(f32[1,1027,1027]{2,1,0:T(8,128)} %maximum_bitcast_fusion.2, f32[1,1027,1027]{2,1,0:T(8,128)} %maximum_bitcast_fusion.1, f32[1,1027,1027]{2,1,0:T(8,128)} %maximum_bitcast_fusion), kind=kLoop, calls=%fused_computation.6 | loop fusion | flops 6328374 | bytes 25313496 | tf_op jit(solution)/shard_map/stack | solution.py:629
  (93 shorter events, 17.9 us)
Async XLA Ops:
  0.6 67.6 %copy-start = (bf16[1027,1024]{1,0:T(8,128)(2,1)S(1)}, bf16[1027,1024]{1,0:T(8,128)(2,1)}, u32[]{:S(2)}) copy-start(bf16[1027,1024]{1,0:T(8,128)(2,1)} %param.20) | copy-start | bytes 6309892
  3.8 1.6 copy-start.2
  5.4 0.9 copy-start.3
  6.3 0.8 copy-start.4
  68.2 50.5 %copy-start.5 = (bf16[1040,1024]{1,0:T(8,128)(2,1)}, bf16[1040,1024]{1,0:T(8,128)(2,1)S(1)}, u32[]{:S(2)}) copy-start(bf16[1040,1024]{1,0:T(8,128)(2,1)S(1)} %get-tuple-element.31) | copy-start | bytes 6389764
  68.2 5.3 %copy-start.18 = (bf16[3,1027,1027]{2,1,0:T(8,128)(2,1)S(1)}, bf16[3,1027,1027]{2,1,0:T(8,128)(2,1)}, u32[]{:S(2)}) copy-start(bf16[3,1027,1027]{2,1,0:T(8,128)(2,1)} %param.18) | copy-start | bytes 18985126
  76.8 3.5 copy-start.22
  80.3 5.2 %copy-start.24 = (bf16[1027,1024]{1,0:T(8,128)(2,1)}, bf16[1027,1024]{1,0:T(8,128)(2,1)S(1)}, u32[]{:S(2)}) copy-start(bf16[1027,1024]{1,0:T(8,128)(2,1)S(1)} %get-tuple-element.73) | copy-start | bytes 6309892
  80.3 5.1 %copy-start.17 = (f32[1024]{0:T(1024)S(1)}, f32[1024]{0:T(1024)}, u32[]{:S(2)}) copy-start(f32[1024]{0:T(1024)} %param.23) | copy-start | bytes 12292
  80.3 5.1 %copy-start.19 = (bf16[1024,1024]{1,0:T(8,128)(2,1)S(1)}, bf16[1024,1024]{1,0:T(8,128)(2,1)}, u32[]{:S(2)}) copy-start(bf16[1024,1024]{1,0:T(8,128)(2,1)} %param.22) | copy-start | bytes 6291460
  80.4 5.1 %copy-start.21 = (f32[1024]{0:T(1024)S(1)}, f32[1024]{0:T(1024)}, u32[]{:S(2)}) copy-start(f32[1024]{0:T(1024)} %param.21) | copy-start | bytes 12292
  85.5 6.2 %copy-start.16 = (s32[1024]{0:T(1024)S(1)}, s32[1024]{0:T(1024)}, u32[]{:S(2)}) copy-start(s32[1024]{0:T(1024)} %param.16) | copy-start | bytes 12292
  96.1 17.2 %copy-start.8 = (bf16[1027,1024]{1,0:T(8,128)(2,1)}, bf16[1027,1024]{1,0:T(8,128)(2,1)S(1)}, u32[]{:S(2)}) copy-start(bf16[1027,1024]{1,0:T(8,128)(2,1)S(1)} %fusion.40) | copy-start | bytes 6309892
  96.1 4.3 %copy-start.20 = (bf16[1024,1024]{1,0:T(8,128)(2,1)S(1)}, bf16[1024,1024]{1,0:T(8,128)(2,1)}, u32[]{:S(2)}) copy-start(bf16[1024,1024]{1,0:T(8,128)(2,1)} %param.22) | copy-start | bytes 6291460
  96.1 4.3 %copy-start.23 = (f32[1024,1024]{1,0:T(8,128)S(1)}, f32[1024,1024]{1,0:T(8,128)}, u32[]{:S(2)}) copy-start(f32[1024,1024]{1,0:T(8,128)} %fusion.68) | copy-start | bytes 12582916
  100.4 6.5 %copy-start.13 = (bf16[1024,1024]{0,1:T(8,128)(2,1)}, bf16[1024,1024]{0,1:T(8,128)(2,1)S(1)}, u32[]{:S(2)}) copy-start(bf16[1024,1024]{0,1:T(8,128)(2,1)S(1)} %get-tuple-element.46) | copy-start | bytes 6291460
  100.4 6.5 %copy-start.26 = (bf16[1027,1024]{1,0:T(8,128)(2,1)S(1)}, bf16[1027,1024]{1,0:T(8,128)(2,1)}, u32[]{:S(2)}) copy-start(bf16[1027,1024]{1,0:T(8,128)(2,1)} %get-tuple-element.51) | copy-start | bytes 6309892
  113.3 5.4 %copy-start.9 = (bf16[1027,1024]{1,0:T(8,128)(2,1)}, bf16[1027,1024]{1,0:T(8,128)(2,1)S(1)}, u32[]{:S(2)}) copy-start(bf16[1027,1024]{1,0:T(8,128)(2,1)S(1)} %get-tuple-element.78) | copy-start | bytes 6309892
  123.4 2.0 copy-start.15
  153.1 7.9 %copy-start.6 = (bf16[1040,1024]{1,0:T(8,128)(2,1)S(1)}, bf16[1040,1024]{1,0:T(8,128)(2,1)}, u32[]{:S(2)}) copy-start(bf16[1040,1024]{1,0:T(8,128)(2,1)} %copy-done.5) | copy-start | bytes 6389764
  156.4 50.4 %all-to-all-start = ((bf16[8,1014,128]{2,1,0:T(8,128)(2,1)}), bf16[8,1014,128]{2,1,0:T(8,128)(2,1)}, u32[]{:S(2)}, u32[]{:S(2)}) async-start(bf16[8,1014,128]{2,1,0:T(8,128)(2,1)} %bitcast.166), calls=%async_computation | async-start | bytes 4161536 | tf_op jit(solution)/shard_map/all_to_all | solution.py:588
  166.2 3.0 copy-start.14
  166.2 3.1 copy-start.11
  171.8 2.3 copy-start.10
  177.0 2.1 copy-start.25
  182.3 2.5 slice-start
  182.3 2.9 copy-start.7
  185.2 3.8 copy-start.12
  383.2 11.5 %copy-start.1 = (bf16[1027,1024]{1,0:T(8,128)(2,1)S(1)}, bf16[1027,1024]{1,0:T(8,128)(2,1)}, u32[]{:S(2)}) copy-start(bf16[1027,1024]{1,0:T(8,128)(2,1)} %param.20) | copy-start | bytes 6309892

commit v4 on v3

--- a/solution.py
+++ b/solution.py
@@ -25,13 +25,15 @@
 VIEW = (2, 2, 4, 2)
 
 
-def reduce_kernel(
-    units, gathered, *refs
-):
+def reduce_kernel(units, gathered, *refs):
     grads = refs[:units]
-    table_ref, small_ref = refs[units : units + 2]
-    whole, pieces, table_out, small_out = refs[units + 2 : units + 6]
-    (rc, sa1, ra1, sb1, rb1, sa2, ra2, sb2, rb2, sz, rz, rtc, st, rt, sm, rm, rmz, send, recv) = refs[units + 6 :]
+    rows_ref, inv_ref, arr_ref, small_ref = refs[units : units + 4]
+    whole, pieces, table_out, small_out = refs[units + 4 : units + 8]
+    (
+        rc, sa1, ra1, sb1, rb1, sa2, ra2, sb2, rb2, sz, rz, packed, back, summed, stc, rtc, st, rt, sm, rm, rmz,
+        send, recv, row_send, row_recv, table_send, table_recv,
+    ) = refs[units + 8 :]
+    pairs, count = rows_ref.shape[0], rows_ref.shape[2]
     section, dp = lax.axis_index("section"), lax.axis_index("dp")
     y, c = section // 2, section % 2
     z, x = dp // 2, dp % 2
@@ -44,7 +46,10 @@
     def z_peer(j):
         return (section, lax.rem(z + j, 4) * 2 + x)
 
-    peers = [core_peer, y_peer, x_peer] + [z_peer(j) for j in (1, 2, 3)]
+    def dp_peer(j):
+        return (section, lax.rem(dp + j, 8))
+
+    peers = [core_peer, y_peer] + [dp_peer(j) for j in range(1, 8)]
     barrier = pltpu.get_barrier_semaphore()
     for peer in peers:
         pl.semaphore_signal(barrier, inc=1, device_id=peer, device_id_type=pl.DeviceIdType.MESH)
@@ -52,12 +57,12 @@
 
     flying = []
 
-    def start(src, dst, m, k, peer):
+    def start(src, dst, m, k, peer, sems=(send, recv)):
         copy = pltpu.make_async_remote_copy(
             src_ref=src,
             dst_ref=dst,
-            send_sem=send.at[m, k],
-            recv_sem=recv.at[m, k],
+            send_sem=sems[0].at[m, k],
+            recv_sem=sems[1].at[m, k],
             device_id=peer,
             device_id_type=pl.DeviceIdType.MESH,
         )
@@ -162,42 +167,94 @@
     def step8(m):
         copies[m, 15].wait_recv()
 
-    t = units
-
-    def table0():
-        copies[t, 0] = start(table_ref.at[:, 1 - c], rtc, t, 0, core_peer)
-
-    def table1():
-        copies[t, 0].wait_recv()
-
-        @pl.loop(0, 8)
+    def lanes(place, size):
+        return pl.ds(pl.multiple_of(place * size, size), size)
+
+    def row_copy(i, j):
+        return pltpu.make_async_remote_copy(
+            src_ref=packed.at[i, :, lanes(lax.rem(dp + j, 8), 128)],
+            dst_ref=back.at[i, :, lanes(dp, 128)],
+            send_sem=row_send.at[i, j],
+            recv_sem=row_recv.at[i, j],
+            device_id=dp_peer(j),
+            device_id_type=pl.DeviceIdType.MESH,
+        )
+
+    def pack():
+        @pl.loop(0, pairs)
         def _(i):
-            rows = pl.ds(pl.multiple_of(i * 32, 32), 32)
-            st[rows] = (wide(table_ref[1 - y, c, rows]) + wide(rtc[1 - y, rows])).astype(BF)
-
-        copies[t, 1] = start(st, rt, t, 1, y_peer)
-
-    def table2():
-        copies[t, 1].wait_recv()
-
-        @pl.loop(0, 8)
+            first = jnp.dot(
+                rows_ref[i, 0:48],
+                one_hot(inv_ref[pl.ds(2 * i, 1)], count),
+                preferred_element_type=F32,
+            )
+            second = jnp.dot(
+                rows_ref[i, 32:80],
+                one_hot(inv_ref[pl.ds(2 * i + 1, 1)], count),
+                preferred_element_type=F32,
+            )
+            packed[i] = jnp.concatenate([first[0:40], second[8:48]], axis=0).astype(BF)
+            for j in range(1, 8):
+                row_copy(i, j).start()
+            back[i, :, lanes(dp, 128)] = packed[i, :, lanes(dp, 128)]
+
+    cuts = [pairs * q // 4 for q in range(5)]
+
+    def scatter(q):
+        @pl.loop(cuts[q], cuts[q + 1])
         def _(i):
-            rows = pl.ds(pl.multiple_of(i * 32, 32), 32)
-            total = wide(table_ref[y, c, rows]) + wide(rtc[y, rows]) + wide(rt[rows])
-            table_out[y, c, rows] = total.astype(BF)
-
-        ours = table_out.at[y, c]
-        copies[t, 2] = start(ours, ours, t, 2, y_peer)
-
-    def table3():
-        copies[t, 2].wait_recv()
-        ours = table_out.at[:, c]
-        copies[t, 3] = start(ours, ours, t, 3, core_peer)
-
-    def table4():
-        copies[t, 3].wait_recv()
-
-    s = units + 1
+            for j in range(1, 8):
+                row_copy(i, j).wait_recv()
+            for h, (low, at) in enumerate(((0, 0), (32, 8))):
+                total = lax.dot_general(
+                    back[i, low : low + 48],
+                    one_hot(arr_ref[pl.ds(2 * i + h, 1)], count),
+                    (((1,), (1,)), ((), ())),
+                    preferred_element_type=F32,
+                )
+                summed[i, 40 * h : 40 * h + 40] = total[at : at + 40]
+            stc[i] = summed[i, :, lanes(1 - c, half)].astype(BF)
+
+        part = pl.ds(cuts[q], cuts[q + 1] - cuts[q])
+        copies["t", q, 0] = start(stc.at[part], rtc.at[part], q, 0, core_peer, (table_send, table_recv))
+
+    quarter = half // 2
+
+    def quarter_of(yy):
+        return lanes(2 * c + yy, quarter)
+
+    def table1(q):
+        copies["t", q, 0].wait_recv()
+
+        @pl.loop(cuts[q], cuts[q + 1])
+        def _(i):
+            st[i] = (summed[i, :, quarter_of(1 - y)] + wide(rtc[i, :, lanes(1 - y, quarter)])).astype(BF)
+
+        part = pl.ds(cuts[q], cuts[q + 1] - cuts[q])
+        copies["t", q, 1] = start(st.at[part], rt.at[part], q, 1, y_peer, (table_send, table_recv))
+
+    def table2(q):
+        copies["t", q, 1].wait_recv()
+
+        @pl.loop(cuts[q], cuts[q + 1])
+        def _(i):
+            total = summed[i, :, quarter_of(y)] + wide(rtc[i, :, lanes(y, quarter)]) + wide(rt[i])
+            table_out[i, :, quarter_of(y)] = total.astype(BF)
+
+        part = pl.ds(cuts[q], cuts[q + 1] - cuts[q])
+        ours = table_out.at[part, :, quarter_of(y)]
+        copies["t", q, 2] = start(ours, ours, q, 2, y_peer, (table_send, table_recv))
+
+    def table3(q):
+        copies["t", q, 2].wait_recv()
+        part = pl.ds(cuts[q], cuts[q + 1] - cuts[q])
+        ours = table_out.at[part, :, lanes(c, half)]
+        copies["t", q, 3] = start(ours, ours, q, 3, core_peer, (table_send, table_recv))
+
+    def table4(q):
+        copies["t", q, 3].wait_recv()
+
+    s = units
 
     def small0():
         copies[s, 0] = start(small_ref.at[1 - c], rm.at[0], s, 0, core_peer)
@@ -235,33 +292,44 @@
     small0()
     for m in range(units):
         step0(m)
-    table0()
+    pack()
     steps = [step1, step2, step3, step4, step5, step6, step7, step8]
-    extras = [small1, small2, table1, small3, table2, small4, table3, small5, table4]
+    smalls = [small1, small2, small3, small4, small5]
+    tables = [scatter, table1, table2, table3, table4]
     for now in range(units + len(steps)):
         for k, step in enumerate(steps):
             m = now - k
             if 0 <= m < units and (k < 4 or m < gathered):
                 step(m)
-        if now < len(extras):
-            extras[now]()
+        if now < len(smalls):
+            smalls[now]()
+        for k in reversed(range(len(tables))):
+            q = now - 1 - k
+            if 0 <= q < 4:
+                tables[k](q)
     for copy in flying:
         copy.wait_send()
 
-
-def reduce_all(grads, gathered, table_g, small):
+    @pl.loop(0, pairs)
+    def _(i):
+        for j in range(1, 8):
+            row_copy(i, j).wait_send()
+
+
+def reduce_all(grads, gathered, rows, source, arrived, small):
     units = len(grads)
+    pairs, _, count = rows.shape
     piece = (32, 1024)
     vmem = pl.BlockSpec(memory_space=pltpu.VMEM)
-    outs = pl.pallas_call(
+    whole, pieces, table_sum, small_sum = pl.pallas_call(
         lambda *refs: reduce_kernel(units, gathered, *refs),
         out_shape=[
             jax.ShapeDtypeStruct((gathered,) + VIEW + piece, BF),
             jax.ShapeDtypeStruct((units - gathered,) + piece, F32),
-            jax.ShapeDtypeStruct((2, 2, 256, 1024), BF),
+            jax.ShapeDtypeStruct((pairs, 80, count), BF),
             jax.ShapeDtypeStruct((2, 16, 1024), F32),
         ],
-        in_specs=[vmem] * (units + 2),
+        in_specs=[vmem] * (units + 4),
         out_specs=[vmem] * 4,
         scratch_shapes=[
             pltpu.VMEM((units, 2, 4, 2) + piece, BF),
@@ -275,31 +343,35 @@
             pltpu.VMEM((units, 4, 32, 512), BF),
             pltpu.VMEM((units, 3) + piece, BF),
             pltpu.VMEM((units, 3) + piece, BF),
-            pltpu.VMEM((2, 256, 1024), BF),
-            pltpu.VMEM((256, 1024), BF),
-            pltpu.VMEM((256, 1024), BF),
+            pltpu.VMEM((pairs, 80, count), BF),
+            pltpu.VMEM((pairs, 80, count), BF),
+            pltpu.VMEM((pairs, 80, count), F32),
+            pltpu.VMEM((pairs, 80, count // 2), BF),
+            pltpu.VMEM((pairs, 80, count // 2), BF),
+            pltpu.VMEM((pairs, 80, count // 4), BF),
+            pltpu.VMEM((pairs, 80, count // 4), BF),
             pltpu.VMEM((3, 16, 1024), F32),
             pltpu.VMEM((3, 16, 1024), F32),
             pltpu.VMEM((3, 16, 1024), F32),
-            pltpu.SemaphoreType.DMA((units + 2, 16)),
-            pltpu.SemaphoreType.DMA((units + 2, 16)),
+            pltpu.SemaphoreType.DMA((units + 1, 16)),
+            pltpu.SemaphoreType.DMA((units + 1, 16)),
+            pltpu.SemaphoreType.DMA((pairs, 8)),
+            pltpu.SemaphoreType.DMA((pairs, 8)),
+            pltpu.SemaphoreType.DMA((4, 4)),
+            pltpu.SemaphoreType.DMA((4, 4)),
         ],
         compiler_params=pltpu.CompilerParams(
-            collective_id=0, has_side_effects=True, vmem_limit_bytes=56 * 2**20
+            collective_id=0, has_side_effects=True, vmem_limit_bytes=60 * 2**20
         ),
         name="reduce_all",
     )(
         *[g.reshape(VIEW + piece) for g in grads],
-        table_g.reshape(2, 2, 256, 1024),
+        rows,
+        source,
+        arrived,
         small.reshape(2, 16, 1024),
     )
-    whole, pieces, table_sum, small_sum = outs
-    return (
-        whole.reshape(gathered, 1024, 1024),
-        pieces,
-        table_sum.reshape(1024, 1024),
-        small_sum.reshape(-1),
-    )
+    return whole.reshape(gathered, 1024, 1024), pieces, table_sum, small_sum.reshape(-1)
 
 
 def one_hot(places, count):
@@ -497,7 +569,6 @@
     if here:
         x0, arrived, source = look_up(idt, table_t, dense.T)
         x0 = x0[:width]
-        arrived, source = arrived[:fields], source[:fields]
     else:
         owner = idt // table_rows
         local = idt % table_rows
@@ -578,21 +649,6 @@
             g = g.astype(BF)
     dx0 = dx0 + g
 
-    packed = lax.dot_general(
-        dx0[:sparse].astype(BF).reshape(fields, edim, examples),
-        (source[:, None, :] == lane[None, :, None]).astype(BF),
-        (((2,), (1,)), ((0,), (0,))),
-        preferred_element_type=F32,
-    ).astype(BF)
-    packed = packed.reshape(sparse, groups, capacity).transpose(1, 0, 2)
-    delivered = lax.all_to_all(packed, "dp", 0, 0, tiled=True)
-    delivered = delivered.transpose(1, 0, 2).reshape(fields, edim, examples)
-    row_hot = (
-        arrived[:, :, None] == jnp.arange(table_rows, dtype=jnp.int32)[None, None, :]
-    ).astype(BF)
-    table_g = lax.dot_general(
-        delivered, row_hot, (((2,), (1,)), ((0,), (0,))), preferred_element_type=F32
-    )
     small = jnp.concatenate(
         cross_b + [head_grad, jnp.sum(s).reshape(1), loss.reshape(1)] + tower_biases
     )
@@ -604,17 +660,20 @@
         edges.append(tower_in_g[:, main:].reshape(-1))
         flat = jnp.concatenate([small] + edges)
         filled = jnp.zeros((32 * 1024,), F32).at[: flat.shape[0]].set(flat)
-        table_flat = jnp.pad(
-            table_g.astype(BF).reshape(sparse, table_rows), ((0, 1024 - sparse), (0, 0))
-        )
+        rows = jnp.pad(
+            dx0[:sparse].astype(BF).reshape(fields, edim, examples),
+            ((0, 0), (0, 40 - edim), (0, 0)),
+        ).reshape(fields // 2, 80, examples)
         whole, pieces32, table_sum, flat = reduce_all(
             [g[:main, :main].astype(BF) for g in cross_g]
             + [tower_in_g[:, :main].astype(BF), tower_out_g.astype(BF)],
             layers,
-            table_flat,
+            rows,
+            source,
+            arrived,
             filled.reshape(32, 1024),
         )
-        table_g = table_sum[:sparse].reshape(fields, edim, table_rows)
+        table_g = table_sum.reshape(fields, 40, table_rows)[:, :edim]
         at = small.shape[0]
         small = flat[:at]
         rest = width - main
@@ -633,6 +692,21 @@
         tower_in_out = jnp.concatenate([pieces32[0], side], axis=1)
         tower_out_out = pieces32[1]
     else:
+        packed = lax.dot_general(
+            dx0[:sparse].astype(BF).reshape(fields, edim, examples),
+            (source[:, None, :] == lane[None, :, None]).astype(BF),
+            (((2,), (1,)), ((0,), (0,))),
+            preferred_element_type=F32,
+        ).astype(BF)
+        packed = packed.reshape(sparse, groups, capacity).transpose(1, 0, 2)
+        delivered = lax.all_to_all(packed, "dp", 0, 0, tiled=True)
+        delivered = delivered.transpose(1, 0, 2).reshape(fields, edim, examples)
+        row_hot = (
+            arrived[:, :, None] == jnp.arange(table_rows, dtype=jnp.int32)[None, None, :]
+        ).astype(BF)
+        table_g = lax.dot_general(
+            delivered, row_hot, (((2,), (1,)), ((0,), (0,))), preferred_element_type=F32
+        )
         table_g = lax.psum(table_g, "section")
         small = lax.psum(small, both)
         cross_out = lax.psum(jnp.stack(cross_g), both)

time: 402 us -> 368 us (0.915)
  matrix products: 116 us -> 71.4 us
  Pallas kernels: 174 us -> 200 us
  waiting for transfers between devices: 7.24 us -> 0 us
  starting transfers between devices: 4.56 us -> 0 us
    dot_general x2 -> x0, matrix products: 46.4 us -> none  [the longest x1 23.5 us: body(): lax.dot_general(delivered, row_hot, (((2,), (1,)), ((0,), (0,))), preferr...]
    pallas_call x1, Pallas kernels: 113 us -> 138 us  [reduce_all(): pl.pallas_call(lambda *refs: reduce_kernel(units, gathered, *refs), out_s...]
    reshape x4 -> x0, local copies, waits for them, and re-layouts: 10.4 us -> none  [the longest x2 5.56 us: body(): packed = packed.reshape(sparse, groups, capacity).transpose(1, 0, 2)]
    all_to_all x1 -> x0, waiting for transfers between devices: 7.24 us -> none  [body(): delivered = lax.all_to_all(packed, 'dp', 0, 0, tiled=True)]
    transpose x2 -> x0, local copies, waits for them, and re-layouts: 7.23 us -> none  [the longest x1 5.37 us: body(): table_g = table_g.astype(F32).transpose(0, 2, 1)]
    slice x3, local copies, waits for them, and re-layouts: 5.05 us -> 11.5 us  [body(): g[:main, :main].astype(BF)]
    all_to_all x1 -> x0, starting transfers between devices: 4.56 us -> none  [body(): delivered = lax.all_to_all(packed, 'dp', 0, 0, tiled=True)]
    unnamed x55 -> x61, local copies, waits for them, and re-layouts: 9.24 us -> 13.1 us
  transfers between devices with their start and end apart: 1 -> 0, of which waited for: 1 -> 0; matrix products, arithmetic and copies ran while one was open for 9% -> 0% of each run, Pallas kernels for 0% -> 0%
where the time goes in v4:
time: 368 us; the launch traced here: 363 us
  Pallas kernels  200 us (54%)
  matrix products  71.4 us (19%)
  local copies, waits for them, and re-layouts  58.2 us (16%)
  other arithmetic  30.1 us (8%)
  between operations  3.94 us (1%)
    pallas_call x1, Pallas kernels, reduce_all(): pl.pallas_call(lambda *refs: reduce_kernel(units, gathered, *refs), out_s...  138 us
    dot_general x15, matrix products, mm(): lax.dot_general(left, right, ((contract[:1], contract[1:]), ((), ())), pr...  71.4 us
    pallas_call x1, Pallas kernels, look_up(): pl.pallas_call(functools.partial(lookup_kernel, fields, edim), out_shape=...  61.4 us
    another operation x4, other arithmetic, body(): cross_out = jnp.stack(crosses)  19.4 us
    unnamed x61, local copies, waits for them, and re-layouts  13.1 us
    slice x3, local copies, waits for them, and re-layouts, body(): g[:main, :main].astype(BF)  11.5 us

profile of v4, /device:TPU:1, one launch (start us, length us, event | category | flops | bytes accessed | tf_op | source)
XLA Modules:
  0.0 363.5 jit_solution(15487718260622096992)
XLA Ops:
  2.9 0.9 slice_reduce_fusion
  3.8 1.6 copy-done.2
  5.4 0.9 copy-done.5
  7.1 61.4 %look_up.1 = (bf16[1040,1024]{1,0:T(8,128)(2,1)S(1)}, s32[32,1024]{1,0:T(8,128)S(1)}, s32[32,1024]{1,0:T(8,128)S(1)}) custom-call(s32[26,1024]{1,0:T(8,128)S(1)} %bitcast.150, bf16[26,39,1024]{2,1,0:T(8,128)(2,1)S(1)} %bitcast.149, bf16[13,1024]{1,0:T(8,128)(2,1)S(1)} %bitcast.151), custom_call_target="tpu_custom_call" | custom-call | tf_op jit(solution)/shard_map/look_up/pallas_call | solution.py:510
  68.6 3.0 fusion.62
  71.6 3.7 %multiply_reduce_fusion.1 = (f32[1024]{0:T(1024)S(1)}, f32[1024,1024]{1,0:T(8,128)S(1)}) fusion(f32[1024]{0:T(1024)S(1)} %slice.160, f32[1024]{0:T(1024)S(1)} %copy-done.19, bf16[1024,1024]{1,0:T(8,128)(2,1)S(1)} %copy-done.20, f32[1024,1024]{1,0:T(8,128)S(1)} %fusion.62, f32[1024]{0:T(1024)S(1)} %copy-done.22), kind=kOutput, calls=%fused_computation.82 | convolution fusion | flops 2169502720 | bytes 10502144 | tf_op jit(solution)/shard_map/dot_general | solution.py:15
  75.4 3.2 fusion.9
  78.7 5.3 %fusion.11 = (bf16[1027,1024]{1,0:T(8,128)(2,1)}, f32[1027,1024]{1,0:T(8,128)S(1)}) fusion(bf16[1027,1024]{1,0:T(8,128)(2,1)S(1)} %get-tuple-element.71, bf16[1040,1024]{1,0:T(8,128)(2,1)S(1)} %get-tuple-element.31, f32[1027]{0:T(1024)S(1)} %get-tuple-element.43, bf16[3,1027,1027]{2,1,0:T(8,128)(2,1)S(1)} %bitcast.166), kind=kOutput, calls=%fused_computation.42 | convolution fusion | flops 2166394880 | bytes 15036416 | tf_op jit(solution)/shard_map/dot_general | solution.py:15
  84.0 7.2 %fusion.7 = (f32[1024]{0:T(1024)S(1)}, bf16[1027,1024]{1,0:T(8,128)(2,1)}, f32[1027,1024]{1,0:T(8,128)S(1)}) fusion(f32[1027]{0:T(1024)S(1)} %slice.159, bf16[1027,1024]{1,0:T(8,128)(2,1)} %get-tuple-element.73, bf16[1040,1024]{1,0:T(8,128)(2,1)S(1)} %get-tuple-element.31, f32[1027]{0:T(1024)S(1)} %get-tuple-element.41, bf16[3,1027,1027]{2,1,0:T(8,128)(2,1)S(1)} %bitcast.166), kind=kOutput, calls=%fused_computation.38 | convolution fusion | flops 2169548800 | bytes 15048704 | tf_op jit(solution)/shard_map/dot_general | solution.py:15
  91.2 1.2 fusion.72
  92.4 4.3 %convert_reduce_fusion.3 = (f32[1024]{0:T(1024)S(1)}, bf16[1024,1024]{0,1:T(8,128)(2,1)S(1)}, f32[1024]{0:T(1024)S(1)}) fusion(f32[1024,1024]{1,0:T(8,128)S(1)} %get-tuple-element.77, f32[1024]{0:T(1024)S(1)} %copy-done.19, f32[1024]{0:T(1024)S(1)} %slice.160, f32[1024]{0:T(1024)S(1)} %get-tuple-element.48), kind=kLoop, calls=%fused_computation.79 | loop fusion | flops 27260928 | bytes 6311936 | tf_op jit(solution)/shard_map/reduce_sum | solution.py:637
  96.7 3.9 %convolution_convert_fusion = bf16[1024,1024]{1,0:T(8,128)(2,1)} fusion(bf16[1024,1024]{0,1:T(8,128)(2,1)S(1)} %get-tuple-element.46, f32[1024,1024]{1,0:T(8,128)S(1)} %copy-done.26, f32[1024]{0:T(1024)S(1)} %copy-done.22), kind=kOutput, calls=%fused_computation.101 | convolution fusion | flops 2159017984 | bytes 8392704 | tf_op jit(solution)/shard_map/dot_general | solution.py:15
  100.7 6.1 %convert_reduce_fusion.4 = (f32[1024]{0:T(1024)S(1)}, bf16[1024,1024]{0,1:T(8,128)(2,1)}) fusion(f32[1024,1024]{1,0:T(8,128)S(1)} %copy-done.26, f32[1024]{0:T(1024)S(1)} %copy-done.22, bf16[1024,1024]{0,1:T(8,128)(2,1)S(1)} %get-tuple-element.46, bf16[1024,1024]{1,0:T(8,128)(2,1)S(1)} %copy-done.21), kind=kOutput, calls=%fused_computation.80 | convolution fusion | flops 2170551296 | bytes 10493952 | tf_op jit(solution)/shard_map/dot_general | solution.py:15
  106.8 5.0 %fusion.36 = bf16[1027,1024]{1,0:T(8,128)(2,1)S(1)} fusion(f32[1024]{0:T(1024)S(1)} %get-tuple-element.48, f32[1027]{0:T(1024)S(1)} %slice.159, bf16[3,1027,1027]{2,1,0:T(8,128)(2,1)} %param.18, bf16[1040,1024]{1,0:T(8,128)(2,1)S(1)} %get-tuple-element.31), kind=kOutput, calls=%fused_computation.84 | convolution fusion | flops 2171653120 | bytes 6619136 | tf_op jit(solution)/shard_map/dot_general | solution.py:15
  111.8 7.1 %convert_reduce_fusion = (f32[1027]{0:T(1024)S(1)}, f32[1027]{0:T(1024)S(1)}, f32[1027]{0:T(1024)S(1)}, f32[1027]{0:T(1024)S(1)}, bf16[1027,1024]{1,0:T(8,128)(2,1)S(1)}) fusion(bf16[1040,1024]{1,0:T(8,128)(2,1)S(1)} %get-tuple-element.31, f32[1027]{0:T(1024)S(1)} %slice.159, f32[1024]{0:T(1024)S(1)} %get-tuple-element.48, ...), kind=kOutput, calls=%fused_computation.48 | convolution fusion | flops 2188475392 | bytes 15077424 | tf_op jit(solution)/shard_map/dot_general | solution.py:15
  118.9 5.4 %fusion.6 = f32[1027,1024]{1,0:T(8,128)S(1)} fusion(bf16[1024,1024]{0,1:T(8,128)(2,1)} %get-tuple-element.80, bf16[1027,1024]{1,0:T(8,128)(2,1)S(1)} %copy-done, f32[1027,1024]{1,0:T(8,128)S(1)} %get-tuple-element.75, f32[1027,1024]{1,0:T(8,128)S(1)} %get-tuple-element.74, bf16[1027,1024]{1,0:T(8,128)(2,1)S(1)} %fusion.36, ...), kind=kOutput, calls=%fused_computation.34 | convolution fusion | flops 2165343232 | bytes 25241612 | tf_op jit(solution)/shard_map/dot_general | solution.py:15
  124.3 5.3 %fusion.3 = f32[1027,1024]{1,0:T(8,128)S(1)} fusion(f32[1027,1024]{1,0:T(8,128)S(1)} %fusion.6, bf16[1027,1024]{1,0:T(8,128)(2,1)S(1)} %get-tuple-element.78, bf16[3,1027,1027]{2,1,0:T(8,128)(2,1)} %param.18, bf16[1040,1024]{1,0:T(8,128)(2,1)S(1)} %get-tuple-element.31), kind=kOutput, calls=%fused_computation.30 | convolution fusion | flops 2167446528 | bytes 17152000 | tf_op jit(solution)/shard_map/dot_general | solution.py:15
  130.2 1.6 slice.292
  131.8 4.1 %reshape.150 = bf16[26,39,1024]{2,1,0:T(8,128)(2,1)} reshape(bf16[1014,1024]{1,0:T(8,128)(2,1)} %slice.292) | data formatting | bytes 4153344 | tf_op jit(solution)/shard_map/reshape | solution.py:664
  135.9 3.4 pad.7
  139.3 3.0 fusion.53
  142.4 2.2 copy-done.16
  144.7 1.1 slice.201
  145.7 3.8 %slice.290 = bf16[1024,1024]{1,0:T(8,128)(2,1)} slice(f32[1027,1027]{1,0:T(8,128)} %copy-done.16), slice={[0:1024], [0:1024]} | slice | bytes 4194304 | tf_op jit(solution)/shard_map/slice | solution.py:668
  149.9 3.9 %fusion.59 = f32[1024,1027]{0,1:T(8,128)S(1)} fusion(bf16[1024,1024]{0,1:T(8,128)(2,1)} %get-tuple-element.80, bf16[1040,1024]{1,0:T(8,128)(2,1)S(1)} %copy-done.8), kind=kOutput, calls=%fused_computation.119 | convolution fusion | flops 2153775104 | bytes 8417280 | tf_op jit(solution)/shard_map/dot_general | solution.py:15
  153.8 1.7 slice.288
  155.5 4.3 %copy.25 = bf16[1024,1024]{1,0:T(8,128)(2,1)} copy(bf16[1024,1024]{0,1:T(8,128)(2,1)} %slice.288) | data formatting | bytes 4194304 | tf_op jit(solution)/shard_map/slice | solution.py:669
  160.3 4.6 %fusion.65 = f32[1027,1027]{1,0:T(8,128)S(1)} fusion(bf16[1027,1024]{1,0:T(8,128)(2,1)} %get-tuple-element.73, f32[1024]{0:T(1024)S(1)} %get-tuple-element.48, f32[1027]{0:T(1024)S(1)} %slice.159, bf16[1040,1024]{1,0:T(8,128)(2,1)S(1)} %copy-done.8), kind=kOutput, calls=%fused_computation.125 | convolution fusion | flops 2166394880 | bytes 8448036 | tf_op jit(solution)/shard_map/dot_general | solution.py:15
  165.0 2.1 copy-done.15
  167.2 4.6 %fusion.51 = f32[1027,1027]{1,0:T(8,128)S(1)} fusion(bf16[1027,1024]{1,0:T(8,128)(2,1)} %copy-done.9, bf16[1040,1024]{1,0:T(8,128)(2,1)S(1)} %copy-done.8), kind=kOutput, calls=%fused_computation.102 | convolution fusion | flops 2164291584 | bytes 10549284 | tf_op jit(solution)/shard_map/dot_general | solution.py:15
  171.8 2.2 copy-done.17
  174.1 1.1 slice.199
  175.2 3.8 %slice.291 = bf16[1024,1024]{1,0:T(8,128)(2,1)} slice(f32[1027,1027]{1,0:T(8,128)} %copy-done.17), slice={[0:1024], [0:1024]} | slice | bytes 4194304 | tf_op jit(solution)/shard_map/slice | solution.py:668
  179.3 1.1 slice.203
  180.4 3.8 %slice.289 = bf16[1024,1024]{1,0:T(8,128)(2,1)} slice(f32[1027,1027]{1,0:T(8,128)} %copy-done.15), slice={[0:1024], [0:1024]} | slice | bytes 4194304 | tf_op jit(solution)/shard_map/slice | solution.py:668
  184.5 1.4 concatenate.26
  186.6 138.5 %reduce_all.1 = (bf16[3,2,2,4,2,32,1024]{6,5,4,3,2,1,0:T(8,128)(2,1)}, f32[2,32,1024]{2,1,0:T(8,128)}, bf16[13,80,1024]{2,1,0:T(8,128)(2,1)}, f32[2,16,1024]{2,1,0:T(8,128)}) custom-call(bf16[2,2,4,2,32,1024]{5,4,3,2,1,0:T(8,128)(2,1)} %bitcast.155, bf16[2,2,4,2,32,1024]{5,4,3,2,1,0:T(8,128)(2,1)} %bitcast.153, bf16[2,2,4,2,32,1024]{5,4,3,2,1,0:T(8,128)(2,1)} %bitcast.156, ...), custom_call_target="tpu_custom_call" | custom-call | tf_op jit(solution)/shard_map/reduce_all/pallas_call | solution.py:324
  325.1 1.1 copy.27
  330.4 1.7 slice_bitcast_fusion
  333.8 1.1 reshape.163
  335.0 2.6 convert_bitcast_fusion
  337.6 1.7 copy-done.12
  339.3 1.1 fusion.74
  341.4 2.7 maximum_bitcast_fusion
  344.1 1.3 bitcast_convert_fusion
  345.4 2.6 maximum_bitcast_fusion.2
  348.0 2.6 maximum_bitcast_fusion.1
  350.6 11.5 %pad_maximum_fusion = f32[3,1027,1027]{2,1,0:T(8,128)} fusion(f32[1,1027,1027]{2,1,0:T(8,128)} %maximum_bitcast_fusion.2, f32[1,1027,1027]{2,1,0:T(8,128)} %maximum_bitcast_fusion.1, f32[1,1027,1027]{2,1,0:T(8,128)} %maximum_bitcast_fusion), kind=kLoop, calls=%fused_computation | loop fusion | flops 6328374 | bytes 25313496 | tf_op jit(solution)/shard_map/stack | solution.py:688
  (89 shorter events, 11.6 us)
Async XLA Ops:
  0.6 67.9 %copy-start = (bf16[1027,1024]{1,0:T(8,128)(2,1)S(1)}, bf16[1027,1024]{1,0:T(8,128)(2,1)}, u32[]{:S(2)}) copy-start(bf16[1027,1024]{1,0:T(8,128)(2,1)} %param.20) | copy-start | bytes 6309892
  3.8 1.6 copy-start.2
  5.4 0.9 copy-start.5
  6.3 0.8 copy-start.6
  68.5 3.1 copy-start.3
  68.5 3.1 copy-start.4
  68.5 55.8 %copy-start.7 = (bf16[1040,1024]{1,0:T(8,128)(2,1)}, bf16[1040,1024]{1,0:T(8,128)(2,1)S(1)}, u32[]{:S(2)}) copy-start(bf16[1040,1024]{1,0:T(8,128)(2,1)S(1)} %get-tuple-element.31) | copy-start | bytes 6389764
  68.5 3.1 copy-start.19
  68.5 3.1 copy-start.20
  68.5 3.1 copy-start.22
  68.5 6.8 %slice-start = ((s8[7133184]{0:T(1024)(128)(4,1)}), s8[4194304]{0:T(1024)(128)(4,1)S(1)}, s32[]{:S(2)}) async-start(s8[7133184]{0:T(1024)(128)(4,1)} %bitcast.165), calls=%async_computation | async-start | bytes 8388608
  71.6 3.8 %copy-start.25 = (f32[1024,1024]{1,0:T(8,128)}, f32[1024,1024]{1,0:T(8,128)S(1)}, u32[]{:S(2)}) copy-start(f32[1024,1024]{1,0:T(8,128)S(1)} %fusion.62) | copy-start | bytes 12582916
  71.6 3.8 %slice-start.1 = ((s8[7133184]{0:T(1024)(128)(4,1)}), s8[2938880]{0:T(1024)(128)(4,1)S(1)}, s32[]{:S(2)}) async-start(s8[7133184]{0:T(1024)(128)(4,1)} %bitcast.165), calls=%async_computation.1 | async-start | bytes 5877760
  78.6 5.4 %copy-start.23 = (bf16[1027,1024]{1,0:T(8,128)(2,1)}, bf16[1027,1024]{1,0:T(8,128)(2,1)S(1)}, u32[]{:S(2)}) copy-start(bf16[1027,1024]{1,0:T(8,128)(2,1)S(1)} %get-tuple-element.71) | copy-start | bytes 6309892
  84.0 7.2 %copy-start.18 = (s32[1024]{0:T(1024)S(1)}, s32[1024]{0:T(1024)}, u32[]{:S(2)}) copy-start(s32[1024]{0:T(1024)} %param.16) | copy-start | bytes 12292
  91.2 5.5 %copy-start.26 = (f32[1024,1024]{1,0:T(8,128)S(1)}, f32[1024,1024]{1,0:T(8,128)}, u32[]{:S(2)}) copy-start(f32[1024,1024]{1,0:T(8,128)} %copy-done.25) | copy-start | bytes 12582916
  96.7 4.0 %copy-start.21 = (bf16[1024,1024]{1,0:T(8,128)(2,1)S(1)}, bf16[1024,1024]{1,0:T(8,128)(2,1)}, u32[]{:S(2)}) copy-start(bf16[1024,1024]{1,0:T(8,128)(2,1)} %param.22) | copy-start | bytes 6291460
  106.8 5.0 %copy-start.27 = (bf16[1027,1024]{1,0:T(8,128)(2,1)S(1)}, bf16[1027,1024]{1,0:T(8,128)(2,1)}, u32[]{:S(2)}) copy-start(bf16[1027,1024]{1,0:T(8,128)(2,1)} %get-tuple-element.51) | copy-start | bytes 6309892
  111.8 7.1 %copy-start.10 = (bf16[1027,1024]{1,0:T(8,128)(2,1)}, bf16[1027,1024]{1,0:T(8,128)(2,1)S(1)}, u32[]{:S(2)}) copy-start(bf16[1027,1024]{1,0:T(8,128)(2,1)S(1)} %fusion.36) | copy-start | bytes 6309892
  118.9 5.4 %copy-start.9 = (bf16[1027,1024]{1,0:T(8,128)(2,1)}, bf16[1027,1024]{1,0:T(8,128)(2,1)S(1)}, u32[]{:S(2)}) copy-start(bf16[1027,1024]{1,0:T(8,128)(2,1)S(1)} %get-tuple-element.78) | copy-start | bytes 6309892
  131.8 7.5 %copy-start.8 = (bf16[1040,1024]{1,0:T(8,128)(2,1)S(1)}, bf16[1040,1024]{1,0:T(8,128)(2,1)}, u32[]{:S(2)}) copy-start(bf16[1040,1024]{1,0:T(8,128)(2,1)} %copy-done.7) | copy-start | bytes 6389764
  135.9 3.4 copy-start.11
  135.9 3.4 copy-start.24
  142.4 2.2 copy-start.16
  165.0 2.2 copy-start.15
  171.8 2.2 copy-start.17
  325.1 9.9 %copy-start.13 = (bf16[13,80,1024]{2,1,0:T(8,128)(2,1)S(1)}, bf16[13,80,1024]{2,1,0:T(8,128)(2,1)}, u32[]{:S(2)}) copy-start(bf16[13,80,1024]{2,1,0:T(8,128)(2,1)} %get-tuple-element.35) | copy-start | bytes 6389764
  335.0 4.3 %copy-start.12 = (bf16[3,2,2,4,2,32,1024]{6,5,4,3,2,1,0:T(8,128)(2,1)S(1)}, bf16[3,2,2,4,2,32,1024]{6,5,4,3,2,1,0:T(8,128)(2,1)}, u32[]{:S(2)}) copy-start(bf16[3,2,2,4,2,32,1024]{6,5,4,3,2,1,0:T(8,128)(2,1)} %get-tuple-element.36) | copy-start | bytes 18874372
  340.4 1.0 copy-start.14
  350.6 11.5 %copy-start.1 = (bf16[1027,1024]{1,0:T(8,128)(2,1)S(1)}, bf16[1027,1024]{1,0:T(8,128)(2,1)}, u32[]{:S(2)}) copy-start(bf16[1027,1024]{1,0:T(8,128)(2,1)} %param.20) | copy-start | bytes 6309892

commit v5 on v4

--- a/solution.py
+++ b/solution.py
@@ -1,4 +1,5 @@
 import functools
+import math
 
 import jax
 import jax.numpy as jnp
@@ -491,6 +492,7 @@
     for f in range(fields):
         x0f[f * edim : f * edim + edim] = wide_rows[f, :edim]
     x0f[sparse : sparse + extra] = dense_ref[...].astype(F32)
+    x0f[sparse + extra : sparse + extra + 1] = jnp.ones_like(x0f[:1])
     x0_ref[...] = x0f[...].astype(BF)
 
     @pl.loop(0, fields // 2)
@@ -505,7 +507,7 @@
 def look_up(ids_t, table_t, dense_t):
     fields, count = ids_t.shape
     edim = table_t.shape[1]
-    tall = -(-(fields * edim + dense_t.shape[0]) // 16) * 16
+    tall = (fields * edim + dense_t.shape[0]) // 16 * 16 + 16
     vmem = pl.BlockSpec(memory_space=pltpu.VMEM)
     return pl.pallas_call(
         functools.partial(lookup_kernel, fields, edim),
@@ -537,7 +539,225 @@
     )(ids_t, table_t, dense_t)
 
 
-def body(
+def gelu_and_slope(pre):
+    root = (2.0 / math.pi) ** 0.5
+    square = pre * pre
+    tanh = jnp.tanh(root * pre * (1.0 + 0.044715 * square))
+    cdf = 0.5 + 0.5 * tanh
+    bend = 0.5 * root * (1.0 - tanh * tanh) * (1.0 + 3 * 0.044715 * square)
+    return pre * cdf, cdf + pre * bend
+
+
+def network_kernel(
+    width, edim, x0_ref, labels_ref, weight_ref, in_ref, out_ref, cols_ref, hb_ref,
+    probs_ref, rows_ref, dense_ref, small_ref, *rest,
+):
+    layers = weight_ref.shape[0]
+    grads = rest[: layers + 2]
+    xs, vs, h1s, q1s, q2s, us, d1s, d2s, dxs, accx, acch, accs, stage, leave = rest[layers + 2 :]
+    main = in_ref.shape[1]
+    edge = slice(main, main + 16)
+    count = x0_ref.shape[1]
+    block = us.shape[2]
+    pairs = rows_ref.shape[0]
+
+    def dot(a, b, ca, cb):
+        return lax.dot_general(a, b, (((ca,), (cb,)), ((), ())), preferred_element_type=F32)
+
+    def fold(value):
+        return functools.reduce(
+            lambda a, b: a + b, [value[:, n : n + 128] for n in range(0, value.shape[1], 128)]
+        )
+
+    for layer in range(1, layers):
+        xs[layer - 1, edge] = x0_ref[edge]
+    for layer in range(layers):
+        vs[layer, main:] = jnp.zeros_like(vs[layer, main:])
+    accx[...] = jnp.zeros_like(accx)
+    acch[...] = jnp.zeros_like(acch)
+    accs[...] = jnp.zeros_like(accs)
+
+    @pl.loop(0, count // block)
+    def _(n):
+        at = pl.ds(pl.multiple_of(n * block, block), block)
+
+        def x_of(layer):
+            return x0_ref[:width, at] if layer == 0 else xs[layer - 1, :width, at]
+
+        def col(k, size):
+            return cols_ref[:size, k : k + 1]
+
+        for layer in range(layers):
+            u = dot(weight_ref[layer], x_of(layer), 0, 0) + col(layer, width)
+            us[layer, :width] = u
+            x = (x_of(0).astype(F32) * u + x_of(layer).astype(F32)).astype(BF)
+            if layer + 1 < layers:
+                xs[layer, :width, at] = x
+        last = x.astype(F32)
+        h1, d1 = gelu_and_slope(dot(in_ref[...], x_of(0), 0, 0) + col(layers, main))
+        d1s[...] = d1
+        h1s[:, at] = h1.astype(BF)
+        h2, d2 = gelu_and_slope(dot(out_ref[...], h1s[:, at], 0, 0) + col(layers + 1, main))
+        d2s[...] = d2
+        head_cross, head_tower = col(layers + 2, width), col(layers + 3, main)
+        z = (
+            jnp.sum(last * head_cross, axis=0, keepdims=True)
+            + jnp.sum(h2 * head_tower, axis=0, keepdims=True)
+            + hb_ref[0]
+        )
+        probs = jax.nn.sigmoid(z)
+        target = labels_ref[:, at].astype(F32)
+        probs_ref[:, at] = probs
+        s = probs - target
+        loss = jnp.maximum(z, 0.0) + jnp.log1p(jnp.exp(-jnp.abs(z))) - target * z
+        accs[0:1] += fold(s)
+        accs[1:2] += fold(loss)
+        accx[:width] += fold(s * last)
+        acch[...] += fold(s * h2)
+
+        q2 = ((s * head_tower) * d2s[...]).astype(BF)
+        q2s[:, at] = q2
+        q1 = (dot(out_ref[...], q2, 1, 0) * d1s[...]).astype(BF)
+        q1s[:, at] = q1
+        dxs[:width] = dot(in_ref[...], q1, 1, 0)
+        g = (s * head_cross).astype(BF)
+        for layer in reversed(range(layers)):
+            wide = g.astype(F32)
+            v = (wide * x_of(0).astype(F32)).astype(BF)
+            vs[layer, :width, at] = v
+            dxs[:width] += wide * us[layer, :width]
+            g = wide + dot(weight_ref[layer], v, 1, 0)
+            if layer:
+                g = g.astype(BF)
+        dxs[:width] += g
+        for i in range(pairs):
+            low = 2 * i * edim
+            both = [dxs[low : low + 40], dxs[low + edim : low + edim + 40]]
+            rows_ref[i, :, at] = jnp.concatenate(both, axis=0).astype(BF)
+        dense_ref[:, at] = dxs[2 * pairs * edim : width]
+
+    def x_all(layer, part):
+        return x0_ref[part] if layer == 0 else xs[layer - 1, part]
+
+    body = slice(0, main)
+
+    def copy_out(m):
+        return pltpu.make_async_copy(stage.at[m % 2], grads[m], leave.at[m % 2])
+
+    def store(m, value):
+        if m >= 2:
+            copy_out(m - 2).wait()
+        stage[m % 2] = value.astype(BF)
+        copy_out(m).start()
+
+    for layer in range(layers):
+        store(layer, dot(x_all(layer, body), vs[layer, body], 1, 1))
+        bottom = dot(x_all(layer, edge), vs[layer], 1, 1)
+        side = dot(vs[layer, edge], x_all(layer, body), 1, 1)
+        corner = jnp.concatenate(
+            [bottom[r : r + 1, main : main + 128] for r in range(4)]
+            + [jnp.zeros((1, main - 512), F32)],
+            axis=1,
+        )
+        small_ref[8 * layer : 8 * layer + 8] = jnp.concatenate(
+            [bottom[0:4, :main], side[0:3], corner], axis=0
+        )
+    store(layers, dot(q1s[...], x0_ref[body], 1, 1))
+    store(layers + 1, dot(q2s[...], h1s[...], 1, 1))
+    in_edge = dot(x0_ref[edge], q1s[...], 1, 1)
+    out_edge = dot(x0_ref[edge], q2s[...], 1, 1)
+    head_x = jnp.sum(accx[...].T, axis=0, keepdims=True)
+    head_h = jnp.sum(acch[...].T, axis=0, keepdims=True)
+    sums = [
+        jnp.broadcast_to(jnp.sum(accs[k : k + 1], axis=1, keepdims=True), (1, 128)) for k in (0, 1)
+    ]
+    misc = jnp.concatenate([head_x[:, main:]] + sums + [jnp.zeros((1, main - 384), F32)], axis=1)
+    small_ref[8 * layers :] = jnp.concatenate(
+        [in_edge[0:4], out_edge[3:4], head_x[:, :main], head_h, misc], axis=0
+    )
+    copy_out(layers).wait()
+    copy_out(layers + 1).wait()
+
+
+def network(x0, labels, cross_weight, tower_in, tower_out, cols, head_bias, edim, pairs):
+    layers, width = cross_weight.shape[:2]
+    main = tower_out.shape[0]
+    count = x0.shape[1]
+    block = 256
+    tall = x0.shape[0]
+    vmem = pl.BlockSpec(memory_space=pltpu.VMEM)
+    return pl.pallas_call(
+        functools.partial(network_kernel, width, edim),
+        out_shape=[
+            jax.ShapeDtypeStruct((1, count), F32),
+            jax.ShapeDtypeStruct((pairs, 80, count), BF),
+            jax.ShapeDtypeStruct((width - 2 * pairs * edim, count), F32),
+            jax.ShapeDtypeStruct((8 * layers + 8, main), F32),
+        ]
+        + [jax.ShapeDtypeStruct((main, main), BF)] * (layers + 2),
+        in_specs=[vmem] * 6 + [pl.BlockSpec(memory_space=pltpu.SMEM)],
+        out_specs=[vmem] * 4 + [pl.BlockSpec(memory_space=pl.ANY)] * (layers + 2),
+        scratch_shapes=[
+            pltpu.VMEM((layers - 1, tall, count), BF),
+            pltpu.VMEM((layers, main + 128, count), BF),
+            pltpu.VMEM((main, count), BF),
+            pltpu.VMEM((main, count), BF),
+            pltpu.VMEM((main, count), BF),
+            pltpu.VMEM((layers, tall, block), F32),
+            pltpu.VMEM((main, block), F32),
+            pltpu.VMEM((main, block), F32),
+            pltpu.VMEM((tall, block), F32),
+            pltpu.VMEM((main + 128, 128), F32),
+            pltpu.VMEM((main, 128), F32),
+            pltpu.VMEM((8, 128), F32),
+            pltpu.VMEM((2, main, main), BF),
+            pltpu.SemaphoreType.DMA((2,)),
+        ],
+        compiler_params=pltpu.CompilerParams(vmem_limit_bytes=60 * 2**20),
+        name="network",
+    )(x0, labels, cross_weight, tower_in, tower_out, cols, head_bias)
+
+
+def finish_kernel(whole_ref, small_ref, out_ref):
+    main = whole_ref.shape[2]
+    rest = out_ref.shape[2] - main
+    block = pl.program_id(1)
+    layer = pl.program_id(0)
+    rows = whole_ref.shape[1]
+
+    @pl.when(block * rows < main)
+    def _():
+        out_ref[0, :, :main] = whole_ref[0].astype(F32)
+        at = pl.ds(pl.multiple_of(block * rows, rows), rows)
+        side = small_ref[0, :, at]
+        out_ref[0, :, main:] = side.T[:, 4 : 4 + rest]
+
+    @pl.when(block * rows == main)
+    def _():
+        out_ref[0, :rest, :main] = small_ref[0, :rest]
+        corner = [small_ref[0, 7:8, 128 * r : 128 * r + rest] for r in range(rest)]
+        out_ref[0, :rest, main:] = jnp.concatenate(corner, axis=0)
+
+
+def finish(whole, small, width):
+    layers, main = whole.shape[:2]
+    rows = 256
+    blocks = main // rows
+    return pl.pallas_call(
+        finish_kernel,
+        out_shape=jax.ShapeDtypeStruct((layers, width, width), F32),
+        grid=(layers, blocks + 1),
+        in_specs=[
+            pl.BlockSpec((1, rows, main), lambda i, j: (i, jnp.minimum(j, blocks - 1), 0)),
+            pl.BlockSpec((1, 8, main), lambda i, j: (i, 0, 0)),
+        ],
+        out_specs=pl.BlockSpec((1, rows, width), lambda i, j: (i, j, 0)),
+        compiler_params=pltpu.CompilerParams(vmem_limit_bytes=32 * 2**20),
+        name="finish",
+    )(whole, small)
+
+
+def general_body(
     ids,
     dense,
     labels,
@@ -563,48 +783,37 @@
     me = lax.axis_index("section") * groups + lax.axis_index("dp")
 
     idt = ids.T
+    owner = idt // table_rows
+    local = idt % table_rows
+    owner_hot = owner[:, None, :] == jnp.arange(groups, dtype=jnp.int32)[None, :, None]
+    lane = jnp.arange(examples, dtype=jnp.int32)
+    before = (lane[:, None] < lane[None, :]).astype(BF)
+    counts = mm(owner_hot.reshape(fields * groups, examples).astype(BF), before, (1, 0))
+    rank = jnp.sum(jnp.where(owner_hot, counts.reshape(fields, groups, examples), 0.0), axis=1)
+    slot = owner * capacity + rank.astype(jnp.int32)
+    slot_hot = (slot[:, None, :] == lane[None, :, None]).astype(BF)
+    halves = jnp.stack([local // 32, local % 32], axis=1).astype(BF)
+    sent = lax.dot_general(
+        halves, slot_hot, (((2,), (2,)), ((0,), (0,))), preferred_element_type=F32
+    )
+    requests = (sent[:, 0] * 32 + sent[:, 1]).astype(jnp.int32)
+    requests = requests.reshape(fields, groups, capacity).transpose(1, 0, 2)
+    arrived = lax.all_to_all(requests, "dp", 0, 0, tiled=True)
+    arrived = arrived.transpose(1, 0, 2).reshape(fields, examples)
+    row_hot = (
+        arrived[:, None, :] == jnp.arange(table_rows, dtype=jnp.int32)[None, :, None]
+    ).astype(BF)
     table_t = table.transpose(0, 2, 1)
-    lane = jnp.arange(examples, dtype=jnp.int32)
-    here = (sections, groups, capacity, table_rows) == (4, 8, 128, 1024)
-    if here:
-        x0, arrived, source = look_up(idt, table_t, dense.T)
-        x0 = x0[:width]
-    else:
-        owner = idt // table_rows
-        local = idt % table_rows
-        owner_hot = owner[:, None, :] == jnp.arange(groups, dtype=jnp.int32)[None, :, None]
-        before = (lane[:, None] < lane[None, :]).astype(BF)
-        counts = mm(owner_hot.reshape(fields * groups, examples).astype(BF), before, (1, 0))
-        rank = jnp.sum(jnp.where(owner_hot, counts.reshape(fields, groups, examples), 0.0), axis=1)
-        slot = owner * capacity + rank.astype(jnp.int32)
-        slot_hot = (slot[:, None, :] == lane[None, :, None]).astype(BF)
-        values = [local // 32, local % 32] + [
-            jnp.broadcast_to(part, idt.shape) for part in (lane // 32, lane % 32)
-        ]
-        sent = lax.dot_general(
-            jnp.stack(values, axis=1).astype(BF),
-            slot_hot,
-            (((2,), (2,)), ((0,), (0,))),
-            preferred_element_type=F32,
-        )
-        requests = (sent[:, 0] * 32 + sent[:, 1]).astype(jnp.int32)
-        source = (sent[:, 2] * 32 + sent[:, 3]).astype(jnp.int32)
-        requests = requests.reshape(fields, groups, capacity).transpose(1, 0, 2)
-        arrived = lax.all_to_all(requests, "dp", 0, 0, tiled=True)
-        arrived = arrived.transpose(1, 0, 2).reshape(fields, examples)
-        row_hot = (
-            arrived[:, None, :] == jnp.arange(table_rows, dtype=jnp.int32)[None, :, None]
-        ).astype(BF)
-        found = lax.dot_general(
-            table_t, row_hot, (((2,), (1,)), ((0,), (0,))), preferred_element_type=F32
-        ).astype(BF)
-        found = found.reshape(sparse, groups, capacity).transpose(1, 0, 2)
-        replies = lax.all_to_all(found, "dp", 0, 0, tiled=True)
-        replies = replies.transpose(1, 0, 2).reshape(fields, edim, examples)
-        embedded = lax.dot_general(
-            replies, slot_hot, (((2,), (1,)), ((0,), (0,))), preferred_element_type=F32
-        ).astype(BF)
-        x0 = jnp.concatenate([embedded.reshape(sparse, examples), dense.T], axis=0)
+    found = lax.dot_general(
+        table_t, row_hot, (((2,), (1,)), ((0,), (0,))), preferred_element_type=F32
+    ).astype(BF)
+    found = found.reshape(sparse, groups, capacity).transpose(1, 0, 2)
+    replies = lax.all_to_all(found, "dp", 0, 0, tiled=True)
+    replies = replies.transpose(1, 0, 2).reshape(fields, edim, examples)
+    embedded = lax.dot_general(
+        replies, slot_hot, (((2,), (1,)), ((0,), (0,))), preferred_element_type=F32
+    ).astype(BF)
+    x0 = jnp.concatenate([embedded.reshape(sparse, examples), dense.T], axis=0)
 
     x0w = x0.astype(F32)
     xs, us = [x0], []
@@ -649,75 +858,37 @@
             g = g.astype(BF)
     dx0 = dx0 + g
 
+    packed = lax.dot_general(
+        dx0[:sparse].astype(BF).reshape(fields, edim, examples),
+        slot_hot,
+        (((2,), (2,)), ((0,), (0,))),
+        preferred_element_type=F32,
+    ).astype(BF)
+    packed = packed.reshape(sparse, groups, capacity).transpose(1, 0, 2)
+    delivered = lax.all_to_all(packed, "dp", 0, 0, tiled=True)
+    delivered = delivered.transpose(1, 0, 2).reshape(fields, edim, examples)
+    table_g = lax.dot_general(
+        delivered, row_hot, (((2,), (2,)), ((0,), (0,))), preferred_element_type=F32
+    )
+    table_g = lax.psum(table_g, "section").transpose(0, 2, 1)
+
     small = jnp.concatenate(
         cross_b + [head_grad, jnp.sum(s).reshape(1), loss.reshape(1)] + tower_biases
     )
-    both = ("section", "dp")
-    share = hidden // device_count
-    main = hidden
-    if here:
-        edges = [jnp.concatenate([g[main:].reshape(-1), g[:main, main:].reshape(-1)]) for g in cross_g]
-        edges.append(tower_in_g[:, main:].reshape(-1))
-        flat = jnp.concatenate([small] + edges)
-        filled = jnp.zeros((32 * 1024,), F32).at[: flat.shape[0]].set(flat)
-        rows = jnp.pad(
-            dx0[:sparse].astype(BF).reshape(fields, edim, examples),
-            ((0, 0), (0, 40 - edim), (0, 0)),
-        ).reshape(fields // 2, 80, examples)
-        whole, pieces32, table_sum, flat = reduce_all(
-            [g[:main, :main].astype(BF) for g in cross_g]
-            + [tower_in_g[:, :main].astype(BF), tower_out_g.astype(BF)],
-            layers,
-            rows,
-            source,
-            arrived,
-            filled.reshape(32, 1024),
-        )
-        table_g = table_sum.reshape(fields, 40, table_rows)[:, :edim]
-        at = small.shape[0]
-        small = flat[:at]
-        rest = width - main
-        crosses = []
-        for layer in range(layers):
-            bottom = flat[at : at + rest * width].reshape(rest, width)
-            at += rest * width
-            side = flat[at : at + main * rest].reshape(main, rest)
-            at += main * rest
-            top = jnp.concatenate([whole[layer].astype(F32), side], axis=1)
-            crosses.append(jnp.concatenate([top, bottom], axis=0))
-        cross_out = jnp.stack(crosses)
-        side = lax.dynamic_slice(
-            flat[at : at + hidden * rest].reshape(hidden, rest), (me * share, 0), (share, rest)
-        )
-        tower_in_out = jnp.concatenate([pieces32[0], side], axis=1)
-        tower_out_out = pieces32[1]
-    else:
-        packed = lax.dot_general(
-            dx0[:sparse].astype(BF).reshape(fields, edim, examples),
-            (source[:, None, :] == lane[None, :, None]).astype(BF),
-            (((2,), (1,)), ((0,), (0,))),
-            preferred_element_type=F32,
-        ).astype(BF)
-        packed = packed.reshape(sparse, groups, capacity).transpose(1, 0, 2)
-        delivered = lax.all_to_all(packed, "dp", 0, 0, tiled=True)
-        delivered = delivered.transpose(1, 0, 2).reshape(fields, edim, examples)
-        row_hot = (
-            arrived[:, :, None] == jnp.arange(table_rows, dtype=jnp.int32)[None, None, :]
-        ).astype(BF)
-        table_g = lax.dot_general(
-            delivered, row_hot, (((2,), (1,)), ((0,), (0,))), preferred_element_type=F32
-        )
-        table_g = lax.psum(table_g, "section")
-        small = lax.psum(small, both)
-        cross_out = lax.psum(jnp.stack(cross_g), both)
-        tower_in_out = lax.psum_scatter(tower_in_g, both, scatter_dimension=0, tiled=True)
-        tower_out_out = lax.psum_scatter(tower_out_g, both, scatter_dimension=0, tiled=True)
-    table_g = table_g.astype(F32).transpose(0, 2, 1)
+    small = lax.psum(small, ("section", "dp"))
     sizes = [layers * width, width + hidden, 1, 1, hidden, hidden]
     ends = [sum(sizes[: i + 1]) for i in range(len(sizes))]
     pieces = [small[e - n : e] for e, n in zip(ends, sizes)]
     cross_b_out = pieces[0].reshape(layers, width)
+    share = hidden // device_count
     bias_in, bias_out = (lax.dynamic_slice(p, (me * share,), (share,)) for p in pieces[4:])
+    cross_out = lax.psum(jnp.stack(cross_g), ("section", "dp"))
+    tower_in_out = lax.psum_scatter(
+        tower_in_g, ("section", "dp"), scatter_dimension=0, tiled=True
+    )
+    tower_out_out = lax.psum_scatter(
+        tower_out_g, ("section", "dp"), scatter_dimension=0, tiled=True
+    )
     return (
         probs,
         pieces[3] / (examples * device_count),
@@ -731,6 +902,86 @@
         bias_out,
         pieces[1],
         pieces[2],
+    )
+
+
+def body(
+    ids,
+    dense,
+    labels,
+    table,
+    cross_weight,
+    cross_bias,
+    tower_in,
+    tower_in_bias,
+    tower_out,
+    tower_out_bias,
+    head_weight,
+    head_bias,
+):
+    groups = lax.axis_size("dp")
+    sections = lax.axis_size("section")
+    device_count = groups * sections
+    examples, fields = ids.shape
+    table_rows, edim = table.shape[1:]
+    layers, width = cross_weight.shape[:2]
+    hidden = tower_out.shape[0]
+    capacity = examples // groups
+    me = lax.axis_index("section") * groups + lax.axis_index("dp")
+    idt = ids.T
+    table_t = table.transpose(0, 2, 1)
+    here = (sections, groups, capacity, table_rows) == (4, 8, 128, 1024)
+    if here:
+        x0, arrived, source = look_up(idt, table_t, dense.T)
+        tall = x0.shape[0]
+
+        def column(vector):
+            return jnp.pad(vector, (0, tall - vector.shape[0]))
+
+        columns = list(cross_bias) + [tower_in_bias, tower_out_bias]
+        columns += [head_weight[:width], head_weight[width:]]
+        probs, rows, dense_g, small, *grads = network(
+            x0,
+            labels.reshape(1, examples),
+            cross_weight,
+            tower_in,
+            tower_out,
+            jnp.stack([column(c) for c in columns], axis=1),
+            head_bias,
+            edim,
+            fields // 2,
+        )
+        whole, pieces, table_sum, small = reduce_all(grads, layers, rows, source, arrived, small)
+        small = small.reshape(8 * layers + 8, hidden)
+        main, rest = hidden, width - hidden
+        edges = small.reshape(layers + 1, 8, hidden)
+        cross_out = finish(whole, edges, width)
+        table_g = table_sum.reshape(fields, 40, table_rows)[:, :edim].astype(F32)
+        cross_b_out = jnp.concatenate(
+            [edges[:layers, 3], edges[:layers, 7, 384 : 384 + rest]], axis=1
+        )
+        share = hidden // device_count
+        mine = lax.dynamic_slice(edges[layers], (0, me * share), (5, share))
+        tower_in_out = jnp.concatenate([pieces[0], mine[:rest].T], axis=1)
+        misc = edges[layers, 7]
+        head_out = jnp.concatenate([edges[layers, 5], misc[:rest], edges[layers, 6]])
+        return (
+            probs.reshape(examples),
+            misc[256:257] / (examples * device_count),
+            dense_g.T,
+            table_g.transpose(0, 2, 1),
+            cross_out,
+            cross_b_out,
+            tower_in_out.T,
+            mine[3],
+            pieces[1].T,
+            mine[4],
+            head_out,
+            misc[128:129],
+        )
+    return general_body(
+        ids, dense, labels, table, cross_weight, cross_bias, tower_in, tower_in_bias, tower_out,
+        tower_out_bias, head_weight, head_bias,
     )
 
 

time: 368 us -> 308 us (0.84); the launches traced: 363 us -> 307 us
  Pallas kernels: 200 us -> 278 us
  matrix products: 71.4 us -> 0 us
  local copies, waits for them, and re-layouts: 58.2 us -> 21.2 us
  other arithmetic: 30.1 us -> 4.51 us
    pallas_call x0 -> x2, Pallas kernels: none -> 78.9 us  [the longest x1 70 us: network(): pl.pallas_call(functools.partial(network_kernel, width, edim), out_shape=...]
    dot_general x15 -> x0, matrix products: 71.4 us -> none  [mm(): lax.dot_general(left, right, ((contract[:1], contract[1:]), ((), ())), pr...]
    slice x23 -> x9, local copies, waits for them, and re-layouts: 27.5 us -> 5.28 us  [the longest x1 0.9 us: body(): edges[:layers, 3]]
    another operation x4 -> x0, other arithmetic: 19.4 us -> none  [body(): cross_out = jnp.stack(crosses)]
    reshape x16 -> x0, local copies, waits for them, and re-layouts: 8.58 us -> none  [the longest x1 4.09 us: body(): dx0[:sparse].astype(BF).reshape(fields, edim, examples)]
    reduce_sum x2 -> x0, other arithmetic: 5.51 us -> none  [the longest x1 4.3 us: body(): jnp.sum(q2.astype(F32), axis=1)]
    unnamed x61 -> x20, local copies, waits for them, and re-layouts: 13.1 us -> 9.59 us
where the time goes in v5:
time: 308 us; the launch traced here: 307 us
  Pallas kernels  278 us (90%)
  local copies, waits for them, and re-layouts  21.2 us (7%)
  other arithmetic  4.51 us (1%)
  between operations  3.2 us (1%)
    pallas_call x1, Pallas kernels, reduce_all(): pl.pallas_call(lambda *refs: reduce_kernel(units, gathered, *refs), out_s...  138 us
    pallas_call x1, Pallas kernels, network(): pl.pallas_call(functools.partial(network_kernel, width, edim), out_shape=...  70 us
    pallas_call x1, Pallas kernels, look_up(): pl.pallas_call(functools.partial(lookup_kernel, fields, edim), out_shape=...  61.1 us
    unnamed x20, local copies, waits for them, and re-layouts  9.59 us
    pallas_call x1, Pallas kernels, finish(): pl.pallas_call(finish_kernel, out_shape=jax.ShapeDtypeStruct((layers, wid...  8.86 us

profile of v5, /device:TPU:1, one launch (start us, length us, event | category | flops | bytes accessed | tf_op | source)
XLA Modules:
  0.0 307.2 jit_solution(13596640114983153868)
XLA Ops:
  0.6 0.9 slice_reduce_fusion
  1.6 0.8 slice.66
  2.4 0.7 pad.26
  3.1 0.7 pad.27
  3.8 0.7 slice_select_fusion
  4.5 0.1 stack.31
  4.6 1.0 copy.33.cols_ref
  5.6 0.0 copy-start.1
  5.6 1.6 copy-done.1
  7.2 0.0 copy-start.6
  7.2 0.9 copy-done.6
  8.1 0.0 copy-start.7
  8.1 0.8 copy-done.7
  8.9 61.1 %look_up.1 = (bf16[1040,1024]{1,0:T(8,128)(2,1)S(1)}, s32[32,1024]{1,0:T(8,128)S(1)}, s32[32,1024]{1,0:T(8,128)S(1)}) custom-call(s32[26,1024]{1,0:T(8,128)S(1)} %bitcast.53, bf16[26,39,1024]{2,1,0:T(8,128)(2,1)S(1)} %bitcast.45, bf16[13,1024]{1,0:T(8,128)(2,1)S(1)} %bitcast.54), custom_call_target="tpu_custom_call" | custom-call | tf_op jit(solution)/shard_map/look_up/pallas_call | solution.py:512
  69.9 0.0 copy-start.2
  70.0 1.3 copy-done.2
  71.3 0.0 copy-start.4
  71.3 0.7 copy-done.4
  71.9 0.0 copy-start.5
  71.9 0.7 copy-done.5
  73.2 70.0 %network.1 = (f32[1,1024]{1,0:T(1,128)}, bf16[13,80,1024]{2,1,0:T(8,128)(2,1)}, f32[13,1024]{1,0:T(8,128)}, f32[32,1024]{1,0:T(8,128)}, bf16[1024,1024]{1,0:T(8,...) custom-call(bf16[1040,1024]{1,0:T(8,128)(2,1)} %copy-done.2, ...), custom_call_target="tpu_custom_call" | custom-call | tf_op jit(solution)/shard_map/network/pallas_call | solution.py:689
  143.3 138.3 %reduce_all.1 = (bf16[3,2,2,4,2,32,1024]{6,5,4,3,2,1,0:T(8,128)(2,1)}, f32[2,32,1024]{2,1,0:T(8,128)}, bf16[13,80,1024]{2,1,0:T(8,128)(2,1)}, f32[2,16,1024]{2,1,0:T(8,128)}) custom-call(bf16[2,2,4,2,32,1024]{5,4,3,2,1,0:T(8,128)(2,1)} %bitcast.56, bf16[2,2,4,2,32,1024]{5,4,3,2,1,0:T(8,128)(2,1)} %bitcast.57, bf16[2,2,4,2,32,1024]{5,4,3,2,1,0:T(8,128)(2,1)} %bitcast.58, ...), custom_call_target="tpu_custom_call" | custom-call | tf_op jit(solution)/shard_map/reduce_all/pallas_call | solution.py:325
  281.6 0.8 fusion.1
  282.5 0.7 slice_bitcast_fusion.3
  283.1 0.7 concatenate.11
  283.8 0.8 slice.88
  284.6 0.1 constant_dynamic-slice_fusion
  284.6 0.1 copy.34
  284.7 1.6 slice_bitcast_fusion
  286.4 0.7 maximum_bitcast_fusion
  287.0 0.9 slice.86
  288.0 0.7 slice.87
  288.7 0.6 pad_maximum_fusion
  289.3 0.0 copy-start
  289.3 2.8 copy-done
  292.1 0.0 copy-start.3
  292.1 0.9 copy-done.3
  293.0 0.0 copy-start.8
  293.0 8.9 %finish.1 = f32[3,1027,1027]{2,1,0:T(8,128)} custom-call(bf16[3,1024,1024]{2,1,0:T(8,128)(2,1)S(1)} %bitcast.44, f32[4,8,1024]{2,1,0:T(8,128)S(1)} %bitcast.51), custom_call_target="tpu_custom_call" | custom-call | tf_op jit(solution)/shard_map/finish/pallas_call | solution.py:746
  301.8 0.5 slice_bitcast_fusion.4
  302.4 0.5 fusion
  303.5 0.0 copy-done.8
  303.5 2.5 convert_bitcast_fusion
  (14 shorter events, 0.1 us)
Async XLA Ops:
  5.6 1.6 copy-start.1
  7.2 0.9 copy-start.6
  8.1 0.8 copy-start.7
  69.9 1.3 copy-start.2
  71.3 0.7 copy-start.4
  71.9 0.7 copy-start.5
  289.3 2.8 copy-start
  292.1 0.9 copy-start.3
  293.0 10.5 %copy-start.8 = (bf16[13,80,1024]{2,1,0:T(8,128)(2,1)S(1)}, bf16[13,80,1024]{2,1,0:T(8,128)(2,1)}, u32[]{:S(2)}) copy-start(bf16[13,80,1024]{2,1,0:T(8,128)(2,1)} %get-tuple-element.41) | copy-start | bytes 6389764

commit v6 on v5

--- a/solution.py
+++ b/solution.py
@@ -23,17 +23,36 @@
     return act, back(jnp.ones_like(pre))[0]
 
 
+ORDER = [
+    "C0 P2 C2 u10",
+    "P1 C1 u12 P0",
+    "u11 C4 u20 C3",
+    "n0 u14 u22 P3",
+    "u13 S0 S1 n1",
+    "T10 u21 u30 S2",
+    "T11 T20 n2 u32",
+    "T12 u24 T21 u40",
+    "S3 n3 T22 u23",
+    "u31 T31 u42 u50",
+    "n4 T13 u60 u41",
+    "u52 u34 T23 n5",
+    "u33 T32 T41 u70",
+    "u51 u62 u61 u72",
+    "u44 T42 u43 T33",
+    "u80 T30 T40 u71",
+    "u82 T43 u81",
+]
 VIEW = (2, 2, 4, 2)
 
 
 def reduce_kernel(units, gathered, *refs):
-    grads = refs[:units]
-    rows_ref, inv_ref, arr_ref, small_ref = refs[units : units + 4]
-    whole, pieces, table_out, small_out = refs[units + 4 : units + 8]
+    lefts, rights = refs[:units], refs[units : 2 * units]
+    rows_ref, inv_ref, arr_ref, part_ref = refs[2 * units : 2 * units + 4]
+    whole, pieces, table_out, small_out = refs[2 * units + 4 : 2 * units + 8]
     (
-        rc, sa1, ra1, sb1, rb1, sa2, ra2, sb2, rb2, sz, rz, packed, back, summed, stc, rtc, st, rt, sm, rm, rmz,
-        send, recv, row_send, row_recv, table_send, table_recv,
-    ) = refs[units + 8 :]
+        grads, left, right, load, small, rc, sa1, ra1, sb1, rb1, sa2, ra2, sb2, rb2, sz, rz, packed, back, summed,
+        stc, rtc, st, rt, sm, rm, rmz, send, recv, row_send, row_recv, table_send, table_recv,
+    ) = refs[2 * units + 8 :]
     pairs, count = rows_ref.shape[0], rows_ref.shape[2]
     section, dp = lax.axis_index("section"), lax.axis_index("dp")
     y, c = section // 2, section % 2
@@ -54,7 +73,6 @@
     barrier = pltpu.get_barrier_semaphore()
     for peer in peers:
         pl.semaphore_signal(barrier, inc=1, device_id=peer, device_id_type=pl.DeviceIdType.MESH)
-    pl.semaphore_wait(barrier, len(peers))
 
     flying = []
 
@@ -77,8 +95,7 @@
     copies = {}
 
     def acc(m, stage, cols, yy, zz, xx):
-        g = grads[m]
-        total = wide(g[yy, c, zz, xx, :, cols]) + wide(rc[m, yy, zz, xx, :, cols])
+        total = wide(grads[m, yy, c, zz, xx, :, cols]) + wide(rc[m, yy, zz, xx, :, cols])
         if cols is lo:
             if stage >= 2:
                 total += wide(ra1[m, yy, zz])
@@ -91,8 +108,57 @@
                 total += wide(rb2[m, zz])
         return total
 
+    tokens = " ".join(ORDER).split()
+    made = [int(t[1]) for t in tokens if t[0] == "C"]
+
+    def height(m):
+        return min(lefts[m].shape[0], left.shape[1])
+
+    def loads(turn):
+        m, slot = made[turn], turn % 2
+        return [
+            pltpu.make_async_copy(ref.at[:rows], buf.at[slot, :rows], load.at[slot, k])
+            for k, (ref, buf, rows) in enumerate(
+                ((lefts[m], left, height(m)), (rights[m], right, rights[m].shape[0]))
+            )
+        ]
+
+    def make(m):
+        turn = made.index(m)
+        slot = turn % 2
+        for copy in loads(turn):
+            copy.wait()
+        tall = height(m) - 1024
+        across = rights[m].shape[0]
+        for r in range(2):
+            total = lax.dot_general(
+                left[slot, 512 * r : 512 * r + 512 + r * tall],
+                right[slot, :across],
+                (((1,), (1,)), ((), ())),
+                preferred_element_type=F32,
+            )
+            grads[m, r] = total[:512, :1024].astype(BF).reshape(2, 4, 2, 32, 1024)
+            if across > 1024:
+                side = total[:512, 1024:].T
+                group, at = m // 2, m % 2 * 8
+                if tall:
+                    small[group, at + 4 : at + 7, 512 * r : 512 * r + 512] = side[0:3]
+                else:
+                    small[group, at : at + 4, 512 * r : 512 * r + 512] = side[0:4]
+                if tall and r:
+                    small[group, at : at + 4] = total[512:516, :1024]
+                    small[group, at + 7 : at + 8, 512:] = jnp.zeros((1, 512), F32)
+                    for k in range(4):
+                        small[group, at + 7 : at + 8, 128 * k : 128 * k + 128] = total[
+                            512 + k : 513 + k, 1024:
+                        ]
+        if turn + 2 < units:
+            for copy in loads(turn + 2):
+                copy.start()
+
     def step0(m):
-        copies[m, 0] = start(grads[m].at[:, 1 - c], rc.at[m], m, 0, core_peer)
+        make(m)
+        copies[m, 0] = start(grads.at[m, :, 1 - c], rc.at[m], m, 0, core_peer)
 
     def step1(m):
         copies[m, 0].wait_recv()
@@ -181,8 +247,10 @@
             device_id_type=pl.DeviceIdType.MESH,
         )
 
-    def pack():
-        @pl.loop(0, pairs)
+    cuts = [pairs * q // 4 for q in range(5)]
+
+    def pack(q):
+        @pl.loop(cuts[q], cuts[q + 1])
         def _(i):
             first = jnp.dot(
                 rows_ref[i, 0:48],
@@ -199,8 +267,6 @@
                 row_copy(i, j).start()
             back[i, :, lanes(dp, 128)] = packed[i, :, lanes(dp, 128)]
 
-    cuts = [pairs * q // 4 for q in range(5)]
-
     def scatter(q):
         @pl.loop(cuts[q], cuts[q + 1])
         def _(i):
@@ -258,11 +324,12 @@
     s = units
 
     def small0():
-        copies[s, 0] = start(small_ref.at[1 - c], rm.at[0], s, 0, core_peer)
+        small[1, 12:16] = part_ref[0:4]
+        copies[s, 0] = start(small.at[1 - c], rm.at[0], s, 0, core_peer)
 
     def small1():
         copies[s, 0].wait_recv()
-        sm[0] = small_ref[c] + rm[0]
+        sm[0] = small[c] + rm[0]
         copies[s, 1] = start(sm.at[0], rm.at[1], s, 1, x_peer)
 
     def small2():
@@ -290,24 +357,24 @@
     def small5():
         copies[s, 6].wait_recv()
 
-    small0()
-    for m in range(units):
-        step0(m)
-    pack()
     steps = [step1, step2, step3, step4, step5, step6, step7, step8]
-    smalls = [small1, small2, small3, small4, small5]
-    tables = [scatter, table1, table2, table3, table4]
-    for now in range(units + len(steps)):
-        for k, step in enumerate(steps):
-            m = now - k
-            if 0 <= m < units and (k < 4 or m < gathered):
-                step(m)
-        if now < len(smalls):
-            smalls[now]()
-        for k in reversed(range(len(tables))):
-            q = now - 1 - k
-            if 0 <= q < 4:
-                tables[k](q)
+    smalls = [small0, small1, small2, small3, small4, small5]
+    tables = [table1, table2, table3, table4]
+    for copy in loads(0) + loads(1):
+        copy.start()
+    pl.semaphore_wait(barrier, len(peers))
+    for token in tokens:
+        kind, numbers = token[0], [int(n) for n in token[1:]]
+        if kind == "C":
+            step0(*numbers)
+        elif kind == "P":
+            pack(*numbers)
+        elif kind == "S":
+            scatter(*numbers)
+        elif kind == "n":
+            smalls[numbers[0]]()
+        else:
+            {"u": steps, "T": tables}[kind][numbers[0] - 1](numbers[1])
     for copy in flying:
         copy.wait_send()
 
@@ -317,8 +384,8 @@
             row_copy(i, j).wait_send()
 
 
-def reduce_all(grads, gathered, rows, source, arrived, small):
-    units = len(grads)
+def reduce_all(lefts, rights, gathered, rows, source, arrived, small):
+    units = len(lefts)
     pairs, _, count = rows.shape
     piece = (32, 1024)
     vmem = pl.BlockSpec(memory_space=pltpu.VMEM)
@@ -330,9 +397,14 @@
             jax.ShapeDtypeStruct((pairs, 80, count), BF),
             jax.ShapeDtypeStruct((2, 16, 1024), F32),
         ],
-        in_specs=[vmem] * (units + 4),
+        in_specs=[pl.BlockSpec(memory_space=pl.ANY)] * (2 * units) + [vmem] * 4,
         out_specs=[vmem] * 4,
         scratch_shapes=[
+            pltpu.VMEM((units,) + VIEW + piece, BF),
+            pltpu.VMEM((2, 1040, count), BF),
+            pltpu.VMEM((2, 1152, count), BF),
+            pltpu.SemaphoreType.DMA((2, 2)),
+            pltpu.VMEM((2, 16, 1024), F32),
             pltpu.VMEM((units, 2, 4, 2) + piece, BF),
             pltpu.VMEM((units, 2, 4, 32, 512), BF),
             pltpu.VMEM((units, 2, 4, 32, 512), BF),
@@ -362,15 +434,16 @@
             pltpu.SemaphoreType.DMA((4, 4)),
         ],
         compiler_params=pltpu.CompilerParams(
-            collective_id=0, has_side_effects=True, vmem_limit_bytes=60 * 2**20
+            collective_id=0, has_side_effects=True, vmem_limit_bytes=62 * 2**20
         ),
         name="reduce_all",
     )(
-        *[g.reshape(VIEW + piece) for g in grads],
+        *lefts,
+        *rights,
         rows,
         source,
         arrived,
-        small.reshape(2, 16, 1024),
+        small,
     )
     return whole.reshape(gathered, 1024, 1024), pieces, table_sum, small_sum.reshape(-1)
 
@@ -507,7 +580,7 @@
 def look_up(ids_t, table_t, dense_t):
     fields, count = ids_t.shape
     edim = table_t.shape[1]
-    tall = (fields * edim + dense_t.shape[0]) // 16 * 16 + 16
+    tall = (fields * edim + dense_t.shape[0]) // 128 * 128 + 128
     vmem = pl.BlockSpec(memory_space=pltpu.VMEM)
     return pl.pallas_call(
         functools.partial(lookup_kernel, fields, edim),
@@ -549,17 +622,24 @@
 
 
 def network_kernel(
-    width, edim, x0_ref, labels_ref, weight_ref, in_ref, out_ref, cols_ref, hb_ref,
+    width, edim, x0_ref, labels_ref, weight_ref, in_ref, out_ref, bias_ref, in_bias_ref, out_bias_ref, head_ref, hb_ref,
     probs_ref, rows_ref, dense_ref, small_ref, *rest,
 ):
     layers = weight_ref.shape[0]
-    grads = rest[: layers + 2]
-    xs, vs, h1s, q1s, q2s, us, d1s, d2s, dxs, accx, acch, accs, stage, leave = rest[layers + 2 :]
+    kept = 2 * layers + 2
+    outs = rest[:kept]
+    xs, vs, h1s, q1s, q2s, us, d1s, d2s, dxs, accx, acch, accq, accs, lines, cols, leave = rest[kept:]
     main = in_ref.shape[1]
     edge = slice(main, main + 16)
     count = x0_ref.shape[1]
     block = us.shape[2]
     pairs = rows_ref.shape[0]
+
+    def leaving(k, n):
+        at = pl.ds(pl.multiple_of(n * block, block), block)
+        here = [xs.at[i] for i in range(layers - 1)] + [vs.at[i] for i in range(layers)]
+        here += [h1s, q1s, q2s]
+        return pltpu.make_async_copy(here[k].at[:, at], outs[k].at[:, at], leave.at[n, k])
 
     def dot(a, b, ca, cb):
         return lax.dot_general(a, b, (((ca,), (cb,)), ((), ())), preferred_element_type=F32)
@@ -575,7 +655,15 @@
         vs[layer, main:] = jnp.zeros_like(vs[layer, main:])
     accx[...] = jnp.zeros_like(accx)
     acch[...] = jnp.zeros_like(acch)
+    accq[...] = jnp.zeros_like(accq)
     accs[...] = jnp.zeros_like(accs)
+    lines[...] = jnp.zeros_like(lines)
+    lines[0:layers, :width] = bias_ref[...]
+    lines[layers : layers + 1, :main] = in_bias_ref[...]
+    lines[layers + 1 : layers + 2, :main] = out_bias_ref[...]
+    lines[layers + 2 : layers + 3, :width] = head_ref[:, :width]
+    lines[layers + 3 : layers + 4, :main] = head_ref[:, width:]
+    cols[...] = lines[...].T
 
     @pl.loop(0, count // block)
     def _(n):
@@ -585,7 +673,7 @@
             return x0_ref[:width, at] if layer == 0 else xs[layer - 1, :width, at]
 
         def col(k, size):
-            return cols_ref[:size, k : k + 1]
+            return cols[:size, k : k + 1]
 
         for layer in range(layers):
             u = dot(weight_ref[layer], x_of(layer), 0, 0) + col(layer, width)
@@ -617,6 +705,8 @@
 
         q2 = ((s * head_tower) * d2s[...]).astype(BF)
         q2s[:, at] = q2
+        acc = fold(q2.astype(F32))
+        accq[...] += acc
         q1 = (dot(out_ref[...], q2, 1, 0) * d1s[...]).astype(BF)
         q1s[:, at] = q1
         dxs[:width] = dot(in_ref[...], q1, 1, 0)
@@ -636,55 +726,33 @@
             rows_ref[i, :, at] = jnp.concatenate(both, axis=0).astype(BF)
         dense_ref[:, at] = dxs[2 * pairs * edim : width]
 
-    def x_all(layer, part):
-        return x0_ref[part] if layer == 0 else xs[layer - 1, part]
-
-    body = slice(0, main)
-
-    def copy_out(m):
-        return pltpu.make_async_copy(stage.at[m % 2], grads[m], leave.at[m % 2])
-
-    def store(m, value):
-        if m >= 2:
-            copy_out(m - 2).wait()
-        stage[m % 2] = value.astype(BF)
-        copy_out(m).start()
-
-    for layer in range(layers):
-        store(layer, dot(x_all(layer, body), vs[layer, body], 1, 1))
-        bottom = dot(x_all(layer, edge), vs[layer], 1, 1)
-        side = dot(vs[layer, edge], x_all(layer, body), 1, 1)
-        corner = jnp.concatenate(
-            [bottom[r : r + 1, main : main + 128] for r in range(4)]
-            + [jnp.zeros((1, main - 512), F32)],
-            axis=1,
-        )
-        small_ref[8 * layer : 8 * layer + 8] = jnp.concatenate(
-            [bottom[0:4, :main], side[0:3], corner], axis=0
-        )
-    store(layers, dot(q1s[...], x0_ref[body], 1, 1))
-    store(layers + 1, dot(q2s[...], h1s[...], 1, 1))
-    in_edge = dot(x0_ref[edge], q1s[...], 1, 1)
-    out_edge = dot(x0_ref[edge], q2s[...], 1, 1)
+        for k in range(kept):
+            leaving(k, n).start()
+
+    @pl.loop(0, count // block)
+    def _(n):
+        for k in range(kept):
+            leaving(k, n).wait()
+
     head_x = jnp.sum(accx[...].T, axis=0, keepdims=True)
     head_h = jnp.sum(acch[...].T, axis=0, keepdims=True)
     sums = [
         jnp.broadcast_to(jnp.sum(accs[k : k + 1], axis=1, keepdims=True), (1, 128)) for k in (0, 1)
     ]
     misc = jnp.concatenate([head_x[:, main:]] + sums + [jnp.zeros((1, main - 384), F32)], axis=1)
-    small_ref[8 * layers :] = jnp.concatenate(
-        [in_edge[0:4], out_edge[3:4], head_x[:, :main], head_h, misc], axis=0
-    )
-    copy_out(layers).wait()
-    copy_out(layers + 1).wait()
-
-
-def network(x0, labels, cross_weight, tower_in, tower_out, cols, head_bias, edim, pairs):
+    bias = jnp.sum(accq[...].T, axis=0, keepdims=True)
+    small_ref[0:4] = jnp.concatenate([bias, head_x[:, :main], head_h, misc], axis=0)
+    small_ref[4:] = jnp.zeros_like(small_ref[4:])
+
+
+def network(
+    x0, labels, cross_weight, tower_in, tower_out, cross_bias, in_bias, out_bias, head, head_bias, edim, pairs
+):
     layers, width = cross_weight.shape[:2]
     main = tower_out.shape[0]
     count = x0.shape[1]
     block = 256
-    tall = x0.shape[0]
+    tall = main + 16
     vmem = pl.BlockSpec(memory_space=pltpu.VMEM)
     return pl.pallas_call(
         functools.partial(network_kernel, width, edim),
@@ -692,11 +760,13 @@
             jax.ShapeDtypeStruct((1, count), F32),
             jax.ShapeDtypeStruct((pairs, 80, count), BF),
             jax.ShapeDtypeStruct((width - 2 * pairs * edim, count), F32),
-            jax.ShapeDtypeStruct((8 * layers + 8, main), F32),
+            jax.ShapeDtypeStruct((8, main), F32),
         ]
-        + [jax.ShapeDtypeStruct((main, main), BF)] * (layers + 2),
-        in_specs=[vmem] * 6 + [pl.BlockSpec(memory_space=pltpu.SMEM)],
-        out_specs=[vmem] * 4 + [pl.BlockSpec(memory_space=pl.ANY)] * (layers + 2),
+        + [jax.ShapeDtypeStruct((tall, count), BF)] * (layers - 1)
+        + [jax.ShapeDtypeStruct((main + 128, count), BF)] * layers
+        + [jax.ShapeDtypeStruct((main, count), BF)] * 3,
+        in_specs=[vmem] * 9 + [pl.BlockSpec(memory_space=pltpu.SMEM)],
+        out_specs=[vmem] * 4 + [pl.BlockSpec(memory_space=pl.ANY)] * (2 * layers + 2),
         scratch_shapes=[
             pltpu.VMEM((layers - 1, tall, count), BF),
             pltpu.VMEM((layers, main + 128, count), BF),
@@ -709,52 +779,99 @@
             pltpu.VMEM((tall, block), F32),
             pltpu.VMEM((main + 128, 128), F32),
             pltpu.VMEM((main, 128), F32),
+            pltpu.VMEM((main, 128), F32),
             pltpu.VMEM((8, 128), F32),
-            pltpu.VMEM((2, main, main), BF),
-            pltpu.SemaphoreType.DMA((2,)),
+            pltpu.VMEM((128, main + 128), F32),
+            pltpu.VMEM((main + 128, 128), F32),
+            pltpu.SemaphoreType.DMA((count // block, 2 * layers + 2)),
         ],
         compiler_params=pltpu.CompilerParams(vmem_limit_bytes=60 * 2**20),
         name="network",
-    )(x0, labels, cross_weight, tower_in, tower_out, cols, head_bias)
-
-
-def finish_kernel(whole_ref, small_ref, out_ref):
-    main = whole_ref.shape[2]
+    )(x0, labels, cross_weight, tower_in, tower_out, cross_bias, in_bias, out_bias, head, head_bias)
+
+
+def finish_kernel(
+    whole_ref, small_ref, rows_ref, pieces_ref, out_ref, table_ref, bias_ref, in_ref, share_ref, out_piece_ref,
+    head_ref, sums_ref, turned,
+):
+    layers, main = small_ref.shape[0] - 1, small_ref.shape[2]
     rest = out_ref.shape[2] - main
-    block = pl.program_id(1)
+    width = main + rest
     layer = pl.program_id(0)
-    rows = whole_ref.shape[1]
-
-    @pl.when(block * rows < main)
+    edim = table_ref.shape[1]
+
+    edge = small_ref[layer]
+    out_ref[0, :main, :main] = whole_ref[0].astype(F32)
+    out_ref[0, :main, main:] = edge.T[:, 4 : 4 + rest]
+    out_ref[0, main:, :main] = edge[:rest]
+    for r in range(rest):
+        out_ref[0, main + r : main + r + 1, main:] = edge[7:8, 128 * r : 128 * r + rest]
+    for f in range(table_ref.shape[0]):
+        table_ref[f] = rows_ref[f // 2, 40 * (f % 2) : 40 * (f % 2) + 40].astype(F32)[:edim]
+
+    @pl.when(layer == 0)
     def _():
-        out_ref[0, :, :main] = whole_ref[0].astype(F32)
-        at = pl.ds(pl.multiple_of(block * rows, rows), rows)
-        side = small_ref[0, :, at]
-        out_ref[0, :, main:] = side.T[:, 4 : 4 + rest]
-
-    @pl.when(block * rows == main)
-    def _():
-        out_ref[0, :rest, :main] = small_ref[0, :rest]
-        corner = [small_ref[0, 7:8, 128 * r : 128 * r + rest] for r in range(rest)]
-        out_ref[0, :rest, main:] = jnp.concatenate(corner, axis=0)
-
-
-def finish(whole, small, width):
+        for k in range(layers):
+            bias_ref[k : k + 1, :main] = small_ref[k, 3:4]
+            bias_ref[k : k + 1, main:] = small_ref[k, 7:8, 384 : 384 + rest]
+        last = small_ref[layers]
+        turned[...] = last.T
+        share = in_ref.shape[0]
+        me = lax.axis_index("section") * lax.axis_size("dp") + lax.axis_index("dp")
+        mine = turned[pl.ds(pl.multiple_of(me * share, share), share)]
+        share_ref[...] = mine
+        in_ref[:, :main] = pieces_ref[0]
+        in_ref[:, main:] = mine[:, :rest]
+        out_piece_ref[...] = pieces_ref[1]
+        head_ref[:, :main] = last[5:6]
+        head_ref[:, main:width] = last[7:8, :rest]
+        head_ref[:, width:] = last[6:7]
+        sums_ref[...] = last[7:8, 128:384]
+
+
+def finish(whole, small, rows, pieces, width, fields, edim):
     layers, main = whole.shape[:2]
-    rows = 256
-    blocks = main // rows
+    share = pieces.shape[1]
+    pairs, _, count = rows.shape
+    parts = 3
+    step = -(-pairs // parts)
+
+    def all_of(*shape):
+        return pl.BlockSpec(shape, lambda i: (0,) * len(shape))
+
     return pl.pallas_call(
         finish_kernel,
-        out_shape=jax.ShapeDtypeStruct((layers, width, width), F32),
-        grid=(layers, blocks + 1),
+        out_shape=[
+            jax.ShapeDtypeStruct((layers, width, width), F32),
+            jax.ShapeDtypeStruct((fields, edim, count), F32),
+            jax.ShapeDtypeStruct((layers, width), F32),
+            jax.ShapeDtypeStruct((share, width), F32),
+            jax.ShapeDtypeStruct((share, 8), F32),
+            jax.ShapeDtypeStruct((share, main), F32),
+            jax.ShapeDtypeStruct((1, width + main), F32),
+            jax.ShapeDtypeStruct((1, 256), F32),
+        ],
+        grid=(layers,),
         in_specs=[
-            pl.BlockSpec((1, rows, main), lambda i, j: (i, jnp.minimum(j, blocks - 1), 0)),
-            pl.BlockSpec((1, 8, main), lambda i, j: (i, 0, 0)),
+            pl.BlockSpec((1, main, main), lambda i: (i, 0, 0)),
+            all_of(layers + 1, 8, main),
+            pl.BlockSpec((step, 80, count), lambda i: (i, 0, 0)),
+            all_of(2, share, main),
         ],
-        out_specs=pl.BlockSpec((1, rows, width), lambda i, j: (i, j, 0)),
-        compiler_params=pltpu.CompilerParams(vmem_limit_bytes=32 * 2**20),
+        out_specs=[
+            pl.BlockSpec((1, width, width), lambda i: (i, 0, 0)),
+            pl.BlockSpec((2 * step, edim, count), lambda i: (i, 0, 0)),
+            all_of(layers, width),
+            all_of(share, width),
+            all_of(share, 8),
+            all_of(share, main),
+            all_of(1, width + main),
+            all_of(1, 256),
+        ],
+        scratch_shapes=[pltpu.VMEM((main, 8), F32)],
+        compiler_params=pltpu.CompilerParams(vmem_limit_bytes=48 * 2**20),
         name="finish",
-    )(whole, small)
+    )(whole, small, rows, pieces)
 
 
 def general_body(
@@ -933,51 +1050,42 @@
     here = (sections, groups, capacity, table_rows) == (4, 8, 128, 1024)
     if here:
         x0, arrived, source = look_up(idt, table_t, dense.T)
-        tall = x0.shape[0]
-
-        def column(vector):
-            return jnp.pad(vector, (0, tall - vector.shape[0]))
-
-        columns = list(cross_bias) + [tower_in_bias, tower_out_bias]
-        columns += [head_weight[:width], head_weight[width:]]
-        probs, rows, dense_g, small, *grads = network(
+        probs, rows, dense_g, small, *kept = network(
             x0,
             labels.reshape(1, examples),
             cross_weight,
             tower_in,
             tower_out,
-            jnp.stack([column(c) for c in columns], axis=1),
+            cross_bias,
+            tower_in_bias.reshape(1, hidden),
+            tower_out_bias.reshape(1, hidden),
+            head_weight.reshape(1, width + hidden),
             head_bias,
             edim,
             fields // 2,
         )
-        whole, pieces, table_sum, small = reduce_all(grads, layers, rows, source, arrived, small)
-        small = small.reshape(8 * layers + 8, hidden)
-        main, rest = hidden, width - hidden
-        edges = small.reshape(layers + 1, 8, hidden)
-        cross_out = finish(whole, edges, width)
-        table_g = table_sum.reshape(fields, 40, table_rows)[:, :edim].astype(F32)
-        cross_b_out = jnp.concatenate(
-            [edges[:layers, 3], edges[:layers, 7, 384 : 384 + rest]], axis=1
+        xs, vs = [x0] + kept[: layers - 1], kept[layers - 1 : 2 * layers - 1]
+        h1, q1, q2 = kept[2 * layers - 1 :]
+        whole, pieces, table_sum, small = reduce_all(
+            xs + [q1, q2], vs + [x0, h1], layers, rows, source, arrived, small
         )
-        share = hidden // device_count
-        mine = lax.dynamic_slice(edges[layers], (0, me * share), (5, share))
-        tower_in_out = jnp.concatenate([pieces[0], mine[:rest].T], axis=1)
-        misc = edges[layers, 7]
-        head_out = jnp.concatenate([edges[layers, 5], misc[:rest], edges[layers, 6]])
+        small = small.reshape(layers + 1, 8, hidden)
+        cross_out, table_g, cross_b_out, in_out, mine, out_out, head_out, sums = finish(
+            whole, small, table_sum, pieces, width, fields, edim
+        )
         return (
             probs.reshape(examples),
-            misc[256:257] / (examples * device_count),
+            sums[0, 128:129] / (examples * device_count),
             dense_g.T,
             table_g.transpose(0, 2, 1),
             cross_out,
             cross_b_out,
-            tower_in_out.T,
-            mine[3],
-            pieces[1].T,
-            mine[4],
-            head_out,
-            misc[128:129],
+            in_out.T,
+            mine[:, 3],
+            out_out.T,
+            mine[:, 4],
+            head_out.reshape(width + hidden),
+            sums[0, 0:1],
         )
     return general_body(
         ids, dense, labels, table, cross_weight, cross_bias, tower_in, tower_in_bias, tower_out,

time: 308 us -> 277 us (0.90); the launches traced: 307 us -> 272 us
  Pallas kernels: 278 us -> 256 us
  local copies, waits for them, and re-layouts: 21.2 us -> 11.9 us
  other arithmetic: 4.51 us -> 0.63 us
    pallas_call x1, Pallas kernels: 70 us -> 53.8 us  [network(): pl.pallas_call(functools.partial(network_kernel, width, edim), out_shape=...]
    pallas_call x1, Pallas kernels: 138 us -> 132 us  [reduce_all(): pl.pallas_call(lambda *refs: reduce_kernel(units, gathered, *refs), out_s...]
    slice x9 -> x2, local copies, waits for them, and re-layouts: 5.28 us -> 1.22 us  [the longest x1 0.7 us: body(): mine[:, 4]]
    transpose x2 -> x0, other arithmetic: 3.18 us -> none  [the longest x1 2.51 us: body(): table_g.transpose(0, 2, 1)]
    unnamed x20 -> x18, local copies, waits for them, and re-layouts: 9.59 us -> 9.42 us
where the time goes in v6:
time: 277 us; the launch traced here: 272 us
  Pallas kernels  256 us (92%)
  local copies, waits for them, and re-layouts  11.9 us (4%)
  between operations  3.12 us (1%)
    pallas_call x1, Pallas kernels, reduce_all(): pl.pallas_call(lambda *refs: reduce_kernel(units, gathered, *refs), out_s...  132 us
    pallas_call x1, Pallas kernels, look_up(): pl.pallas_call(functools.partial(lookup_kernel, fields, edim), out_shape=...  61.1 us
    pallas_call x1, Pallas kernels, network(): pl.pallas_call(functools.partial(network_kernel, width, edim), out_shape=...  53.8 us
    unnamed x18, local copies, waits for them, and re-layouts  9.42 us
    pallas_call x1, Pallas kernels, finish(): pl.pallas_call(finish_kernel, out_shape=[jax.ShapeDtypeStruct((layers, wi...  8.95 us

profile of v6, /device:TPU:1, one launch (start us, length us, event | category | flops | bytes accessed | tf_op | source)
XLA Modules:
  0.0 271.8 jit_solution(14712274091368381257)
XLA Ops:
  1.3 1.3 reshape.50.head_ref
  2.6 0.0 copy-start.1
  2.6 1.6 copy-done.1
  4.2 0.0 copy-start.7
  4.2 0.9 copy-done.7
  5.1 0.0 copy-start.8
  5.1 0.8 copy-done.8
  5.9 61.1 %look_up.1 = (bf16[1152,1024]{1,0:T(8,128)(2,1)S(1)}, s32[32,1024]{1,0:T(8,128)S(1)}, s32[32,1024]{1,0:T(8,128)S(1)}) custom-call(s32[26,1024]{1,0:T(8,128)S(1)} %bitcast.17, bf16[26,39,1024]{2,1,0:T(8,128)(2,1)S(1)} %bitcast.15, bf16[13,1024]{1,0:T(8,128)(2,1)S(1)} %bitcast.18), custom_call_target="tpu_custom_call" | custom-call | tf_op jit(solution)/shard_map/look_up/pallas_call | solution.py:585
  67.0 0.0 copy-start
  67.0 1.4 copy-done
  68.4 0.0 copy-start.5
  68.4 0.7 copy-done.5
  69.0 0.0 copy-start.6
  69.0 0.7 copy-done.6
  69.7 53.8 %network.1 = (f32[1,1024]{1,0:T(1,128)}, bf16[13,80,1024]{2,1,0:T(8,128)(2,1)}, f32[13,1024]{1,0:T(8,128)}, f32[8,1024]{1,0:T(8,128)}, bf16[1040,1024]{1,0:T(8,1...) custom-call(bf16[1152,1024]{1,0:T(8,128)(2,1)} %copy-done, ...), custom_call_target="tpu_custom_call" | custom-call | tf_op jit(solution)/shard_map/network/pallas_call | solution.py:757
  123.5 132.2 %reduce_all.1 = (bf16[3,2,2,4,2,32,1024]{6,5,4,3,2,1,0:T(8,128)(2,1)}, f32[2,32,1024]{2,1,0:T(8,128)}, bf16[13,80,1024]{2,1,0:T(8,128)(2,1)}, f32[2,16,1024]{2,1,0:T(8,128)}) custom-call(bf16[1152,1024]{1,0:T(8,128)(2,1)} %copy-done, bf16[1040,1024]{1,0:T(8,128)(2,1)} %get-tuple-element.41.refs_1_, bf16[1040,1024]{1,0:T(8,128)(2,1)} %get-tuple-element.42.refs_2_, ...), custom_call_target="tpu_custom_call" | custom-call | tf_op jit(solution)/shard_map/reduce_all/pallas_call | solution.py:392
  255.8 0.0 copy-start.2
  255.8 1.6 copy-done.2
  257.4 0.0 copy-start.3
  257.4 0.9 copy-done.3
  258.3 0.0 copy-start.4
  258.3 0.9 copy-done.4
  259.2 9.0 %finish.1 = (f32[3,1027,1027]{2,1,0:T(8,128)}, f32[26,39,1024]{2,1,0:T(8,128)}, f32[3,1027]{1,0:T(4,128)}, f32[32,1027]{1,0:T(8,128)}, f32[32,8]{1,0:T(8,128)S(1...) custom-call(bf16[3,1024,1024]{2,1,0:T(8,128)(2,1)} %bitcast.19, f32[4,8,1024]{2,1,0:T(8,128)S(1)} %bitcast.16, ...), custom_call_target="tpu_custom_call" | custom-call | tf_op jit(solution)/shard_map/finish/pallas_call | solution.py:842
  268.2 0.5 fusion
  269.3 0.7 slice_reduce_fusion
  270.0 0.6 reduce.2
Async XLA Ops:
  2.6 1.6 copy-start.1
  4.2 0.9 copy-start.7
  5.1 0.8 copy-start.8
  67.0 1.4 copy-start
  68.4 0.7 copy-start.5
  69.0 0.7 copy-start.6
  255.8 1.6 copy-start.2
  257.4 0.9 copy-start.3
  258.3 0.9 copy-start.4

commit v7 on v6

--- a/solution.py
+++ b/solution.py
@@ -24,33 +24,64 @@
 
 
 ORDER = [
-    "C0 P2 C2 u10",
-    "P1 C1 u12 P0",
-    "u11 C4 u20 C3",
-    "n0 u14 u22 P3",
-    "u13 S0 S1 n1",
-    "T10 u21 u30 S2",
-    "T11 T20 n2 u32",
-    "T12 u24 T21 u40",
-    "S3 n3 T22 u23",
-    "u31 T31 u42 u50",
-    "n4 T13 u60 u41",
-    "u52 u34 T23 n5",
-    "u33 T32 T41 u70",
-    "u51 u62 u61 u72",
-    "u44 T42 u43 T33",
-    "u80 T30 T40 u71",
-    "u82 T43 u81",
+    "C1 P0 u11 C0",
+    "P1 u10 S0 C2",
+    "u21 T10 P2 u12",
+    "S1 u20 C3 u31",
+    "T20 T11 u13 P3",
+    "T21 C4 n0 T30",
+    "u22 S2 u23 u41",
+    "n1 u14 S3 u30",
+    "u32 T13 n2 u51",
+    "T40 T23 u61 u40",
+    "n3 u42 u24 u50",
+    "T12 u71 n4 u52",
+    "u34 u60 u33 u62",
+    "n5 u70 T33 T22",
+    "u43 T43 u72 u44",
+    "T31 T32 T42 T41",
+    "u81 u80 u82",
 ]
 VIEW = (2, 2, 4, 2)
+
+
+def one_hot(places, count):
+    rows = lax.broadcasted_iota(jnp.int32, (count, places.shape[1]), 0)
+    return (rows == places).astype(F32).astype(BF)
+
+
+def pick(slab, places):
+    low, block = places & 255, lax.shift_right_logical(places, 8)
+    blocks = [slab[:, 256 * b : 256 * b + 256] for b in range(4)]
+    rows = slab.shape[0]
+    every = jnp.dot(
+        jnp.concatenate(blocks, axis=0), one_hot(low, 256), preferred_element_type=F32
+    )
+    chosen = every[:rows]
+    for b in range(1, 4):
+        chosen = jnp.where(block == b, every[rows * b : rows * b + rows], chosen)
+    return chosen
+
+
+def add_up(slab, places):
+    low, block = places & 255, lax.shift_right_logical(places, 8)
+    rows = slab.shape[0]
+    masked = [slab * (block == b).astype(F32).astype(BF) for b in range(4)]
+    every = lax.dot_general(
+        jnp.concatenate(masked, axis=0),
+        one_hot(low, 256),
+        (((1,), (1,)), ((), ())),
+        preferred_element_type=F32,
+    )
+    return jnp.concatenate([every[rows * b : rows * b + rows] for b in range(4)], axis=1)
 
 
 def reduce_kernel(units, gathered, *refs):
     lefts, rights = refs[:units], refs[units : 2 * units]
     rows_ref, inv_ref, arr_ref, part_ref = refs[2 * units : 2 * units + 4]
-    whole, pieces, table_out, small_out = refs[2 * units + 4 : 2 * units + 8]
+    whole_out, pieces, table_hbm, small_out = refs[2 * units + 4 : 2 * units + 8]
     (
-        grads, left, right, load, small, rc, sa1, ra1, sb1, rb1, sa2, ra2, sb2, rb2, sz, rz, packed, back, summed,
+        whole, table_out, leave, grads, left, right, load, small, rc, sa1, ra1, sb1, rb1, sa2, ra2, sb2, rb2, sz, rz, packed, back, summed,
         stc, rtc, st, rt, sm, rm, rmz, send, recv, row_send, row_recv, table_send, table_recv,
     ) = refs[2 * units + 8 :]
     pairs, count = rows_ref.shape[0], rows_ref.shape[2]
@@ -93,6 +124,12 @@
         return value.astype(F32)
 
     copies = {}
+    gone = []
+
+    def leave_with(src, dst, k):
+        copy = pltpu.make_async_copy(src, dst, leave.at[k])
+        copy.start()
+        gone.append(copy)
 
     def acc(m, stage, cols, yy, zz, xx):
         total = wide(grads[m, yy, c, zz, xx, :, cols]) + wide(rc[m, yy, zz, xx, :, cols])
@@ -233,6 +270,7 @@
 
     def step8(m):
         copies[m, 15].wait_recv()
+        leave_with(whole.at[m], whole_out.at[m], m)
 
     def lanes(place, size):
         return pl.ds(pl.multiple_of(place * size, size), size)
@@ -252,16 +290,8 @@
     def pack(q):
         @pl.loop(cuts[q], cuts[q + 1])
         def _(i):
-            first = jnp.dot(
-                rows_ref[i, 0:48],
-                one_hot(inv_ref[pl.ds(2 * i, 1)], count),
-                preferred_element_type=F32,
-            )
-            second = jnp.dot(
-                rows_ref[i, 32:80],
-                one_hot(inv_ref[pl.ds(2 * i + 1, 1)], count),
-                preferred_element_type=F32,
-            )
+            first = pick(rows_ref[i, 0:48], inv_ref[pl.ds(2 * i, 1)])
+            second = pick(rows_ref[i, 32:80], inv_ref[pl.ds(2 * i + 1, 1)])
             packed[i] = jnp.concatenate([first[0:40], second[8:48]], axis=0).astype(BF)
             for j in range(1, 8):
                 row_copy(i, j).start()
@@ -273,12 +303,7 @@
             for j in range(1, 8):
                 row_copy(i, j).wait_recv()
             for h, (low, at) in enumerate(((0, 0), (32, 8))):
-                total = lax.dot_general(
-                    back[i, low : low + 48],
-                    one_hot(arr_ref[pl.ds(2 * i + h, 1)], count),
-                    (((1,), (1,)), ((), ())),
-                    preferred_element_type=F32,
-                )
+                total = add_up(back[i, low : low + 48], arr_ref[pl.ds(2 * i + h, 1)])
                 summed[i, 40 * h : 40 * h + 40] = total[at : at + 40]
             stc[i] = summed[i, :, lanes(1 - c, half)].astype(BF)
 
@@ -320,6 +345,8 @@
 
     def table4(q):
         copies["t", q, 3].wait_recv()
+        part = pl.ds(cuts[q], cuts[q + 1] - cuts[q])
+        leave_with(table_out.at[part], table_hbm.at[part], gathered + q)
 
     s = units
 
@@ -377,6 +404,8 @@
             {"u": steps, "T": tables}[kind][numbers[0] - 1](numbers[1])
     for copy in flying:
         copy.wait_send()
+    for copy in gone:
+        copy.wait()
 
     @pl.loop(0, pairs)
     def _(i):
@@ -389,6 +418,7 @@
     pairs, _, count = rows.shape
     piece = (32, 1024)
     vmem = pl.BlockSpec(memory_space=pltpu.VMEM)
+    hbm = pl.BlockSpec(memory_space=pl.ANY)
     whole, pieces, table_sum, small_sum = pl.pallas_call(
         lambda *refs: reduce_kernel(units, gathered, *refs),
         out_shape=[
@@ -397,9 +427,12 @@
             jax.ShapeDtypeStruct((pairs, 80, count), BF),
             jax.ShapeDtypeStruct((2, 16, 1024), F32),
         ],
-        in_specs=[pl.BlockSpec(memory_space=pl.ANY)] * (2 * units) + [vmem] * 4,
-        out_specs=[vmem] * 4,
+        in_specs=[hbm] * (2 * units) + [vmem] * 4,
+        out_specs=[hbm, vmem, hbm, vmem],
         scratch_shapes=[
+            pltpu.VMEM((gathered,) + VIEW + piece, BF),
+            pltpu.VMEM((pairs, 80, count), BF),
+            pltpu.SemaphoreType.DMA((gathered + 4,)),
             pltpu.VMEM((units,) + VIEW + piece, BF),
             pltpu.VMEM((2, 1040, count), BF),
             pltpu.VMEM((2, 1152, count), BF),
@@ -434,7 +467,7 @@
             pltpu.SemaphoreType.DMA((4, 4)),
         ],
         compiler_params=pltpu.CompilerParams(
-            collective_id=0, has_side_effects=True, vmem_limit_bytes=62 * 2**20
+            collective_id=0, has_side_effects=True, vmem_limit_bytes=63 * 2**20
         ),
         name="reduce_all",
     )(
@@ -448,14 +481,9 @@
     return whole.reshape(gathered, 1024, 1024), pieces, table_sum, small_sum.reshape(-1)
 
 
-def one_hot(places, count):
-    rows = lax.broadcasted_iota(jnp.int32, (count, places.shape[1]), 0)
-    return (rows == places).astype(F32).astype(BF)
-
-
 def lookup_kernel(
     fields, edim, ids_ref, table_ref, dense_ref, x0_ref, arr_ref, inv_ref,
-    ids, slots, req, found, rep, pair, wide_rows, x0f, id_send, id_recv, send, recv,
+    ids, slots, req, found, rep, held, pair, wide_rows, x0f, id_send, id_recv, send, recv,
 ):
     section, me = lax.axis_index("section"), lax.axis_index("dp")
     dot = functools.partial(jnp.dot, preferred_element_type=F32)
@@ -542,12 +570,14 @@
         )
 
     pair[...] = jnp.zeros_like(pair)
+    held[...] = jnp.zeros_like(held)
 
     @pl.loop(0, fields // 2)
     def _(i):
         for h in range(2):
-            hot = one_hot(arr_ref[pl.ds(2 * i + h, 1)], count)
-            pair[40 * h : 40 * h + edim] = dot(table_ref[2 * i + h], hot)
+            held[h, :edim] = table_ref[2 * i + h]
+            chosen = pick(held[h], arr_ref[pl.ds(2 * i + h, 1)])
+            pair[40 * h : 40 * h + edim] = chosen[:edim]
         found[i] = pair[...].astype(BF)
         for j in range(1, 8):
             row_copy(i, j).start()
@@ -557,8 +587,8 @@
     def _(i):
         for j in range(1, 8):
             row_copy(i, j).wait_recv()
-        wide_rows[2 * i] = dot(rep[i, 0:48], one_hot(slots[pl.ds(2 * i, 1)], count))[0:40]
-        wide_rows[2 * i + 1] = dot(rep[i, 32:80], one_hot(slots[pl.ds(2 * i + 1, 1)], count))[8:48]
+        wide_rows[2 * i] = pick(rep[i, 0:48], slots[pl.ds(2 * i, 1)])[0:40]
+        wide_rows[2 * i + 1] = pick(rep[i, 32:80], slots[pl.ds(2 * i + 1, 1)])[8:48]
 
     sparse, extra = fields * edim, dense_ref.shape[0]
     x0f[sparse // 8 * 8 :] = jnp.zeros_like(x0f[sparse // 8 * 8 :])
@@ -597,6 +627,7 @@
             pltpu.VMEM((32, count), jnp.int32),
             pltpu.VMEM((fields // 2, 80, count), BF),
             pltpu.VMEM((fields // 2, 80, count), BF),
+            pltpu.VMEM((2, 48, count), BF),
             pltpu.VMEM((80, count), F32),
             pltpu.VMEM((fields, 40, count), F32),
             pltpu.VMEM((tall, count), F32),
@@ -606,7 +637,7 @@
             pltpu.SemaphoreType.DMA((fields // 2, 8)),
         ],
         compiler_params=pltpu.CompilerParams(
-            collective_id=1, has_side_effects=True, vmem_limit_bytes=48 * 2**20
+            collective_id=1, has_side_effects=True, vmem_limit_bytes=63 * 2**20
         ),
         name="look_up",
     )(ids_t, table_t, dense_t)
@@ -622,24 +653,38 @@
 
 
 def network_kernel(
-    width, edim, x0_ref, labels_ref, weight_ref, in_ref, out_ref, bias_ref, in_bias_ref, out_bias_ref, head_ref, hb_ref,
+    width, edim, x0_hbm, labels_ref, weight_hbm, in_hbm, out_hbm, bias_ref, in_bias_ref, out_bias_ref, head_ref, hb_ref,
     probs_ref, rows_ref, dense_ref, small_ref, *rest,
 ):
-    layers = weight_ref.shape[0]
+    layers = weight_hbm.shape[0]
     kept = 2 * layers + 2
     outs = rest[:kept]
-    xs, vs, h1s, q1s, q2s, us, d1s, d2s, dxs, accx, acch, accq, accs, lines, cols, leave = rest[kept:]
-    main = in_ref.shape[1]
+    (
+        x0_ref, weight_ref, in_ref, out_ref, xs, vs, h1s, q1s, q2s, gs, us, d1s, d2s, dxs, accx, acch, accq, accs,
+        lines, cols, enter, leave,
+    ) = rest[kept:]
+    main = in_hbm.shape[1]
     edge = slice(main, main + 16)
-    count = x0_ref.shape[1]
+    count = x0_hbm.shape[1]
     block = us.shape[2]
     pairs = rows_ref.shape[0]
 
+    entering = [
+        pltpu.make_async_copy(src, dst, enter.at[k])
+        for k, (src, dst) in enumerate(
+            [(x0_hbm, x0_ref)]
+            + [(weight_hbm.at[i], weight_ref.at[i]) for i in range(layers)]
+            + [(in_hbm, in_ref), (out_hbm, out_ref)]
+        )
+    ]
+    for copy in entering:
+        copy.start()
+
     def leaving(k, n):
         at = pl.ds(pl.multiple_of(n * block, block), block)
-        here = [xs.at[i] for i in range(layers - 1)] + [vs.at[i] for i in range(layers)]
-        here += [h1s, q1s, q2s]
-        return pltpu.make_async_copy(here[k].at[:, at], outs[k].at[:, at], leave.at[n, k])
+        here = [xs.at[i, :, at] for i in range(layers - 1)] + [vs.at[i] for i in range(layers)]
+        here += [h1s.at[:, at], q1s, q2s]
+        return pltpu.make_async_copy(here[k], outs[k].at[:, at], leave.at[n, k])
 
     def dot(a, b, ca, cb):
         return lax.dot_general(a, b, (((ca,), (cb,)), ((), ())), preferred_element_type=F32)
@@ -649,8 +694,6 @@
             lambda a, b: a + b, [value[:, n : n + 128] for n in range(0, value.shape[1], 128)]
         )
 
-    for layer in range(1, layers):
-        xs[layer - 1, edge] = x0_ref[edge]
     for layer in range(layers):
         vs[layer, main:] = jnp.zeros_like(vs[layer, main:])
     accx[...] = jnp.zeros_like(accx)
@@ -664,10 +707,21 @@
     lines[layers + 2 : layers + 3, :width] = head_ref[:, :width]
     lines[layers + 3 : layers + 4, :main] = head_ref[:, width:]
     cols[...] = lines[...].T
-
-    @pl.loop(0, count // block)
-    def _(n):
-        at = pl.ds(pl.multiple_of(n * block, block), block)
+    entering[0].wait()
+    for layer in range(1, layers):
+        xs[layer - 1, edge] = x0_ref[edge]
+    for copy in entering[1:]:
+        copy.wait()
+
+    blocks = count // block
+
+    def one_block(n):
+        at = slice(n * block, n * block + block)
+
+        def before(*which):
+            if n:
+                for k in which:
+                    leaving(k, n - 1).wait()
 
         def x_of(layer):
             return x0_ref[:width, at] if layer == 0 else xs[layer - 1, :width, at]
@@ -704,22 +758,26 @@
         acch[...] += fold(s * h2)
 
         q2 = ((s * head_tower) * d2s[...]).astype(BF)
-        q2s[:, at] = q2
+        before(2 * layers + 1)
+        q2s[...] = q2
         acc = fold(q2.astype(F32))
         accq[...] += acc
         q1 = (dot(out_ref[...], q2, 1, 0) * d1s[...]).astype(BF)
-        q1s[:, at] = q1
-        dxs[:width] = dot(in_ref[...], q1, 1, 0)
+        before(2 * layers)
+        q1s[...] = q1
         g = (s * head_cross).astype(BF)
+        before(*range(layers - 1, 2 * layers - 1))
         for layer in reversed(range(layers)):
-            wide = g.astype(F32)
-            v = (wide * x_of(0).astype(F32)).astype(BF)
-            vs[layer, :width, at] = v
-            dxs[:width] += wide * us[layer, :width]
-            g = wide + dot(weight_ref[layer], v, 1, 0)
+            gs[layer, :width] = g
+            v = (g.astype(F32) * x_of(0).astype(F32)).astype(BF)
+            vs[layer, :width] = v
+            g = g.astype(F32) + dot(weight_ref[layer], v, 1, 0)
             if layer:
                 g = g.astype(BF)
-        dxs[:width] += g
+        g += dot(in_ref[...], q1, 1, 0)
+        for layer in range(layers):
+            g += gs[layer, :width].astype(F32) * us[layer, :width]
+        dxs[:width] = g
         for i in range(pairs):
             low = 2 * i * edim
             both = [dxs[low : low + 40], dxs[low + edim : low + edim + 40]]
@@ -729,10 +787,12 @@
         for k in range(kept):
             leaving(k, n).start()
 
-    @pl.loop(0, count // block)
-    def _(n):
+    for n in range(blocks):
+        one_block(n)
+    for n in range(blocks):
         for k in range(kept):
-            leaving(k, n).wait()
+            if n == blocks - 1 or k < layers - 1 or k == 2 * layers - 1:
+                leaving(k, n).wait()
 
     head_x = jnp.sum(accx[...].T, axis=0, keepdims=True)
     head_h = jnp.sum(acch[...].T, axis=0, keepdims=True)
@@ -751,9 +811,10 @@
     layers, width = cross_weight.shape[:2]
     main = tower_out.shape[0]
     count = x0.shape[1]
-    block = 256
+    block = 512
     tall = main + 16
     vmem = pl.BlockSpec(memory_space=pltpu.VMEM)
+    hbm = pl.BlockSpec(memory_space=pl.ANY)
     return pl.pallas_call(
         functools.partial(network_kernel, width, edim),
         out_shape=[
@@ -765,14 +826,19 @@
         + [jax.ShapeDtypeStruct((tall, count), BF)] * (layers - 1)
         + [jax.ShapeDtypeStruct((main + 128, count), BF)] * layers
         + [jax.ShapeDtypeStruct((main, count), BF)] * 3,
-        in_specs=[vmem] * 9 + [pl.BlockSpec(memory_space=pltpu.SMEM)],
+        in_specs=[hbm, vmem, hbm, hbm, hbm] + [vmem] * 4 + [pl.BlockSpec(memory_space=pltpu.SMEM)],
         out_specs=[vmem] * 4 + [pl.BlockSpec(memory_space=pl.ANY)] * (2 * layers + 2),
         scratch_shapes=[
+            pltpu.VMEM(x0.shape, BF),
+            pltpu.VMEM(cross_weight.shape, BF),
+            pltpu.VMEM(tower_in.shape, BF),
+            pltpu.VMEM(tower_out.shape, BF),
             pltpu.VMEM((layers - 1, tall, count), BF),
-            pltpu.VMEM((layers, main + 128, count), BF),
+            pltpu.VMEM((layers, main + 128, block), BF),
             pltpu.VMEM((main, count), BF),
-            pltpu.VMEM((main, count), BF),
-            pltpu.VMEM((main, count), BF),
+            pltpu.VMEM((main, block), BF),
+            pltpu.VMEM((main, block), BF),
+            pltpu.VMEM((layers, tall, block), BF),
             pltpu.VMEM((layers, tall, block), F32),
             pltpu.VMEM((main, block), F32),
             pltpu.VMEM((main, block), F32),
@@ -783,9 +849,10 @@
             pltpu.VMEM((8, 128), F32),
             pltpu.VMEM((128, main + 128), F32),
             pltpu.VMEM((main + 128, 128), F32),
+            pltpu.SemaphoreType.DMA((layers + 3,)),
             pltpu.SemaphoreType.DMA((count // block, 2 * layers + 2)),
         ],
-        compiler_params=pltpu.CompilerParams(vmem_limit_bytes=60 * 2**20),
+        compiler_params=pltpu.CompilerParams(vmem_limit_bytes=63 * 2**20),
         name="network",
     )(x0, labels, cross_weight, tower_in, tower_out, cross_bias, in_bias, out_bias, head, head_bias)
 
@@ -869,7 +936,7 @@
             all_of(1, 256),
         ],
         scratch_shapes=[pltpu.VMEM((main, 8), F32)],
-        compiler_params=pltpu.CompilerParams(vmem_limit_bytes=48 * 2**20),
+        compiler_params=pltpu.CompilerParams(vmem_limit_bytes=63 * 2**20),
         name="finish",
     )(whole, small, rows, pieces)
 

time: 277 us -> 252 us (0.910)
  Pallas kernels: 256 us -> 240 us
  local copies, waits for them, and re-layouts: 11.9 us -> 4 us
    pallas_call x1, Pallas kernels: 53.8 us -> 43.1 us  [network(): pl.pallas_call(functools.partial(network_kernel, width, edim), out_shape=...]
    unnamed x18 -> x0, local copies, waits for them, and re-layouts: 9.42 us -> none
    pallas_call x1, Pallas kernels: 132 us -> 124 us  [reduce_all(): pl.pallas_call(lambda *refs: reduce_kernel(units, gathered, *refs), out_s...]
where the time goes in v7:
time: 252 us; the launch traced here: 249 us
  Pallas kernels  240 us (95%)
  local copies, waits for them, and re-layouts  4 us (2%)
  between operations  3.29 us (1%)
    pallas_call x1, Pallas kernels, reduce_all(): pl.pallas_call(lambda *refs: reduce_kernel(units, gathered, *refs), out_s...  124 us
    pallas_call x1, Pallas kernels, look_up(): pl.pallas_call(functools.partial(lookup_kernel, fields, edim), out_shape=...  63.9 us
    pallas_call x1, Pallas kernels, network(): pl.pallas_call(functools.partial(network_kernel, width, edim), out_shape=...  43.1 us
    pallas_call x1, Pallas kernels, finish(): pl.pallas_call(finish_kernel, out_shape=[jax.ShapeDtypeStruct((layers, wi...  9.45 us

profile of v7, /device:TPU:1, one launch (start us, length us, event | category | flops | bytes accessed | tf_op | source)
XLA Modules:
  0.0 248.6 jit_solution(14594813347855544207)
XLA Ops:
  1.3 1.3 reshape.50.head_ref
  2.6 63.9 %look_up.1 = (bf16[1152,1024]{1,0:T(8,128)(2,1)}, s32[32,1024]{1,0:T(8,128)}, s32[32,1024]{1,0:T(8,128)}) custom-call(s32[26,1024]{1,0:T(8,128)} %bitcast.18, bf16[26,39,1024]{2,1,0:T(8,128)(2,1)} %bitcast.16, bf16[13,1024]{1,0:T(8,128)(2,1)} %bitcast.19), custom_call_target="tpu_custom_call" | custom-call | tf_op jit(solution)/shard_map/look_up/pallas_call | solution.py:615
  66.5 43.1 %network.1 = (f32[1,1024]{1,0:T(1,128)}, bf16[13,80,1024]{2,1,0:T(8,128)(2,1)}, f32[13,1024]{1,0:T(8,128)}, f32[8,1024]{1,0:T(8,128)}, bf16[1040,1024]{1,0:T(8,1...) custom-call(bf16[1152,1024]{1,0:T(8,128)(2,1)} %get-tuple-element.39, ...), custom_call_target="tpu_custom_call" | custom-call | tf_op jit(solution)/shard_map/network/pallas_call | solution.py:818
  109.6 123.6 %reduce_all.1 = (bf16[3,2,2,4,2,32,1024]{6,5,4,3,2,1,0:T(8,128)(2,1)}, f32[2,32,1024]{2,1,0:T(8,128)}, bf16[13,80,1024]{2,1,0:T(8,128)(2,1)}, f32[2,16,1024]{2,1,0:T(8,128)}) custom-call(bf16[1152,1024]{1,0:T(8,128)(2,1)} %get-tuple-element.39.x0_hbm.refs_0_.refs_8_, bf16[1040,1024]{1,0:T(8,128)(2,1)} %get-tuple-element.41.refs_1_, ...), custom_call_target="tpu_custom_call" | custom-call | tf_op jit(solution)/shard_map/reduce_all/pallas_call | solution.py:422
  233.2 9.4 %finish.1 = (f32[3,1027,1027]{2,1,0:T(8,128)}, f32[26,39,1024]{2,1,0:T(8,128)}, f32[3,1027]{1,0:T(4,128)}, f32[32,1027]{1,0:T(8,128)}, f32[32,8]{1,0:T(8,128)}, ...) custom-call(bf16[3,1024,1024]{2,1,0:T(8,128)(2,1)} %bitcast.15, f32[4,8,1024]{2,1,0:T(8,128)} %bitcast.17, ...), custom_call_target="tpu_custom_call" | custom-call | tf_op jit(solution)/shard_map/finish/pallas_call | solution.py:909
  242.6 1.2 fusion
  244.5 1.5 slice_reduce_fusion
  246.0 1.3 reduce.2

commit v8 on v7

--- a/solution.py
+++ b/solution.py
@@ -24,24 +24,28 @@
 
 
 ORDER = [
-    "C1 P0 u11 C0",
-    "P1 u10 S0 C2",
-    "u21 T10 P2 u12",
-    "S1 u20 C3 u31",
-    "T20 T11 u13 P3",
-    "T21 C4 n0 T30",
-    "u22 S2 u23 u41",
-    "n1 u14 S3 u30",
-    "u32 T13 n2 u51",
-    "T40 T23 u61 u40",
-    "n3 u42 u24 u50",
-    "T12 u71 n4 u52",
-    "u34 u60 u33 u62",
-    "n5 u70 T33 T22",
-    "u43 T43 u72 u44",
-    "T31 T32 T42 T41",
-    "u81 u80 u82",
+    "P3 P4 C1 P1",
+    "u11 C2 C0 u12",
+    "u21 P0 u10 C4",
+    "S1 u31 T11 u14",
+    "S4 T21 P5 u22",
+    "T14 C3 u20 u41",
+    "T24 u13 S5 u32",
+    "u24 n0 T15 u30",
+    "n1 S0 u51 T10",
+    "u42 u23 T25 T20",
+    "u61 u40 S3 n2",
+    "T13 T30 u52 P2",
+    "T31 T34 u50 T40",
+    "n3 u62 u60 u33",
+    "T35 u71 u34 S2",
+    "T12 u72 n4 T23",
+    "T22 u70 T33 n5",
+    "T32 u80 u43 T43",
+    "u44 u82 T44 T42",
+    "T41 T45 u81",
 ]
+PARTS = 6
 VIEW = (2, 2, 4, 2)
 
 
@@ -285,7 +289,7 @@
             device_id_type=pl.DeviceIdType.MESH,
         )
 
-    cuts = [pairs * q // 4 for q in range(5)]
+    cuts = [pairs * q // PARTS for q in range(PARTS + 1)]
 
     def pack(q):
         @pl.loop(cuts[q], cuts[q + 1])
@@ -432,7 +436,7 @@
         scratch_shapes=[
             pltpu.VMEM((gathered,) + VIEW + piece, BF),
             pltpu.VMEM((pairs, 80, count), BF),
-            pltpu.SemaphoreType.DMA((gathered + 4,)),
+            pltpu.SemaphoreType.DMA((gathered + PARTS,)),
             pltpu.VMEM((units,) + VIEW + piece, BF),
             pltpu.VMEM((2, 1040, count), BF),
             pltpu.VMEM((2, 1152, count), BF),
@@ -463,8 +467,8 @@
             pltpu.SemaphoreType.DMA((units + 1, 16)),
             pltpu.SemaphoreType.DMA((pairs, 8)),
             pltpu.SemaphoreType.DMA((pairs, 8)),
-            pltpu.SemaphoreType.DMA((4, 4)),
-            pltpu.SemaphoreType.DMA((4, 4)),
+            pltpu.SemaphoreType.DMA((PARTS, 4)),
+            pltpu.SemaphoreType.DMA((PARTS, 4)),
         ],
         compiler_params=pltpu.CompilerParams(
             collective_id=0, has_side_effects=True, vmem_limit_bytes=63 * 2**20
@@ -483,22 +487,46 @@
 
 def lookup_kernel(
     fields, edim, ids_ref, table_ref, dense_ref, x0_ref, arr_ref, inv_ref,
-    ids, slots, req, found, rep, held, pair, wide_rows, x0f, id_send, id_recv, send, recv,
+    ids, slots, req, found, rep, held, pair, wide_rows, x0f, far, arr_far,
+    id_send, id_recv, send, recv, far_send, far_recv, far_id_send, far_id_recv, half_send, half_recv,
 ):
     section, me = lax.axis_index("section"), lax.axis_index("dp")
+    direct = fields // 2 - far.shape[0] // 2
+    half, spot = me // 4, lax.rem(me, 4)
+    twin = lax.rem(me + 4, 8)
+    y, core = section // 2, lax.rem(section, 2)
+    core_peer = (y * 2 + 1 - core, me)
+    y_peer = ((1 - y) * 2 + core, me)
     dot = functools.partial(jnp.dot, preferred_element_type=F32)
     count = ids.shape[1]
 
     def peer(j):
         return lax.rem(me + j, 8)
 
-    def lanes(place):
-        return pl.ds(pl.multiple_of(place * 128, 128), 128)
+    def near(j):
+        return lax.rem(spot + j, 4)
+
+    def lanes(place, size=128):
+        return pl.ds(pl.multiple_of(place * size, size), size)
 
     barrier = pltpu.get_barrier_semaphore()
     for j in range(1, 8):
         pl.semaphore_signal(
             barrier, inc=1, device_id=(section, peer(j)), device_id_type=pl.DeviceIdType.MESH
+        )
+    for other in (core_peer, y_peer):
+        pl.semaphore_signal(barrier, inc=1, device_id=other, device_id_type=pl.DeviceIdType.MESH)
+
+    def far_copy(k):
+        quarter = section if k < 3 else (1 - y) * 2 + core
+        window = far.at[:, :, lanes(quarter, count // 4)]
+        return pltpu.make_async_remote_copy(
+            src_ref=window if k else table_ref.at[2 * direct :, :, lanes(quarter, count // 4)],
+            dst_ref=window,
+            send_sem=far_send.at[k],
+            recv_sem=far_recv.at[k],
+            device_id=((section, twin), core_peer, y_peer, core_peer)[k],
+            device_id_type=pl.DeviceIdType.MESH,
         )
 
     ids[...] = jnp.zeros_like(ids)
@@ -515,7 +543,31 @@
     for o in range(8):
         rank = jnp.where(owner == o, ranks[32 * o : 32 * o + 32], rank)
     slots[...] = owner * 128 + rank.astype(jnp.int32)
+    pl.semaphore_wait(barrier, 9)
+    far_copy(0).start()
     ids[...] = every & 1023
+    def id_copy(group, j):
+        eight = pl.ds(pl.multiple_of(8 * group, 8), 8)
+        return pltpu.make_async_remote_copy(
+            src_ref=req.at[eight, lanes(peer(j))],
+            dst_ref=arr_ref.at[eight, lanes(me)],
+            send_sem=id_send.at[group, j],
+            recv_sem=id_recv.at[group, j],
+            device_id=(section, peer(j)),
+            device_id_type=pl.DeviceIdType.MESH,
+        )
+
+    def far_id_copy(group, j):
+        eight = pl.ds(pl.multiple_of(8 * group, 8), 8)
+        return pltpu.make_async_remote_copy(
+            src_ref=req.at[eight, lanes(4 * (1 - half) + near(j))],
+            dst_ref=arr_far.at[eight, lanes(spot)],
+            send_sem=far_id_send.at[group, j],
+            recv_sem=far_id_recv.at[group, j],
+            device_id=(section, 4 * half + near(j)),
+            device_id_type=pl.DeviceIdType.MESH,
+        )
+
     @pl.loop(0, 4)
     def _(group):
         eight = pl.ds(pl.multiple_of(8 * group, 8), 8)
@@ -541,23 +593,17 @@
                 taken.append(jnp.concatenate([r[o : o + 1] for o in range(8)], axis=1))
         req[eight] = jnp.concatenate(wanted, axis=0)
         inv_ref[eight] = jnp.concatenate(source, axis=0)
-
-    def id_copy(j):
-        return pltpu.make_async_remote_copy(
-            src_ref=req.at[:, lanes(peer(j))],
-            dst_ref=arr_ref.at[:, lanes(me)],
-            send_sem=id_send.at[j],
-            recv_sem=id_recv.at[j],
-            device_id=(section, peer(j)),
-            device_id_type=pl.DeviceIdType.MESH,
-        )
-
-    pl.semaphore_wait(barrier, 7)
-    for j in range(1, 8):
-        id_copy(j).start()
-    arr_ref[:, lanes(me)] = req[:, lanes(me)]
-    for j in range(1, 8):
-        id_copy(j).wait_recv()
+        for j in range(1, 8):
+            id_copy(group, j).start()
+        for j in range(1, 4):
+            far_id_copy(group, j).start()
+        arr_ref[eight, lanes(me)] = req[eight, lanes(me)]
+        arr_far[eight, lanes(spot)] = req[eight, lanes(4 * (1 - half) + spot)]
+
+    def ids_of(group):
+        for j in range(1, 8):
+            id_copy(group, j).wait_recv()
+
 
     def row_copy(i, j):
         return pltpu.make_async_remote_copy(
@@ -572,8 +618,25 @@
     pair[...] = jnp.zeros_like(pair)
     held[...] = jnp.zeros_like(held)
 
-    @pl.loop(0, fields // 2)
+    def half_copy(i, j, far_side):
+        owner_place = 4 * (1 - half) + spot if far_side else me
+        return pltpu.make_async_remote_copy(
+            src_ref=found.at[i, :, lanes(4 * far_side + near(j))],
+            dst_ref=rep.at[i, :, lanes(owner_place)],
+            send_sem=half_send.at[far_side, i - direct, j],
+            recv_sem=half_recv.at[far_side, i - direct, j],
+            device_id=(section, 4 * half + near(j)),
+            device_id_type=pl.DeviceIdType.MESH,
+        )
+
+    assert direct % 4 == 0
+
+    @pl.loop(0, direct)
     def _(i):
+        @pl.when(lax.rem(i, 4) == 0)
+        def _():
+            ids_of(i // 4)
+
         for h in range(2):
             held[h, :edim] = table_ref[2 * i + h]
             chosen = pick(held[h], arr_ref[pl.ds(2 * i + h, 1)])
@@ -583,12 +646,58 @@
             row_copy(i, j).start()
         rep[i, :, lanes(me)] = found[i, :, lanes(me)]
 
-    @pl.loop(0, fields // 2)
+    for group in range(direct // 4, 4):
+        ids_of(group)
+
+    @pl.loop(direct, fields // 2)
+    def _(i):
+        for h in range(2):
+            held[h, :edim] = table_ref[2 * i + h]
+            places = arr_ref[pl.ds(2 * i + h, 1), lanes(half, count // 2)]
+            pair[40 * h : 40 * h + edim, : count // 2] = pick(held[h], places)[:edim]
+        found[i, :, : count // 2] = pair[:, : count // 2].astype(BF)
+        for j in range(1, 4):
+            half_copy(i, j, 0).start()
+        rep[i, :, lanes(me)] = found[i, :, lanes(spot)]
+
+    far_copy(0).wait_recv()
+    far_copy(2).start()
+    far_copy(1).start()
+    for group in range(4):
+        for j in range(1, 4):
+            far_id_copy(group, j).wait_recv()
+    far_copy(2).wait_recv()
+    far_copy(3).start()
+    far_copy(1).wait_recv()
+    far_copy(3).wait_recv()
+
+    @pl.loop(direct, fields // 2)
+    def _(i):
+        for h in range(2):
+            held[h, :edim] = far[2 * (i - direct) + h]
+            places = arr_far[pl.ds(2 * i + h, 1)]
+            pair[40 * h : 40 * h + edim, count // 2 :] = pick(held[h], places)[:edim]
+        found[i, :, count // 2 :] = pair[:, count // 2 :].astype(BF)
+        for j in range(1, 4):
+            half_copy(i, j, 1).start()
+        rep[i, :, lanes(4 * (1 - half) + spot)] = found[i, :, lanes(4 + spot)]
+
+    def unpack(i):
+        wide_rows[2 * i] = pick(rep[i, 0:48], slots[pl.ds(2 * i, 1)])[0:40]
+        wide_rows[2 * i + 1] = pick(rep[i, 32:80], slots[pl.ds(2 * i + 1, 1)])[8:48]
+
+    @pl.loop(0, direct)
     def _(i):
         for j in range(1, 8):
             row_copy(i, j).wait_recv()
-        wide_rows[2 * i] = pick(rep[i, 0:48], slots[pl.ds(2 * i, 1)])[0:40]
-        wide_rows[2 * i + 1] = pick(rep[i, 32:80], slots[pl.ds(2 * i + 1, 1)])[8:48]
+        unpack(i)
+
+    @pl.loop(direct, fields // 2)
+    def _(i):
+        for j in range(1, 4):
+            half_copy(i, j, 0).wait_recv()
+            half_copy(i, j, 1).wait_recv()
+        unpack(i)
 
     sparse, extra = fields * edim, dense_ref.shape[0]
     x0f[sparse // 8 * 8 :] = jnp.zeros_like(x0f[sparse // 8 * 8 :])
@@ -598,19 +707,31 @@
     x0f[sparse + extra : sparse + extra + 1] = jnp.ones_like(x0f[:1])
     x0_ref[...] = x0f[...].astype(BF)
 
-    @pl.loop(0, fields // 2)
+    @pl.loop(0, direct)
     def _(i):
         for j in range(1, 8):
             row_copy(i, j).wait_send()
 
-    for j in range(1, 8):
-        id_copy(j).wait_send()
+    @pl.loop(direct, fields // 2)
+    def _(i):
+        for j in range(1, 4):
+            half_copy(i, j, 0).wait_send()
+            half_copy(i, j, 1).wait_send()
+
+    for group in range(4):
+        for j in range(1, 8):
+            id_copy(group, j).wait_send()
+        for j in range(1, 4):
+            far_id_copy(group, j).wait_send()
+    for n in range(4):
+        far_copy(n).wait_send()
 
 
 def look_up(ids_t, table_t, dense_t):
     fields, count = ids_t.shape
     edim = table_t.shape[1]
     tall = (fields * edim + dense_t.shape[0]) // 128 * 128 + 128
+    mirrored = fields // 4 - 1
     vmem = pl.BlockSpec(memory_space=pltpu.VMEM)
     return pl.pallas_call(
         functools.partial(lookup_kernel, fields, edim),
@@ -631,10 +752,18 @@
             pltpu.VMEM((80, count), F32),
             pltpu.VMEM((fields, 40, count), F32),
             pltpu.VMEM((tall, count), F32),
-            pltpu.SemaphoreType.DMA((8,)),
-            pltpu.SemaphoreType.DMA((8,)),
+            pltpu.VMEM((2 * mirrored, edim, count), BF),
+            pltpu.VMEM((32, count // 2), jnp.int32),
+            pltpu.SemaphoreType.DMA((4, 8)),
+            pltpu.SemaphoreType.DMA((4, 8)),
             pltpu.SemaphoreType.DMA((fields // 2, 8)),
             pltpu.SemaphoreType.DMA((fields // 2, 8)),
+            pltpu.SemaphoreType.DMA((4,)),
+            pltpu.SemaphoreType.DMA((4,)),
+            pltpu.SemaphoreType.DMA((4, 4)),
+            pltpu.SemaphoreType.DMA((4, 4)),
+            pltpu.SemaphoreType.DMA((2, mirrored, 4)),
+            pltpu.SemaphoreType.DMA((2, mirrored, 4)),
         ],
         compiler_params=pltpu.CompilerParams(
             collective_id=1, has_side_effects=True, vmem_limit_bytes=63 * 2**20

time: 252 us -> 240 us (0.952)
  Pallas kernels: 240 us -> 227 us
    pallas_call x1, Pallas kernels: 63.9 us -> 56.8 us  [look_up(): pl.pallas_call(functools.partial(lookup_kernel, fields, edim), out_shape=...]
    pallas_call x1, Pallas kernels: 124 us -> 117 us  [reduce_all(): pl.pallas_call(lambda *refs: reduce_kernel(units, gathered, *refs), out_s...]
where the time goes in v8:
time: 240 us; the launch traced here: 235 us
  Pallas kernels  227 us (95%)
  local copies, waits for them, and re-layouts  4 us (2%)
  between operations  3.29 us (1%)
    pallas_call x1, Pallas kernels, reduce_all(): pl.pallas_call(lambda *refs: reduce_kernel(units, gathered, *refs), out_s...  117 us
    pallas_call x1, Pallas kernels, look_up(): pl.pallas_call(functools.partial(lookup_kernel, fields, edim), out_shape=...  56.8 us
    pallas_call x1, Pallas kernels, network(): pl.pallas_call(functools.partial(network_kernel, width, edim), out_shape=...  43.1 us
    pallas_call x1, Pallas kernels, finish(): pl.pallas_call(finish_kernel, out_shape=[jax.ShapeDtypeStruct((layers, wi...  9.45 us

profile of v8, /device:TPU:1, one launch (start us, length us, event | category | flops | bytes accessed | tf_op | source)
XLA Modules:
  0.0 235.4 jit_solution(16903393439764773517)
XLA Ops:
  1.3 1.3 reshape.50.head_ref
  2.6 56.8 %look_up.1 = (bf16[1152,1024]{1,0:T(8,128)(2,1)}, s32[32,1024]{1,0:T(8,128)}, s32[32,1024]{1,0:T(8,128)}) custom-call(s32[26,1024]{1,0:T(8,128)} %bitcast.18, bf16[26,39,1024]{2,1,0:T(8,128)(2,1)} %bitcast.16, bf16[13,1024]{1,0:T(8,128)(2,1)} %bitcast.19), custom_call_target="tpu_custom_call" | custom-call | tf_op jit(solution)/shard_map/look_up/pallas_call | solution.py:736
  59.5 43.1 %network.1 = (f32[1,1024]{1,0:T(1,128)}, bf16[13,80,1024]{2,1,0:T(8,128)(2,1)}, f32[13,1024]{1,0:T(8,128)}, f32[8,1024]{1,0:T(8,128)}, bf16[1040,1024]{1,0:T(8,1...) custom-call(bf16[1152,1024]{1,0:T(8,128)(2,1)} %get-tuple-element.39, ...), custom_call_target="tpu_custom_call" | custom-call | tf_op jit(solution)/shard_map/network/pallas_call | solution.py:947
  102.5 117.4 %reduce_all.1 = (bf16[3,2,2,4,2,32,1024]{6,5,4,3,2,1,0:T(8,128)(2,1)}, f32[2,32,1024]{2,1,0:T(8,128)}, bf16[13,80,1024]{2,1,0:T(8,128)(2,1)}, f32[2,16,1024]{2,1,0:T(8,128)}) custom-call(bf16[1152,1024]{1,0:T(8,128)(2,1)} %get-tuple-element.39.x0_hbm.refs_0_.refs_8_, bf16[1040,1024]{1,0:T(8,128)(2,1)} %get-tuple-element.41.refs_1_, ...), custom_call_target="tpu_custom_call" | custom-call | tf_op jit(solution)/shard_map/reduce_all/pallas_call | solution.py:426
  219.9 9.4 %finish.1 = (f32[3,1027,1027]{2,1,0:T(8,128)}, f32[26,39,1024]{2,1,0:T(8,128)}, f32[3,1027]{1,0:T(4,128)}, f32[32,1027]{1,0:T(8,128)}, f32[32,8]{1,0:T(8,128)}, ...) custom-call(bf16[3,1024,1024]{2,1,0:T(8,128)(2,1)} %bitcast.15, f32[4,8,1024]{2,1,0:T(8,128)} %bitcast.17, ...), custom_call_target="tpu_custom_call" | custom-call | tf_op jit(solution)/shard_map/finish/pallas_call | solution.py:1038
  229.4 1.2 fusion
  231.2 1.5 slice_reduce_fusion
  232.7 1.3 reduce.2

commit v9 on v8

--- a/solution.py
+++ b/solution.py
@@ -82,13 +82,13 @@
 
 def reduce_kernel(units, gathered, *refs):
     lefts, rights = refs[:units], refs[units : 2 * units]
-    rows_ref, inv_ref, arr_ref, part_ref = refs[2 * units : 2 * units + 4]
+    rows_hbm, inv_ref, arr_ref, part_ref = refs[2 * units : 2 * units + 4]
     whole_out, pieces, table_hbm, small_out = refs[2 * units + 4 : 2 * units + 8]
     (
-        whole, table_out, leave, grads, left, right, load, small, rc, sa1, ra1, sb1, rb1, sa2, ra2, sb2, rb2, sz, rz, packed, back, summed,
+        rows_ref, rows_in, whole, table_out, leave, grads, left, right, load, small, rc, sa1, ra1, sb1, rb1, sa2, ra2, sb2, rb2, sz, rz, packed, back, summed,
         stc, rtc, st, rt, sm, rm, rmz, send, recv, row_send, row_recv, table_send, table_recv,
     ) = refs[2 * units + 8 :]
-    pairs, count = rows_ref.shape[0], rows_ref.shape[2]
+    pairs, count = rows_hbm.shape[0], rows_hbm.shape[2]
     section, dp = lax.axis_index("section"), lax.axis_index("dp")
     y, c = section // 2, section % 2
     z, x = dp // 2, dp % 2
@@ -279,17 +279,18 @@
     def lanes(place, size):
         return pl.ds(pl.multiple_of(place * size, size), size)
 
-    def row_copy(i, j):
+    cuts = [pairs * q // PARTS for q in range(PARTS + 1)]
+
+    def row_copy(q, j):
+        part = pl.ds(cuts[q], cuts[q + 1] - cuts[q])
         return pltpu.make_async_remote_copy(
-            src_ref=packed.at[i, :, lanes(lax.rem(dp + j, 8), 128)],
-            dst_ref=back.at[i, :, lanes(dp, 128)],
-            send_sem=row_send.at[i, j],
-            recv_sem=row_recv.at[i, j],
+            src_ref=packed.at[part, :, lanes(lax.rem(dp + j, 8), 128)],
+            dst_ref=back.at[part, :, lanes(dp, 128)],
+            send_sem=row_send.at[q, j],
+            recv_sem=row_recv.at[q, j],
             device_id=dp_peer(j),
             device_id_type=pl.DeviceIdType.MESH,
         )
-
-    cuts = [pairs * q // PARTS for q in range(PARTS + 1)]
 
     def pack(q):
         @pl.loop(cuts[q], cuts[q + 1])
@@ -297,15 +298,17 @@
             first = pick(rows_ref[i, 0:48], inv_ref[pl.ds(2 * i, 1)])
             second = pick(rows_ref[i, 32:80], inv_ref[pl.ds(2 * i + 1, 1)])
             packed[i] = jnp.concatenate([first[0:40], second[8:48]], axis=0).astype(BF)
-            for j in range(1, 8):
-                row_copy(i, j).start()
             back[i, :, lanes(dp, 128)] = packed[i, :, lanes(dp, 128)]
 
+        for j in range(1, 8):
+            row_copy(q, j).start()
+
     def scatter(q):
+        for j in range(1, 8):
+            row_copy(q, j).wait_recv()
+
         @pl.loop(cuts[q], cuts[q + 1])
         def _(i):
-            for j in range(1, 8):
-                row_copy(i, j).wait_recv()
             for h, (low, at) in enumerate(((0, 0), (32, 8))):
                 total = add_up(back[i, low : low + 48], arr_ref[pl.ds(2 * i + h, 1)])
                 summed[i, 40 * h : 40 * h + 40] = total[at : at + 40]
@@ -391,9 +394,12 @@
     steps = [step1, step2, step3, step4, step5, step6, step7, step8]
     smalls = [small0, small1, small2, small3, small4, small5]
     tables = [table1, table2, table3, table4]
+    rows_copy = pltpu.make_async_copy(rows_hbm, rows_ref, rows_in)
+    rows_copy.start()
     for copy in loads(0) + loads(1):
         copy.start()
     pl.semaphore_wait(barrier, len(peers))
+    rows_copy.wait()
     for token in tokens:
         kind, numbers = token[0], [int(n) for n in token[1:]]
         if kind == "C":
@@ -411,10 +417,9 @@
     for copy in gone:
         copy.wait()
 
-    @pl.loop(0, pairs)
-    def _(i):
+    for q in range(PARTS):
         for j in range(1, 8):
-            row_copy(i, j).wait_send()
+            row_copy(q, j).wait_send()
 
 
 def reduce_all(lefts, rights, gathered, rows, source, arrived, small):
@@ -431,9 +436,11 @@
             jax.ShapeDtypeStruct((pairs, 80, count), BF),
             jax.ShapeDtypeStruct((2, 16, 1024), F32),
         ],
-        in_specs=[hbm] * (2 * units) + [vmem] * 4,
+        in_specs=[hbm] * (2 * units + 1) + [vmem] * 3,
         out_specs=[hbm, vmem, hbm, vmem],
         scratch_shapes=[
+            pltpu.VMEM((pairs, 80, count), BF),
+            pltpu.SemaphoreType.DMA,
             pltpu.VMEM((gathered,) + VIEW + piece, BF),
             pltpu.VMEM((pairs, 80, count), BF),
             pltpu.SemaphoreType.DMA((gathered + PARTS,)),
@@ -465,8 +472,8 @@
             pltpu.VMEM((3, 16, 1024), F32),
             pltpu.SemaphoreType.DMA((units + 1, 16)),
             pltpu.SemaphoreType.DMA((units + 1, 16)),
-            pltpu.SemaphoreType.DMA((pairs, 8)),
-            pltpu.SemaphoreType.DMA((pairs, 8)),
+            pltpu.SemaphoreType.DMA((PARTS, 8)),
+            pltpu.SemaphoreType.DMA((PARTS, 8)),
             pltpu.SemaphoreType.DMA((PARTS, 4)),
             pltpu.SemaphoreType.DMA((PARTS, 4)),
         ],
@@ -486,8 +493,8 @@
 
 
 def lookup_kernel(
-    fields, edim, ids_ref, table_ref, dense_ref, x0_ref, arr_ref, inv_ref,
-    ids, slots, req, found, rep, held, pair, wide_rows, x0f, far, arr_far,
+    fields, edim, ids_ref, table_hbm, dense_ref, x0_ref, arr_ref, inv_ref,
+    table_ref, table_in, ids, slots, req, found, rep, held, pair, wide_rows, x0f, far, arr_far,
     id_send, id_recv, send, recv, far_send, far_recv, far_id_send, far_id_recv, half_send, half_recv,
 ):
     section, me = lax.axis_index("section"), lax.axis_index("dp")
@@ -499,6 +506,9 @@
     y_peer = ((1 - y) * 2 + core, me)
     dot = functools.partial(jnp.dot, preferred_element_type=F32)
     count = ids.shape[1]
+
+    table_copy = pltpu.make_async_copy(table_hbm, table_ref, table_in)
+    table_copy.start()
 
     def peer(j):
         return lax.rem(me + j, 8)
@@ -544,6 +554,7 @@
         rank = jnp.where(owner == o, ranks[32 * o : 32 * o + 32], rank)
     slots[...] = owner * 128 + rank.astype(jnp.int32)
     pl.semaphore_wait(barrier, 9)
+    table_copy.wait()
     far_copy(0).start()
     ids[...] = every & 1023
     def id_copy(group, j):
@@ -740,9 +751,11 @@
             jax.ShapeDtypeStruct((32, count), jnp.int32),
             jax.ShapeDtypeStruct((32, count), jnp.int32),
         ],
-        in_specs=[vmem] * 3,
+        in_specs=[vmem, pl.BlockSpec(memory_space=pl.ANY), vmem],
         out_specs=[vmem] * 3,
         scratch_shapes=[
+            pltpu.VMEM(table_t.shape, BF),
+            pltpu.SemaphoreType.DMA,
             pltpu.VMEM((32, count), jnp.int32),
             pltpu.VMEM((32, count), jnp.int32),
             pltpu.VMEM((32, count), jnp.int32),
@@ -833,14 +846,13 @@
     lines[0:layers, :width] = bias_ref[...]
     lines[layers : layers + 1, :main] = in_bias_ref[...]
     lines[layers + 1 : layers + 2, :main] = out_bias_ref[...]
-    lines[layers + 2 : layers + 3, :width] = head_ref[:, :width]
-    lines[layers + 3 : layers + 4, :main] = head_ref[:, width:]
+    head = head_ref[...].reshape(1, width + main)
+    lines[layers + 2 : layers + 3, :width] = head[:, :width]
+    lines[layers + 3 : layers + 4, :main] = head[:, width:]
     cols[...] = lines[...].T
     entering[0].wait()
     for layer in range(1, layers):
         xs[layer - 1, edge] = x0_ref[edge]
-    for copy in entering[1:]:
-        copy.wait()
 
     blocks = count // block
 
@@ -852,6 +864,13 @@
                 for k in which:
                     leaving(k, n - 1).wait()
 
+        def arrived(k):
+            if n == 0:
+                entering[k].wait()
+
+        def complete(k):
+            leaving(k, n).start()
+
         def x_of(layer):
             return x0_ref[:width, at] if layer == 0 else xs[layer - 1, :width, at]
 
@@ -859,15 +878,20 @@
             return cols[:size, k : k + 1]
 
         for layer in range(layers):
+            arrived(1 + layer)
             u = dot(weight_ref[layer], x_of(layer), 0, 0) + col(layer, width)
             us[layer, :width] = u
             x = (x_of(0).astype(F32) * u + x_of(layer).astype(F32)).astype(BF)
             if layer + 1 < layers:
                 xs[layer, :width, at] = x
+                complete(layer)
         last = x.astype(F32)
+        arrived(layers + 1)
         h1, d1 = gelu_and_slope(dot(in_ref[...], x_of(0), 0, 0) + col(layers, main))
         d1s[...] = d1
         h1s[:, at] = h1.astype(BF)
+        complete(2 * layers - 1)
+        arrived(layers + 2)
         h2, d2 = gelu_and_slope(dot(out_ref[...], h1s[:, at], 0, 0) + col(layers + 1, main))
         d2s[...] = d2
         head_cross, head_tower = col(layers + 2, width), col(layers + 3, main)
@@ -889,17 +913,20 @@
         q2 = ((s * head_tower) * d2s[...]).astype(BF)
         before(2 * layers + 1)
         q2s[...] = q2
+        complete(2 * layers + 1)
         acc = fold(q2.astype(F32))
         accq[...] += acc
         q1 = (dot(out_ref[...], q2, 1, 0) * d1s[...]).astype(BF)
         before(2 * layers)
         q1s[...] = q1
+        complete(2 * layers)
         g = (s * head_cross).astype(BF)
         before(*range(layers - 1, 2 * layers - 1))
         for layer in reversed(range(layers)):
             gs[layer, :width] = g
             v = (g.astype(F32) * x_of(0).astype(F32)).astype(BF)
             vs[layer, :width] = v
+            complete(layers - 1 + layer)
             g = g.astype(F32) + dot(weight_ref[layer], v, 1, 0)
             if layer:
                 g = g.astype(BF)
@@ -912,9 +939,6 @@
             both = [dxs[low : low + 40], dxs[low + edim : low + edim + 40]]
             rows_ref[i, :, at] = jnp.concatenate(both, axis=0).astype(BF)
         dense_ref[:, at] = dxs[2 * pairs * edim : width]
-
-        for k in range(kept):
-            leaving(k, n).start()
 
     for n in range(blocks):
         one_block(n)
@@ -987,8 +1011,8 @@
 
 
 def finish_kernel(
-    whole_ref, small_ref, rows_ref, pieces_ref, out_ref, table_ref, bias_ref, in_ref, share_ref, out_piece_ref,
-    head_ref, sums_ref, turned,
+    examples, whole_ref, small_ref, rows_ref, pieces_ref, out_ref, table_ref, bias_ref, in_ref, in_bias_ref,
+    out_bias_ref, out_piece_ref, head_ref, slope_ref, loss_ref, turned,
 ):
     layers, main = small_ref.shape[0] - 1, small_ref.shape[2]
     rest = out_ref.shape[2] - main
@@ -1015,17 +1039,19 @@
         share = in_ref.shape[0]
         me = lax.axis_index("section") * lax.axis_size("dp") + lax.axis_index("dp")
         mine = turned[pl.ds(pl.multiple_of(me * share, share), share)]
-        share_ref[...] = mine
+        rolled = pltpu.roll(last, lax.rem(main - me * share, main), 1)
+        in_bias_ref[...] = rolled[3:4, :share]
+        out_bias_ref[...] = rolled[4:5, :share]
         in_ref[:, :main] = pieces_ref[0]
         in_ref[:, main:] = mine[:, :rest]
         out_piece_ref[...] = pieces_ref[1]
-        head_ref[:, :main] = last[5:6]
-        head_ref[:, main:width] = last[7:8, :rest]
-        head_ref[:, width:] = last[6:7]
-        sums_ref[...] = last[7:8, 128:384]
-
-
-def finish(whole, small, rows, pieces, width, fields, edim):
+        head = jnp.concatenate([last[5:6], last[7:8, :rest], last[6:7]], axis=1)
+        head_ref[...] = head.reshape(width + main)
+        slope_ref[...] = last[7:8, 128:129]
+        loss_ref[...] = last[7:8, 256:257] / examples
+
+
+def finish(whole, small, rows, pieces, width, fields, edim, examples):
     layers, main = whole.shape[:2]
     share = pieces.shape[1]
     pairs, _, count = rows.shape
@@ -1036,16 +1062,18 @@
         return pl.BlockSpec(shape, lambda i: (0,) * len(shape))
 
     return pl.pallas_call(
-        finish_kernel,
+        functools.partial(finish_kernel, examples),
         out_shape=[
             jax.ShapeDtypeStruct((layers, width, width), F32),
             jax.ShapeDtypeStruct((fields, edim, count), F32),
             jax.ShapeDtypeStruct((layers, width), F32),
             jax.ShapeDtypeStruct((share, width), F32),
-            jax.ShapeDtypeStruct((share, 8), F32),
+            jax.ShapeDtypeStruct((1, share), F32),
+            jax.ShapeDtypeStruct((1, share), F32),
             jax.ShapeDtypeStruct((share, main), F32),
-            jax.ShapeDtypeStruct((1, width + main), F32),
-            jax.ShapeDtypeStruct((1, 256), F32),
+            jax.ShapeDtypeStruct((width + main,), F32),
+            jax.ShapeDtypeStruct((1, 1), F32),
+            jax.ShapeDtypeStruct((1, 1), F32),
         ],
         grid=(layers,),
         in_specs=[
@@ -1059,10 +1087,12 @@
             pl.BlockSpec((2 * step, edim, count), lambda i: (i, 0, 0)),
             all_of(layers, width),
             all_of(share, width),
-            all_of(share, 8),
+            all_of(1, share),
+            all_of(1, share),
             all_of(share, main),
-            all_of(1, width + main),
-            all_of(1, 256),
+            all_of(width + main),
+            all_of(1, 1),
+            all_of(1, 1),
         ],
         scratch_shapes=[pltpu.VMEM((main, 8), F32)],
         compiler_params=pltpu.CompilerParams(vmem_limit_bytes=63 * 2**20),
@@ -1255,7 +1285,7 @@
             cross_bias,
             tower_in_bias.reshape(1, hidden),
             tower_out_bias.reshape(1, hidden),
-            head_weight.reshape(1, width + hidden),
+            head_weight,
             head_bias,
             edim,
             fields // 2,
@@ -1266,22 +1296,22 @@
             xs + [q1, q2], vs + [x0, h1], layers, rows, source, arrived, small
         )
         small = small.reshape(layers + 1, 8, hidden)
-        cross_out, table_g, cross_b_out, in_out, mine, out_out, head_out, sums = finish(
-            whole, small, table_sum, pieces, width, fields, edim
+        cross_out, table_g, cross_b_out, in_out, in_b, out_b, out_out, head_out, slopes, loss = finish(
+            whole, small, table_sum, pieces, width, fields, edim, examples * device_count
         )
         return (
             probs.reshape(examples),
-            sums[0, 128:129] / (examples * device_count),
+            loss.reshape(1),
             dense_g.T,
             table_g.transpose(0, 2, 1),
             cross_out,
             cross_b_out,
             in_out.T,
-            mine[:, 3],
+            in_b.reshape(in_b.shape[1]),
             out_out.T,
-            mine[:, 4],
-            head_out.reshape(width + hidden),
-            sums[0, 0:1],
+            out_b.reshape(out_b.shape[1]),
+            head_out,
+            slopes.reshape(1),
         )
     return general_body(
         ids, dense, labels, table, cross_weight, cross_bias, tower_in, tower_in_bias, tower_out,

time: 240 us -> 228 us (0.950)
  Pallas kernels: 227 us -> 222 us
  local copies, waits for them, and re-layouts: 4 us -> 0 us
    slice x2 -> x0, local copies, waits for them, and re-layouts: 2.69 us -> none  [the longest x1 1.5 us: body(): mine[:, 4]]
where the time goes in v9:
time: 228 us; the launch traced here: 223 us
  Pallas kernels  222 us (97%)
    pallas_call x1, Pallas kernels, reduce_all(): pl.pallas_call(lambda *refs: reduce_kernel(units, gathered, *refs), out_s...  115 us
    pallas_call x1, Pallas kernels, look_up(): pl.pallas_call(functools.partial(lookup_kernel, fields, edim), out_shape=...  55.5 us
    pallas_call x1, Pallas kernels, network(): pl.pallas_call(functools.partial(network_kernel, width, edim), out_shape=...  41.5 us
    pallas_call x1, Pallas kernels, finish(): pl.pallas_call(functools.partial(finish_kernel, examples), out_shape=[jax...  9.46 us

profile of v9, /device:TPU:1, one launch (start us, length us, event | category | flops | bytes accessed | tf_op | source)
XLA Modules:
  0.0 223.3 jit_solution(2730885598132683155)
XLA Ops:
  1.3 55.5 %look_up.1 = (bf16[1152,1024]{1,0:T(8,128)(2,1)}, s32[32,1024]{1,0:T(8,128)}, s32[32,1024]{1,0:T(8,128)}) custom-call(s32[26,1024]{1,0:T(8,128)} %bitcast.20, bf16[26,39,1024]{2,1,0:T(8,128)(2,1)} %bitcast.18, bf16[13,1024]{1,0:T(8,128)(2,1)} %bitcast.21), custom_call_target="tpu_custom_call" | custom-call | tf_op jit(solution)/shard_map/look_up/pallas_call | solution.py:747
  56.8 41.5 %network.1 = (f32[1,1024]{1,0:T(1,128)}, bf16[13,80,1024]{2,1,0:T(8,128)(2,1)}, f32[13,1024]{1,0:T(8,128)}, f32[8,1024]{1,0:T(8,128)}, bf16[1040,1024]{1,0:T(8,1...) custom-call(bf16[1152,1024]{1,0:T(8,128)(2,1)} %get-tuple-element.41, ...), custom_call_target="tpu_custom_call" | custom-call | tf_op jit(solution)/shard_map/network/pallas_call | solution.py:971
  98.3 115.3 %reduce_all.1 = (bf16[3,2,2,4,2,32,1024]{6,5,4,3,2,1,0:T(8,128)(2,1)}, f32[2,32,1024]{2,1,0:T(8,128)}, bf16[13,80,1024]{2,1,0:T(8,128)(2,1)}, f32[2,16,1024]{2,1,0:T(8,128)}) custom-call(bf16[1152,1024]{1,0:T(8,128)(2,1)} %get-tuple-element.41.x0_hbm.refs_0_.refs_8_, bf16[1040,1024]{1,0:T(8,128)(2,1)} %get-tuple-element.43.refs_1_, ...), custom_call_target="tpu_custom_call" | custom-call | tf_op jit(solution)/shard_map/reduce_all/pallas_call | solution.py:431
  213.7 9.5 %finish.1 = (f32[3,1027,1027]{2,1,0:T(8,128)}, f32[26,39,1024]{2,1,0:T(8,128)}, f32[3,1027]{1,0:T(4,128)}, f32[32,1027]{1,0:T(8,128)}, f32[1,32]{1,0:T(1,128)}, ...) custom-call(bf16[3,1024,1024]{2,1,0:T(8,128)(2,1)} %bitcast.17, ...), custom_call_target="tpu_custom_call" | custom-call | tf_op jit(solution)/shard_map/finish/pallas_call | solution.py:1064

commit v10 on v9

--- a/solution.py
+++ b/solution.py
@@ -24,29 +24,31 @@
 
 
 ORDER = [
-    "P3 P4 C1 P1",
-    "u11 C2 C0 u12",
-    "u21 P0 u10 C4",
-    "S1 u31 T11 u14",
-    "S4 T21 P5 u22",
-    "T14 C3 u20 u41",
-    "T24 u13 S5 u32",
-    "u24 n0 T15 u30",
-    "n1 S0 u51 T10",
-    "u42 u23 T25 T20",
-    "u61 u40 S3 n2",
-    "T13 T30 u52 P2",
-    "T31 T34 u50 T40",
-    "n3 u62 u60 u33",
-    "T35 u71 u34 S2",
-    "T12 u72 n4 T23",
-    "T22 u70 T33 n5",
-    "T32 u80 u43 T43",
-    "u44 u82 T44 T42",
-    "T41 T45 u81",
+    "P4 C1 C2 u11",
+    "C0 u12 S4 u21",
+    "P5 T14 u10 C4",
+    "u31 C3 u22 P3",
+    "T24 u14 u41 S5",
+    "u20 n0 u51 u32",
+    "u13 T15 P2 u61",
+    "S3 T25 u42 T13",
+    "u30 n1 u24 P1",
+    "u71 u52 T23 S2",
+    "n2 T12 u62 u23",
+    "u34 u40 u81 S1",
+    "u72 u50 T11 T35",
+    "u33 P0 T22 T33",
+    "T21 u60 u82 S0",
+    "T45 u70 T32 u43",
+    "T34 T31 u92 n3",
+    "T10 u44 u80 u53",
+    "n4 u91 n5 T20",
+    "T43 T41 u90 ua1",
+    "T42 T30 u54 T44",
+    "ua0 T40 ua2 n6",
 ]
 PARTS = 6
-VIEW = (2, 2, 4, 2)
+VIEW = (2, 2, 2, 2, 2)
 
 
 def one_hot(places, count):
@@ -85,21 +87,22 @@
     rows_hbm, inv_ref, arr_ref, part_ref = refs[2 * units : 2 * units + 4]
     whole_out, pieces, table_hbm, small_out = refs[2 * units + 4 : 2 * units + 8]
     (
-        rows_ref, rows_in, whole, table_out, leave, grads, left, right, load, small, rc, sa1, ra1, sb1, rb1, sa2, ra2, sb2, rb2, sz, rz, packed, back, summed,
-        stc, rtc, st, rt, sm, rm, rmz, send, recv, row_send, row_recv, table_send, table_recv,
+        rows_ref, rows_in, whole, table_out, leave, grads, left, right, load, small, rc, sa1, ra1, sb1, rb1, sa2, ra2, sb2, rb2, sz, rz, sf, rf, packed, back, summed,
+        stc, rtc, st, rt, sm, rm, send, recv, row_send, row_recv, table_send, table_recv,
     ) = refs[2 * units + 8 :]
     pairs, count = rows_hbm.shape[0], rows_hbm.shape[2]
     section, dp = lax.axis_index("section"), lax.axis_index("dp")
     y, c = section // 2, section % 2
     z, x = dp // 2, dp % 2
+    zh, zl = z // 2, z % 2
     core_peer = (y * 2 + 1 - c, dp)
     y_peer = ((1 - y) * 2 + c, dp)
     x_peer = (section, z * 2 + 1 - x)
     half = 512
     lo, hi = pl.ds(0, half), pl.ds(half, half)
 
-    def z_peer(j):
-        return (section, lax.rem(z + j, 4) * 2 + x)
+    near_peer = (section, zh * 4 + (1 - zl) * 2 + x)
+    far_peer = (section, (1 - zh) * 4 + zl * 2 + x)
 
     def dp_peer(j):
         return (section, lax.rem(dp + j, 8))
@@ -135,8 +138,9 @@
         copy.start()
         gone.append(copy)
 
-    def acc(m, stage, cols, yy, zz, xx):
-        total = wide(grads[m, yy, c, zz, xx, :, cols]) + wide(rc[m, yy, zz, xx, :, cols])
+    def acc(m, stage, cols, yy, hh, ll, xx):
+        zz = 2 * hh + ll
+        total = wide(grads[m, yy, c, hh, ll, xx, :, cols]) + wide(rc[m, yy, hh, ll, xx, :, cols])
         if cols is lo:
             if stage >= 2:
                 total += wide(ra1[m, yy, zz])
@@ -178,7 +182,7 @@
                 (((1,), (1,)), ((), ())),
                 preferred_element_type=F32,
             )
-            grads[m, r] = total[:512, :1024].astype(BF).reshape(2, 4, 2, 32, 1024)
+            grads[m, r] = total[:512, :1024].astype(BF).reshape(2, 2, 2, 2, 32, 1024)
             if across > 1024:
                 side = total[:512, 1024:].T
                 group, at = m // 2, m % 2 * 8
@@ -204,11 +208,12 @@
     def step1(m):
         copies[m, 0].wait_recv()
 
-        @pl.loop(0, 4)
-        def _(zz):
-            for i in range(2):
-                sa1[m, i, zz] = acc(m, 1, lo, i, zz, 1 - x).astype(BF)
-                sb1[m, zz, i] = acc(m, 1, hi, 1 - y, zz, i).astype(BF)
+        @pl.loop(0, 2)
+        def _(hh):
+            for ll in range(2):
+                for i in range(2):
+                    sa1[m, i, 2 * hh + ll] = acc(m, 1, lo, i, hh, ll, 1 - x).astype(BF)
+                    sb1[m, 2 * hh + ll, i] = acc(m, 1, hi, 1 - y, hh, ll, i).astype(BF)
 
         copies[m, 1] = start(sa1.at[m], ra1.at[m], m, 1, x_peer)
         copies[m, 2] = start(sb1.at[m], rb1.at[m], m, 2, y_peer)
@@ -217,10 +222,11 @@
         copies[m, 1].wait_recv()
         copies[m, 2].wait_recv()
 
-        @pl.loop(0, 4)
-        def _(zz):
-            sa2[m, zz] = acc(m, 2, lo, 1 - y, zz, x).astype(BF)
-            sb2[m, zz] = acc(m, 2, hi, y, zz, 1 - x).astype(BF)
+        @pl.loop(0, 2)
+        def _(hh):
+            for ll in range(2):
+                sa2[m, 2 * hh + ll] = acc(m, 2, lo, 1 - y, hh, ll, x).astype(BF)
+                sb2[m, 2 * hh + ll] = acc(m, 2, hi, y, hh, ll, 1 - x).astype(BF)
 
         copies[m, 3] = start(sa2.at[m], ra2.at[m], m, 3, y_peer)
         copies[m, 4] = start(sb2.at[m], rb2.at[m], m, 4, x_peer)
@@ -228,51 +234,57 @@
     def step3(m):
         copies[m, 3].wait_recv()
         copies[m, 4].wait_recv()
-        for j in (1, 2, 3):
-            zz = lax.rem(z + j, 4)
-            sz[m, j - 1, :, lo] = acc(m, 3, lo, y, zz, x).astype(BF)
-            sz[m, j - 1, :, hi] = acc(m, 3, hi, y, zz, x).astype(BF)
-            copies[m, 4 + j] = start(sz.at[m, j - 1], rz.at[m, j - 1], m, 4 + j, z_peer(j))
+        for hh in range(2):
+            for cols in (lo, hi):
+                sz[m, hh, :, cols] = acc(m, 3, cols, y, hh, 1 - zl, x).astype(BF)
+        copies[m, 5] = start(sz.at[m], rz.at[m], m, 5, near_peer)
 
     def step4(m):
-        for j in (1, 2, 3):
-            copies[m, 4 + j].wait_recv()
+        copies[m, 5].wait_recv()
         for cols in (lo, hi):
-            total = acc(m, 3, cols, y, z, x)
-            for j in range(3):
-                total += wide(rz[m, j, :, cols])
+            total = acc(m, 3, cols, y, 1 - zh, zl, x) + wide(rz[m, 1 - zh, :, cols])
+            sf[m, :, cols] = total.astype(BF)
+        copies[m, 6] = start(sf.at[m], rf.at[m], m, 6, far_peer)
+
+    def step5(m):
+        copies[m, 6].wait_recv()
+        for cols in (lo, hi):
+            total = acc(m, 3, cols, y, zh, zl, x) + wide(rz[m, zh, :, cols]) + wide(rf[m, :, cols])
             if m < gathered:
-                whole[m, y, c, z, x, :, cols] = total.astype(BF)
+                whole[m, y, c, zh, zl, x, :, cols] = total.astype(BF)
             else:
                 pieces[m - gathered, :, cols] = total
         if m < gathered:
-            for j in (1, 2, 3):
-                mine = whole.at[m, y, c, z, x]
-                copies[m, 7 + j] = start(mine, mine, m, 7 + j, z_peer(j))
-
-    def step5(m):
-        for j in (1, 2, 3):
-            copies[m, 7 + j].wait_recv()
-        ours = whole.at[m, y, c, :, x, :, lo]
+            ours = whole.at[m, y, c, zh, zl, x]
+            copies[m, 7] = start(ours, ours, m, 7, far_peer)
+
+    def step6(m):
+        copies[m, 7].wait_recv()
+        ours = whole.at[m, y, c, :, zl, x]
+        copies[m, 8] = start(ours, ours, m, 8, near_peer)
+
+    def step7(m):
+        copies[m, 8].wait_recv()
+        ours = whole.at[m, y, c, :, :, x, :, lo]
         copies[m, 11] = start(ours, ours, m, 11, y_peer)
-        ours = whole.at[m, y, c, :, x, :, hi]
+        ours = whole.at[m, y, c, :, :, x, :, hi]
         copies[m, 12] = start(ours, ours, m, 12, x_peer)
 
-    def step6(m):
+    def step8(m):
         copies[m, 11].wait_recv()
         copies[m, 12].wait_recv()
-        ours = whole.at[m, :, c, :, x, :, lo]
+        ours = whole.at[m, :, c, :, :, x, :, lo]
         copies[m, 13] = start(ours, ours, m, 13, x_peer)
-        ours = whole.at[m, y, c, :, :, :, hi]
+        ours = whole.at[m, y, c, :, :, :, :, hi]
         copies[m, 14] = start(ours, ours, m, 14, y_peer)
 
-    def step7(m):
+    def step9(m):
         copies[m, 13].wait_recv()
         copies[m, 14].wait_recv()
         ours = whole.at[m, :, c]
         copies[m, 15] = start(ours, ours, m, 15, core_peer)
 
-    def step8(m):
+    def step10(m):
         copies[m, 15].wait_recv()
         leave_with(whole.at[m], whole_out.at[m], m)
 
@@ -374,25 +386,24 @@
     def small3():
         copies[s, 2].wait_recv()
         sm[2] = sm[1] + rm[2]
-        for j in (1, 2, 3):
-            copies[s, 2 + j] = start(sm.at[2], rmz.at[j - 1], s, 2 + j, z_peer(j))
+        copies[s, 3] = start(sm.at[2], rm.at[3], s, 3, near_peer)
 
     def small4():
-        for j in (1, 2, 3):
-            copies[s, 2 + j].wait_recv()
-        even = lax.rem(z, 2)
-        near = [sm[2], rmz[0], rmz[1], rmz[2]]
-        first = near[0] + near[2]
-        second = near[1] + near[3]
-        small_out[c] = jnp.where(even == 0, first, second) + jnp.where(even == 0, second, first)
+        copies[s, 3].wait_recv()
+        sm[3] = sm[2] + rm[3]
+        copies[s, 4] = start(sm.at[3], rm.at[4], s, 4, far_peer)
+
+    def small5():
+        copies[s, 4].wait_recv()
+        small_out[c] = sm[3] + rm[4]
         ours = small_out.at[c]
         copies[s, 6] = start(ours, ours, s, 6, core_peer)
 
-    def small5():
+    def small6():
         copies[s, 6].wait_recv()
 
-    steps = [step1, step2, step3, step4, step5, step6, step7, step8]
-    smalls = [small0, small1, small2, small3, small4, small5]
+    steps = [step1, step2, step3, step4, step5, step6, step7, step8, step9, step10]
+    smalls = [small0, small1, small2, small3, small4, small5, small6]
     tables = [table1, table2, table3, table4]
     rows_copy = pltpu.make_async_copy(rows_hbm, rows_ref, rows_in)
     rows_copy.start()
@@ -401,7 +412,7 @@
     pl.semaphore_wait(barrier, len(peers))
     rows_copy.wait()
     for token in tokens:
-        kind, numbers = token[0], [int(n) for n in token[1:]]
+        kind, numbers = token[0], [int(n, 16) for n in token[1:]]
         if kind == "C":
             step0(*numbers)
         elif kind == "P":
@@ -449,7 +460,7 @@
             pltpu.VMEM((2, 1152, count), BF),
             pltpu.SemaphoreType.DMA((2, 2)),
             pltpu.VMEM((2, 16, 1024), F32),
-            pltpu.VMEM((units, 2, 4, 2) + piece, BF),
+            pltpu.VMEM((units, 2, 2, 2, 2) + piece, BF),
             pltpu.VMEM((units, 2, 4, 32, 512), BF),
             pltpu.VMEM((units, 2, 4, 32, 512), BF),
             pltpu.VMEM((units, 4, 2, 32, 512), BF),
@@ -458,8 +469,10 @@
             pltpu.VMEM((units, 4, 32, 512), BF),
             pltpu.VMEM((units, 4, 32, 512), BF),
             pltpu.VMEM((units, 4, 32, 512), BF),
-            pltpu.VMEM((units, 3) + piece, BF),
-            pltpu.VMEM((units, 3) + piece, BF),
+            pltpu.VMEM((units, 2) + piece, BF),
+            pltpu.VMEM((units, 2) + piece, BF),
+            pltpu.VMEM((units,) + piece, BF),
+            pltpu.VMEM((units,) + piece, BF),
             pltpu.VMEM((pairs, 80, count), BF),
             pltpu.VMEM((pairs, 80, count), BF),
             pltpu.VMEM((pairs, 80, count), F32),
@@ -467,9 +480,8 @@
             pltpu.VMEM((pairs, 80, count // 2), BF),
             pltpu.VMEM((pairs, 80, count // 4), BF),
             pltpu.VMEM((pairs, 80, count // 4), BF),
-            pltpu.VMEM((3, 16, 1024), F32),
-            pltpu.VMEM((3, 16, 1024), F32),
-            pltpu.VMEM((3, 16, 1024), F32),
+            pltpu.VMEM((4, 16, 1024), F32),
+            pltpu.VMEM((5, 16, 1024), F32),
             pltpu.SemaphoreType.DMA((units + 1, 16)),
             pltpu.SemaphoreType.DMA((units + 1, 16)),
             pltpu.SemaphoreType.DMA((PARTS, 8)),

time: 228 us -> 226 us (level)
  no operation moved by 1% of the time
where the time goes in v10:
time: 226 us; the launch traced here: 223 us
  Pallas kernels  221 us (98%)
    pallas_call x1, Pallas kernels, reduce_all(): pl.pallas_call(lambda *refs: reduce_kernel(units, gathered, *refs), out_s...  115 us
    pallas_call x1, Pallas kernels, look_up(): pl.pallas_call(functools.partial(lookup_kernel, fields, edim), out_shape=...  55.5 us
    pallas_call x1, Pallas kernels, network(): pl.pallas_call(functools.partial(network_kernel, width, edim), out_shape=...  41.5 us
    pallas_call x1, Pallas kernels, finish(): pl.pallas_call(functools.partial(finish_kernel, examples), out_shape=[jax...  9.46 us

profile of v10, /device:TPU:1, one launch (start us, length us, event | category | flops | bytes accessed | tf_op | source)
XLA Modules:
  0.0 222.6 jit_solution(6708774013377063061)
XLA Ops:
  1.3 55.5 %look_up.1 = (bf16[1152,1024]{1,0:T(8,128)(2,1)}, s32[32,1024]{1,0:T(8,128)}, s32[32,1024]{1,0:T(8,128)}) custom-call(s32[26,1024]{1,0:T(8,128)} %bitcast.20, bf16[26,39,1024]{2,1,0:T(8,128)(2,1)} %bitcast.18, bf16[13,1024]{1,0:T(8,128)(2,1)} %bitcast.21), custom_call_target="tpu_custom_call" | custom-call | tf_op jit(solution)/shard_map/look_up/pallas_call | solution.py:759
  56.8 41.5 %network.1 = (f32[1,1024]{1,0:T(1,128)}, bf16[13,80,1024]{2,1,0:T(8,128)(2,1)}, f32[13,1024]{1,0:T(8,128)}, f32[8,1024]{1,0:T(8,128)}, bf16[1040,1024]{1,0:T(8,1...) custom-call(bf16[1152,1024]{1,0:T(8,128)(2,1)} %get-tuple-element.41, ...), custom_call_target="tpu_custom_call" | custom-call | tf_op jit(solution)/shard_map/network/pallas_call | solution.py:983
  98.3 114.6 %reduce_all.1 = (bf16[3,2,2,2,2,2,32,1024]{7,6,5,4,3,2,1,0:T(8,128)(2,1)}, f32[2,32,1024]{2,1,0:T(8,128)}, bf16[13,80,1024]{2,1,0:T(8,128)(2,1)}, f32[2,16,1024]{2,1,0:T(8,128)}) custom-call(bf16[1152,1024]{1,0:T(8,128)(2,1)} %get-tuple-element.41.x0_hbm.refs_0_.refs_8_, bf16[1040,1024]{1,0:T(8,128)(2,1)} %get-tuple-element.43.refs_1_, ...), custom_call_target="tpu_custom_call" | custom-call | tf_op jit(solution)/shard_map/reduce_all/pallas_call | solution.py:442
  212.9 9.5 %finish.1 = (f32[3,1027,1027]{2,1,0:T(8,128)}, f32[26,39,1024]{2,1,0:T(8,128)}, f32[3,1027]{1,0:T(4,128)}, f32[32,1027]{1,0:T(8,128)}, f32[1,32]{1,0:T(1,128)}, ...) custom-call(bf16[3,1024,1024]{2,1,0:T(8,128)(2,1)} %bitcast.17, ...), custom_call_target="tpu_custom_call" | custom-call | tf_op jit(solution)/shard_map/finish/pallas_call | solution.py:1076

commit v11 on v10

--- a/solution.py
+++ b/solution.py
@@ -112,9 +112,15 @@
     for peer in peers:
         pl.semaphore_signal(barrier, inc=1, device_id=peer, device_id_type=pl.DeviceIdType.MESH)
 
-    flying = []
+    flying, entered, loaded = [], [], []
+
+    def enter():
+        if not entered:
+            pl.semaphore_wait(barrier, len(peers))
+            entered.append(True)
 
     def start(src, dst, m, k, peer, sems=(send, recv)):
+        enter()
         copy = pltpu.make_async_remote_copy(
             src_ref=src,
             dst_ref=dst,
@@ -304,7 +310,13 @@
             device_id_type=pl.DeviceIdType.MESH,
         )
 
+    rows_copy = pltpu.make_async_copy(rows_hbm, rows_ref, rows_in)
+
     def pack(q):
+        if not loaded:
+            rows_copy.wait()
+            loaded.append(True)
+
         @pl.loop(cuts[q], cuts[q + 1])
         def _(i):
             first = pick(rows_ref[i, 0:48], inv_ref[pl.ds(2 * i, 1)])
@@ -312,6 +324,7 @@
             packed[i] = jnp.concatenate([first[0:40], second[8:48]], axis=0).astype(BF)
             back[i, :, lanes(dp, 128)] = packed[i, :, lanes(dp, 128)]
 
+        enter()
         for j in range(1, 8):
             row_copy(q, j).start()
 
@@ -405,12 +418,9 @@
     steps = [step1, step2, step3, step4, step5, step6, step7, step8, step9, step10]
     smalls = [small0, small1, small2, small3, small4, small5, small6]
     tables = [table1, table2, table3, table4]
-    rows_copy = pltpu.make_async_copy(rows_hbm, rows_ref, rows_in)
     rows_copy.start()
     for copy in loads(0) + loads(1):
         copy.start()
-    pl.semaphore_wait(barrier, len(peers))
-    rows_copy.wait()
     for token in tokens:
         kind, numbers = token[0], [int(n, 16) for n in token[1:]]
         if kind == "C":

time: 226 us -> 225 us (level)
  no operation moved by 1% of the time
where the time goes in v11:
time: 225 us; the launch traced here: 222 us
  Pallas kernels  220 us (98%)
    pallas_call x1, Pallas kernels, reduce_all(): pl.pallas_call(lambda *refs: reduce_kernel(units, gathered, *refs), out_s...  114 us
    pallas_call x1, Pallas kernels, look_up(): pl.pallas_call(functools.partial(lookup_kernel, fields, edim), out_shape=...  55.5 us
    pallas_call x1, Pallas kernels, network(): pl.pallas_call(functools.partial(network_kernel, width, edim), out_shape=...  41.5 us
    pallas_call x1, Pallas kernels, finish(): pl.pallas_call(functools.partial(finish_kernel, examples), out_shape=[jax...  9.46 us

profile of v11, /device:TPU:1, one launch (start us, length us, event | category | flops | bytes accessed | tf_op | source)
XLA Modules:
  0.0 221.9 jit_solution(15523628994958152262)
XLA Ops:
  1.3 55.5 %look_up.1 = (bf16[1152,1024]{1,0:T(8,128)(2,1)}, s32[32,1024]{1,0:T(8,128)}, s32[32,1024]{1,0:T(8,128)}) custom-call(s32[26,1024]{1,0:T(8,128)} %bitcast.20, bf16[26,39,1024]{2,1,0:T(8,128)(2,1)} %bitcast.18, bf16[13,1024]{1,0:T(8,128)(2,1)} %bitcast.21), custom_call_target="tpu_custom_call" | custom-call | tf_op jit(solution)/shard_map/look_up/pallas_call | solution.py:769
  56.8 41.5 %network.1 = (f32[1,1024]{1,0:T(1,128)}, bf16[13,80,1024]{2,1,0:T(8,128)(2,1)}, f32[13,1024]{1,0:T(8,128)}, f32[8,1024]{1,0:T(8,128)}, bf16[1040,1024]{1,0:T(8,1...) custom-call(bf16[1152,1024]{1,0:T(8,128)(2,1)} %get-tuple-element.41, ...), custom_call_target="tpu_custom_call" | custom-call | tf_op jit(solution)/shard_map/network/pallas_call | solution.py:993
  98.3 113.9 %reduce_all.1 = (bf16[3,2,2,2,2,2,32,1024]{7,6,5,4,3,2,1,0:T(8,128)(2,1)}, f32[2,32,1024]{2,1,0:T(8,128)}, bf16[13,80,1024]{2,1,0:T(8,128)(2,1)}, f32[2,16,1024]{2,1,0:T(8,128)}) custom-call(bf16[1152,1024]{1,0:T(8,128)(2,1)} %get-tuple-element.41.x0_hbm.refs_0_.refs_8_, bf16[1040,1024]{1,0:T(8,128)(2,1)} %get-tuple-element.43.refs_1_, ...), custom_call_target="tpu_custom_call" | custom-call | tf_op jit(solution)/shard_map/reduce_all/pallas_call | solution.py:452
  212.2 9.5 %finish.1 = (f32[3,1027,1027]{2,1,0:T(8,128)}, f32[26,39,1024]{2,1,0:T(8,128)}, f32[3,1027]{1,0:T(4,128)}, f32[32,1027]{1,0:T(8,128)}, f32[1,32]{1,0:T(1,128)}, ...) custom-call(bf16[3,1024,1024]{2,1,0:T(8,128)(2,1)} %bitcast.17, ...), custom_call_target="tpu_custom_call" | custom-call | tf_op jit(solution)/shard_map/finish/pallas_call | solution.py:1086
